TPU v7x, 128 devices: a whole 4x4x4 slice. The times are simulated.
128 devices in a mesh: seq: 64 (over x, y, z), ch: 2 (over core).
Axes of the slice: x: 4, y: 4, z: 4, core: 2. Of those that a mesh axis runs over, the one named last changes fastest.
Arguments:
- tokens: bfloat16 [8192, 1536], P('seq'), may hold values from -16 to 16
- cotangent: bfloat16 [8192, 1536], P('seq'), may hold values from -16 to 16
- seq_lengths: int32 [4], replicated, may hold values from 1 to 4096, 8192 in all
- block_slots: int32 [64], replicated, may hold values from 0 to 63, each once
- mixgain: float32 [1536], replicated, may hold values from 0.25 to 1.75
- inproj: bfloat16 [3, 1536, 1536], P(None, None, 'ch'), may hold values from -0.15625 to 0.15625
- conv_taps: float32 [3, 1536], P(None, 'ch'), may hold values from -3 to 3
- outproj: bfloat16 [1536, 1536], P('ch'), may hold values from -0.15625 to 0.15625
- glugain: float32 [1536], replicated, may hold values from 0.25 to 1.75
- gate_weight: bfloat16 [1536, 6912], P(None, 'ch'), may hold values from -0.15625 to 0.15625
- lift_weight: bfloat16 [1536, 6912], P(None, 'ch'), may hold values from -0.15625 to 0.15625
- down_weight: bfloat16 [6912, 1536], P('ch'), may hold values from -0.078125 to 0.078125
Outputs:
- layer_out: bfloat16 [8192, 1536], P('seq')
- input_grad: bfloat16 [8192, 1536], P('seq')
- mixgain_grad: float32 [1536], P('ch')
- inproj_grad: float32 [3, 1536, 1536], P(None, 'seq', 'ch')
- taps_grad: float32 [3, 1536], P(None, 'ch')
- outproj_grad: float32 [1536, 1536], P('ch', 'seq')
- glugain_grad: float32 [1536], P('ch')
- gate_grad: float32 [1536, 6912], P('seq', 'ch')
- lift_grad: float32 [1536, 6912], P('seq', 'ch')
- down_grad: float32 [6912, 1536], P('ch', 'seq')
Inputs may be any that keep to these rules, and one draw needn't show every extreme that they name: `seq_lengths`: the lengths sum to 8192 and the longest is 4096. `block_slots`: A permutation of the 64 blocks; held slot j lies on index j // 1 of seq.
All inputs are finite; a program needn't handle non-finite values.
Results may differ from a plain program's by a relative error of at most 0.014.
Values may be sent and summed in bfloat16 or wider, within the bound.
A program may use at most 512 MiB of HBM per device.

v0:
```python
import jax
import jax.numpy as jnp
from jax import lax
from jax.sharding import PartitionSpec as P

BLK = 128


epsilon = 1e-05


def from_everyone(value, axis):
    copies = jnp.broadcast_to(value, (lax.axis_size(axis), *value.shape))
    return lax.all_to_all(copies, axis, split_axis=0, concat_axis=0, tiled=True)


def laid_out(tiles, dim):
    tiles = jnp.moveaxis(tiles, 0, dim)
    shape = tiles.shape
    return tiles.reshape(*shape[:dim], shape[dim] * shape[dim + 1], *shape[dim + 2 :])


def collect(value, axis, dim):
    tiles = from_everyone(value, axis)
    return laid_out(tiles, dim)


def over_copies(value, axis):
    everything = from_everyone(value, axis)
    return jnp.sum(everything, axis=0)


def taken_together(value, axis):
    everything = from_everyone(value, axis)
    return jnp.sum(everything.astype(jnp.float32), axis=0)


def together(arrays, axis):
    vector, at, finished = (jnp.concatenate([a.reshape(-1) for a in arrays]), 0, [])
    subtotal = over_copies(vector, axis)
    for a in arrays:
        finished.append(subtotal[at : at + a.size].reshape(a.shape))
        at += a.size
    return tuple(finished)


def rms_scale(values):
    return lax.rsqrt(jnp.mean(values * values, axis=1, keepdims=True) + epsilon)


def norm_back(grad_normed, normed, scale, gain):
    scaled = grad_normed * gain
    return scale * (scaled - normed * jnp.mean(scaled * normed, axis=1, keepdims=True))


def outer_all(left, right):
    return lax.dot_general(
        left, right, (((0,), (0,)), ((), ())), preferred_element_type=jnp.float32
    )


def on_device(
    tokens,
    cotangent,
    seq_lengths,
    block_slots,
    mixgain,
    inproj,
    conv_taps,
    outproj,
    glugain,
    gate_weight,
    lift_weight,
    down_weight,
):
    rows_here, width = tokens.shape
    channels = inproj.shape[2]
    hidden_units = gate_weight.shape[1]
    local_blocks = rows_here // BLK
    total_blocks = block_slots.shape[0]
    seq_index = lax.axis_index("seq")
    ch_index = lax.axis_index("ch")
    slots = seq_index * local_blocks + jnp.arange(local_blocks, dtype=jnp.int32)
    matches = (block_slots[None, :] == slots[:, None]).astype(jnp.int32)
    block_ids = jnp.sum(matches * jnp.arange(total_blocks, dtype=jnp.int32)[None, :], axis=1)
    before_slot = jnp.take(block_slots, jnp.maximum(block_ids - 1, 0))
    after_slot = jnp.take(block_slots, jnp.minimum(block_ids + 1, total_blocks - 1))
    has_after = block_ids + 1 < total_blocks
    offsets = jnp.cumsum(seq_lengths) - seq_lengths
    positions = block_ids[:, None] * BLK + jnp.arange(BLK, dtype=jnp.int32)[None, :]
    starts = jnp.max(
        jnp.where(offsets[None, None, :] <= positions[:, :, None], offsets[None, None, :], 0),
        axis=2,
    )
    tap_masks = [
        (positions - shift_by >= starts).astype(jnp.float32)[:, :, None] for shift_by in range(3)
    ]
    resid = tokens.astype(jnp.float32)
    scale_a = rms_scale(resid)
    normed_a = resid * scale_a
    mixer_in = (normed_a * mixgain).astype(jnp.bfloat16)
    projected = jnp.einsum("td,kde->kte", mixer_in, inproj, preferred_element_type=jnp.float32)
    b_proj, c_proj, x_proj = (projected[0], projected[1], projected[2])
    signal = (b_proj * x_proj).astype(jnp.bfloat16)
    blocked = signal.reshape(local_blocks, BLK, channels)
    tails = blocked[:, BLK - 2 :, :]
    all_tails = collect(tails, "seq", 0)
    carried = jnp.take(all_tails, before_slot, axis=0)
    extended = jnp.concatenate([carried, blocked], axis=1).astype(jnp.float32)
    conv_out = jnp.zeros((local_blocks, BLK, channels), jnp.float32)
    for shift_by in range(3):
        conv_out = (
            conv_out
            + conv_taps[shift_by][None, None, :]
            * extended[:, 2 - shift_by : 2 - shift_by + BLK, :]
            * tap_masks[shift_by]
        )
    conv_flat = conv_out.reshape(rows_here, channels)
    gated = (c_proj * conv_flat).astype(jnp.bfloat16)
    mixed = over_copies(jnp.dot(gated, outproj, preferred_element_type=jnp.float32), "ch")
    middle = resid + mixed
    scale_b = rms_scale(middle)
    normed_b = middle * scale_b
    glu_in = (normed_b * glugain).astype(jnp.bfloat16)
    gate_pre = jnp.dot(glu_in, gate_weight, preferred_element_type=jnp.float32)
    lift_pre = jnp.dot(glu_in, lift_weight, preferred_element_type=jnp.float32)
    sigmoid_gate = jax.nn.sigmoid(gate_pre)
    silu_gate = gate_pre * sigmoid_gate
    hidden = (silu_gate * lift_pre).astype(jnp.bfloat16)
    glu_out = taken_together(
        jnp.dot(hidden, down_weight, preferred_element_type=jnp.float32).astype(jnp.bfloat16), "ch"
    ).astype(jnp.float32)
    layer_out = (middle + glu_out).astype(jnp.bfloat16)
    upstream = cotangent.astype(jnp.float32)
    hidden_grad = jnp.dot(cotangent, down_weight.T, preferred_element_type=jnp.float32)
    lift_act = (hidden_grad * silu_gate).astype(jnp.bfloat16)
    gate_act = (
        hidden_grad * lift_pre * sigmoid_gate * (1.0 + gate_pre * (1.0 - sigmoid_gate))
    ).astype(jnp.bfloat16)
    glu_in_grad = taken_together(
        (
            jnp.dot(gate_act, gate_weight.T, preferred_element_type=jnp.float32)
            + jnp.dot(lift_act, lift_weight.T, preferred_element_type=jnp.float32)
        ).astype(jnp.bfloat16),
        "ch",
    ).astype(jnp.float32)
    glugain_term = jnp.sum(glu_in_grad * normed_b, axis=0)
    middle_grad = upstream + norm_back(glu_in_grad, normed_b, scale_b, glugain)
    mixed_grad = middle_grad.astype(jnp.bfloat16)
    gated_grad = jnp.dot(mixed_grad, outproj.T, preferred_element_type=jnp.float32)
    c_grad = (gated_grad * conv_flat).astype(jnp.bfloat16)
    conv_grad = (gated_grad * c_proj).reshape(local_blocks, BLK, channels)
    extended_grad = jnp.zeros((local_blocks, BLK + 2, channels), jnp.float32)
    tap_terms = []
    for shift_by in range(3):
        weighted = conv_grad * tap_masks[shift_by]
        tap_terms.append(
            jnp.sum(weighted * extended[:, 2 - shift_by : 2 - shift_by + BLK, :], axis=(0, 1))
        )
        extended_grad = extended_grad + jnp.pad(
            conv_taps[shift_by][None, None, :] * weighted,
            ((0, 0), (2 - shift_by, shift_by), (0, 0)),
        )
    heads = extended_grad[:, :2, :]
    all_heads = collect(heads, "seq", 0)
    incoming = jnp.where(has_after[:, None, None], jnp.take(all_heads, after_slot, axis=0), 0.0)
    signal_grad = (
        extended_grad[:, 2:, :] + jnp.pad(incoming, ((0, 0), (BLK - 2, 0), (0, 0)))
    ).reshape(rows_here, channels)
    proj_grads = jnp.stack(
        [
            (signal_grad * x_proj).astype(jnp.bfloat16),
            c_grad,
            (signal_grad * b_proj).astype(jnp.bfloat16),
        ]
    )
    mixer_in_grad = taken_together(
        jnp.einsum("kte,kde->td", proj_grads, inproj, preferred_element_type=jnp.float32).astype(
            jnp.bfloat16
        ),
        "ch",
    ).astype(jnp.float32)
    mixgain_term = jnp.sum(mixer_in_grad * normed_a, axis=0)
    input_grad = (middle_grad + norm_back(mixer_in_grad, normed_a, scale_a, mixgain)).astype(
        jnp.bfloat16
    )
    gate_term = outer_all(glu_in, gate_act)
    lift_term = outer_all(glu_in, lift_act)
    down_term = outer_all(cotangent, hidden)
    proj_term = jnp.einsum("tr,kte->rke", mixer_in, proj_grads, preferred_element_type=jnp.float32)
    out_term = outer_all(mixed_grad, gated)
    reduced = lax.psum_scatter(
        jnp.concatenate(
            [
                jnp.concatenate([proj_term.reshape(width, 3 * channels), out_term], axis=1),
                jnp.concatenate([gate_term, lift_term, down_term], axis=1),
            ],
            axis=1,
        ),
        "seq",
        scatter_dimension=0,
        tiled=True,
    )
    mixer_part = reduced[:, : 4 * channels]
    swiglu_part = reduced[:, 4 * channels :]
    rows_out = mixer_part.shape[0]
    inproj_grad = jnp.transpose(
        mixer_part[:, : 3 * channels].reshape(rows_out, 3, channels), (1, 0, 2)
    )
    outproj_grad = mixer_part[:, 3 * channels :].T
    gate_grad = swiglu_part[:, :hidden_units]
    lift_grad = swiglu_part[:, hidden_units : 2 * hidden_units]
    down_grad = swiglu_part[:, 2 * hidden_units :].T
    mix_half = lax.dynamic_slice_in_dim(mixgain_term, ch_index * channels, channels, 0)
    glu_half = lax.dynamic_slice_in_dim(glugain_term, ch_index * channels, channels, 0)
    mixgain_grad, glugain_grad, taps_grad = together(
        (mix_half, glu_half, jnp.stack(tap_terms)), "seq"
    )
    return (
        layer_out,
        input_grad,
        mixgain_grad,
        inproj_grad,
        taps_grad,
        outproj_grad,
        glugain_grad,
        gate_grad,
        lift_grad,
        down_grad,
    )


def solution(mesh):
    in_specs = (
        P("seq", None),
        P("seq", None),
        P(),
        P(),
        P(),
        P(None, None, "ch"),
        P(None, "ch"),
        P("ch", None),
        P(),
        P(None, "ch"),
        P(None, "ch"),
        P("ch", None),
    )
    out_specs = (
        P("seq", None),
        P("seq", None),
        P("ch"),
        P(None, "seq", "ch"),
        P(None, "ch"),
        P("ch", "seq"),
        P("ch"),
        P("seq", "ch"),
        P("seq", "ch"),
        P("ch", "seq"),
    )
    return jax.shard_map(
        on_device, mesh=mesh, in_specs=in_specs, out_specs=out_specs, check_vma=False
    )
```

profile of v0, /device:TPU:0, one launch (start us, length us, event | category | flops | bytes accessed | tf_op | source)
XLA Modules:
  0.0 881.1 jit_solution(16586147356240797843)
XLA Ops:
  7.2 1.3 fusion.14
  8.5 4.3 convolution_bitcast_fusion.1
  12.9 1.0 copy-done.7
  14.8 11.5 %all-to-all-start = ((bf16[64,1,2,768]{3,2,1,0:T(2,128)(2,1)}), bf16[64,1,2,768]{3,2,1,0:T(2,128)(2,1)S(1)}, u32[]{:S(2)}, u32[]{:S(2)}) async-start(bf16[64,1,2,768]{3,2,1,0:T(2,128)(2,1)} %broadcast_in_dim.96), calls=%async_computation | async-start | bytes 393216 | tf_op jit(solution)/shard_map/all_to_all | solution.py:14
  30.5 5.8 all-to-all-done
  37.2 1.9 fusion.19
  40.5 5.8 all_to_all.36
  46.4 1.6 reduce_sum.137
  48.2 0.9 copy-done.3
  49.3 7.1 fusion.38
  56.4 2.9 fusion.37
  59.3 9.6 %multiply_convert_fusion = (bf16[128,3456]{1,0:T(8,128)(2,1)S(1)}, bf16[128,3456]{1,0:T(8,128)(2,1)}, bf16[128,3456]{1,0:T(8,128)(2,1)S(1)}) fusion(f32[128,3456]{1,0:T(8,128)} %fusion.37, f32[128,3456]{1,0:T(8,128)} %fusion.38, bf16[128,1536]{1,0:T(8,128)(2,1)S(1)} %copy-done.18, bf16[3456,1536]{1,0:T(8,128)(2,1)} %param.23), kind=kOutput, calls=%fused_computation.9 | convolution fusion | flops 1365590016 | bytes 17203200 | tf_op jit(solution)/shard_map/dot_general | solution.py:135
  68.9 6.4 convolution_convert_fusion
  75.3 3.5 fusion.39
  78.8 7.5 fusion
  86.4 5.2 all_to_all.37
  91.5 0.9 broadcast_in_dim.100
  92.5 4.5 all-to-all-start.2
  97.0 1.3 convert_reduce_fusion.1
  98.3 0.9 copy-done.12
  99.2 2.0 multiply_reduce_fusion
  101.8 1.4 convert_reduce_fusion.2
  103.2 2.4 multiply_add_fusion
  105.7 0.9 copy-done.4
  106.6 3.0 fusion.18
  110.7 5.0 all-to-all-start.4
  116.5 11.4 %all-to-all-done.4 = f32[64,1,2,768]{3,2,1,0:T(2,128)S(1)} async-done(((f32[64,1,2,768]{3,2,1,0:T(2,128)}), f32[64,1,2,768]{3,2,1,0:T(2,128)S(1)}, u32[]{:S(2)}, u32[]{:S(2)}) %all-to-all-start.4) | async-done | bytes 393248 | tf_op jit(solution)/shard_map/all_to_all | solution.py:14
  127.9 1.2 multiply_convert_fusion.5
  129.1 7.9 fusion.22
  137.0 15.2 %copy.45 = f32[1536,2304]{1,0:T(8,128)} copy(f32[1536,2304]{0,1:T(8,128)} %bitcast.99) | data formatting | bytes 28311552 | tf_op jit(solution)/shard_map/reshape | solution.py:195
  152.2 11.4 %constant_dynamic-update-slice_fusion = f32[1536,13440]{1,0:T(8,128)} fusion(f32[1536,2304]{1,0:T(8,128)} %copy.45), kind=kLoop, calls=%fused_computation.72 | loop fusion | bytes 28311552
  163.6 3.0 convolution_dynamic-update-slice_fusion.2
  166.6 10.3 %convolution_dynamic-update-slice_fusion.1 = f32[1536,13440]{1,0:T(8,128)} fusion(f32[1536,13440]{1,0:T(8,128)} %convolution_dynamic-update-slice_fusion.2, bf16[128,1536]{1,0:T(8,128)(2,1)S(1)} %multiply_convert_fusion.3, bf16[128,3456]{1,0:T(8,128)(2,1)} %get-tuple-element.113), kind=kOutput, calls=%fused_computation.1 | convolution fusion | flops 1358954496 | bytes 22511616 | tf_op jit(solution)/shard_map/dot_general | solution.py:57
  176.9 9.0 %convolution_dynamic-update-slice_fusion = f32[1536,13440]{1,0:T(8,128)} fusion(f32[1536,13440]{1,0:T(8,128)} %convolution_dynamic-update-slice_fusion.1, bf16[128,1536]{1,0:T(8,128)(2,1)S(1)} %multiply_convert_fusion.3, bf16[128,3456]{1,0:T(8,128)(2,1)S(1)} %copy-done.14), kind=kOutput, calls=%fused_computation | convolution fusion | flops 1358954496 | bytes 22511616 | tf_op jit(solution)/shard_map/dot_general | solution.py:57
  185.9 8.9 %bitcast_dynamic-update-slice_fusion = f32[1536,13440]{1,0:T(8,128)} fusion(f32[1536,13440]{1,0:T(8,128)} %convolution_dynamic-update-slice_fusion, bf16[128,3456]{1,0:T(8,128)(2,1)S(1)} %copy-done.10, bf16[128,1536]{1,0:T(8,128)(2,1)S(1)} %copy-done.18), kind=kOutput, calls=%fused_computation.2 | convolution fusion | flops 1358954496 | bytes 22511616 | tf_op jit(solution)/shard_map/dot_general | solution.py:57
  196.3 5.7 fusion.1
  202.0 4.5 all_to_all.38
  206.7 0.9 copy-done.11
  208.0 1.5 broadcast_in_dim.110
  209.4 5.5 all-to-all-start.6
  214.9 1.2 dynamic-slice.16
  216.8 2.2 fusion.12
  219.0 23.8 %all-to-all-done.6 = f32[64,1,3840]{2,1,0:T(1,128)} async-done(((f32[64,1,3840]{2,1,0:T(1,128)}), f32[64,1,3840]{2,1,0:T(1,128)}, u32[]{:S(2)}, u32[]{:S(2)}) %all-to-all-start.6) | async-done | bytes 983072 | tf_op jit(solution)/shard_map/all_to_all | solution.py:14
  242.8 1.8 reduce_sum.149
  245.8 622.6 %all-reduce.7.cloned.1.call-done = f32[1536,13440]{1,0:T(8,128)} async-done(((f32[1536,13440]{1,0:T(8,128)}), f32[1536,13440]{1,0:T(8,128)}) %all-reduce.7.cloned.1.call-update) | async-done | bytes 82575376
  868.4 0.9 constant_dynamic-slice_fusion
  870.2 1.6 dynamic-slice_bitcast_fusion.1
  871.8 2.4 dynamic-slice_bitcast_fusion
  (130 shorter events, 10.8 us)
Async XLA Ops:
  7.2 32.6 %copy-start = (bf16[768,1536]{1,0:T(8,128)(2,1)S(1)}, bf16[768,1536]{1,0:T(8,128)(2,1)}, u32[]{:S(2)}) copy-start(bf16[768,1536]{1,0:T(8,128)(2,1)} %param.19) | copy-start | bytes 7077892
  7.2 19.1 %copy-start.39 = (s32[64]{0:T(128)S(1)}, s32[64]{0:T(128)}, u32[]{:S(2)}) copy-start(s32[64]{0:T(128)} %param.15) | copy-start | bytes 772
  7.2 22.9 %copy-start.40 = (s32[4]{0:T(128)S(1)}, s32[4]{0:T(128)}, u32[]{:S(2)}) copy-start(s32[4]{0:T(128)} %param.14) | copy-start | bytes 52
  7.2 23.1 %copy-start.37 = (f32[3,768]{1,0:T(4,128)S(1)}, f32[3,768]{1,0:T(4,128)}, u32[]{:S(2)}) copy-start(f32[3,768]{1,0:T(4,128)} %param.18) | copy-start | bytes 27652
  8.5 5.4 copy-start.29
  12.9 1.0 copy-start.7
  14.8 21.6 %all-to-all-start = ((bf16[64,1,2,768]{3,2,1,0:T(2,128)(2,1)}), bf16[64,1,2,768]{3,2,1,0:T(2,128)(2,1)S(1)}, u32[]{:S(2)}, u32[]{:S(2)}) async-start(bf16[64,1,2,768]{3,2,1,0:T(2,128)(2,1)} %broadcast_in_dim.96), calls=%async_computation | async-start | bytes 393216 | tf_op jit(solution)/shard_map/all_to_all | solution.py:14
  26.3 21.7 %copy-start.2 = (bf16[128,1536]{1,0:T(8,128)(2,1)S(1)}, bf16[128,1536]{1,0:T(8,128)(2,1)}, u32[]{:S(2)}) copy-start(bf16[128,1536]{1,0:T(8,128)(2,1)} %param.12) | copy-start | bytes 1179652
  30.4 10.1 %copy-start.23 = (f32[768]{0:T(1024)}, f32[768]{0:T(1024)S(1)}, u32[]{:S(2)}) copy-start(f32[768]{0:T(1024)S(1)} %get-tuple-element.103) | copy-start | bytes 9220
  30.5 10.0 %copy-start.31 = (f32[128]{0:T(128)}, f32[128]{0:T(128)S(1)}, u32[]{:S(2)}) copy-start(f32[128]{0:T(128)S(1)} %get-tuple-element.126) | copy-start | bytes 1540
  30.5 10.0 %copy-start.33 = (f32[128]{0:T(128)}, f32[128]{0:T(128)S(1)}, u32[]{:S(2)}) copy-start(f32[128]{0:T(128)S(1)} %get-tuple-element.127) | copy-start | bytes 1540
  30.5 10.0 %copy-start.35 = (f32[128]{0:T(128)}, f32[128]{0:T(128)S(1)}, u32[]{:S(2)}) copy-start(f32[128]{0:T(128)S(1)} %get-tuple-element.128) | copy-start | bytes 1540
  36.4 0.8 copy-start.8
  39.1 10.0 %copy-start.21 = (f32[1536]{0:T(1024)S(1)}, f32[1536]{0:T(1024)}, u32[]{:S(2)}) copy-start(f32[1536]{0:T(1024)} %param.20) | copy-start | bytes 18436
  48.0 8.4 slice-start
  48.2 0.9 copy-start.3
  48.2 1.1 copy-start.38
  49.3 7.1 slice-start.1
  49.3 7.1 slice-start.2
  56.4 2.9 copy-start.18
  68.9 6.4 copy-start.9
  68.9 9.9 %copy-start.13 = (bf16[128,3456]{1,0:T(8,128)(2,1)}, bf16[128,3456]{1,0:T(8,128)(2,1)S(1)}, u32[]{:S(2)}) copy-start(bf16[128,3456]{1,0:T(8,128)(2,1)S(1)} %get-tuple-element.112) | copy-start | bytes 2654212
  68.9 6.4 copy-start.15
  92.5 9.3 %all-to-all-start.2 = ((bf16[2,128,1536]{2,1,0:T(8,128)(2,1)}), bf16[2,128,1536]{2,1,0:T(8,128)(2,1)}, u32[]{:S(2)}, u32[]{:S(2)}) async-start(bf16[2,128,1536]{2,1,0:T(8,128)(2,1)} %broadcast_in_dim.100), calls=%async_computation.2 | async-start | bytes 1572864 | tf_op jit(solution)/shard_map/all_to_all | solution.py:14
  98.3 0.9 copy-start.12
  101.8 7.8 copy-start.19
  101.8 7.8 copy-start.24
  101.8 7.8 copy-start.32
  101.8 7.8 copy-start.34
  101.8 7.8 copy-start.36
  105.7 0.9 copy-start.4
  105.7 23.5 %copy-start.20 = (f32[1536]{0:T(1024)S(1)}, f32[1536]{0:T(1024)}, u32[]{:S(2)}) copy-start(f32[1536]{0:T(1024)} %param.16) | copy-start | bytes 18436
  110.7 17.3 %all-to-all-start.4 = ((f32[64,1,2,768]{3,2,1,0:T(2,128)}), f32[64,1,2,768]{3,2,1,0:T(2,128)S(1)}, u32[]{:S(2)}, u32[]{:S(2)}) async-start(f32[64,1,2,768]{3,2,1,0:T(2,128)} %broadcast_in_dim.106), calls=%async_computation.4 | async-start | bytes 786432 | tf_op jit(solution)/shard_map/all_to_all | solution.py:14
  115.7 752.7 %all-reduce.7.cloned.1.call-start = ((), (), s32[]{:S(2)}) async-start(), calls=%async_computation.7 | async-start | bytes 165150720
  152.2 11.4 %copy-start.5 = (f32[128,1536]{1,0:T(8,128)S(1)}, f32[128,1536]{1,0:T(8,128)}, u32[]{:S(2)}) copy-start(f32[128,1536]{1,0:T(8,128)} %copy-done.4) | copy-start | bytes 2359300
  152.2 11.4 %copy-start.17 = (bf16[128,768]{1,0:T(8,128)(2,1)S(1)}, bf16[128,768]{1,0:T(8,128)(2,1)}, u32[]{:S(2)}) copy-start(bf16[128,768]{1,0:T(8,128)(2,1)} %copy-done.16) | copy-start | bytes 589828
  166.6 10.3 %copy-start.14 = (bf16[128,3456]{1,0:T(8,128)(2,1)S(1)}, bf16[128,3456]{1,0:T(8,128)(2,1)}, u32[]{:S(2)}) copy-start(bf16[128,3456]{1,0:T(8,128)(2,1)} %copy-done.13) | copy-start | bytes 2654212
  176.9 9.0 %copy-start.10 = (bf16[128,3456]{1,0:T(8,128)(2,1)S(1)}, bf16[128,3456]{1,0:T(8,128)(2,1)}, u32[]{:S(2)}) copy-start(bf16[128,3456]{1,0:T(8,128)(2,1)} %copy-done.9) | copy-start | bytes 2654212
  194.8 0.7 copy-start.28
  194.8 0.7 copy-start.27
  194.8 0.7 copy-start.26
  194.8 1.3 copy-start.25
  196.3 11.3 %copy-start.30 = (f32[128]{0:T(128)S(1)}, f32[128]{0:T(128)}, u32[]{:S(2)}) copy-start(f32[128]{0:T(128)} %copy-done.29) | copy-start | bytes 1540
  196.3 11.7 %copy-start.22 = (f32[2304]{0:T(1024)S(1)}, f32[2304]{0:T(1024)}, u32[]{:S(2)}) copy-start(f32[2304]{0:T(1024)} %reshape.330) | copy-start | bytes 27652
  196.3 20.6 %copy-start.6 = (f32[128,1536]{1,0:T(8,128)S(1)}, f32[128,1536]{1,0:T(8,128)}, u32[]{:S(2)}) copy-start(f32[128,1536]{1,0:T(8,128)} %copy-done.4) | copy-start | bytes 2359300
  202.0 672.3 %copy-start.1 = (bf16[768,1536]{1,0:T(8,128)(2,1)S(1)}, bf16[768,1536]{1,0:T(8,128)(2,1)}, u32[]{:S(2)}) copy-start(bf16[768,1536]{1,0:T(8,128)(2,1)} %param.19) | copy-start | bytes 7077892
  206.7 0.9 copy-start.11
  209.4 33.4 %all-to-all-start.6 = ((f32[64,1,3840]{2,1,0:T(1,128)}), f32[64,1,3840]{2,1,0:T(1,128)}, u32[]{:S(2)}, u32[]{:S(2)}) async-start(f32[64,1,3840]{2,1,0:T(1,128)} %broadcast_in_dim.110), calls=%async_computation.6 | async-start | bytes 1966080 | tf_op jit(solution)/shard_map/all_to_all | solution.py:14
  (1 other events, 0.7 us)
Sparse Core Ops, SparseCore 0:
  195.0 673.3 all-reduce.6
where the time goes:
time: 882 us; the launch traced here: 881 us
  waiting for transfers between devices  664 us (75%)
  matrix products  89.6 us (10%)
  local copies, waits for them, and re-layouts  47.5 us (5%)
  starting transfers between devices  26.6 us (3%)
  other arithmetic  19.8 us (2%)
  between operations  18.6 us (2%)
  blocking collectives  15.5 us (2%)
    unnamed x2, waiting for transfers between devices  623 us
    all_to_all x4, waiting for transfers between devices, from_everyone(): return lax.all_to_all(copies, axis, split_axis=0, concat_axis=0, tiled=True)  41 us
    dot_general x4, matrix products, outer_all(): lax.dot_general(left, right, (((0,), (0,)), ((), ())), preferred_element_...  31.3 us
    all_to_all x4, starting transfers between devices, from_everyone(): return lax.all_to_all(copies, axis, split_axis=0, concat_axis=0, tiled=True)  26.5 us
    unnamed x91, local copies, waits for them, and re-layouts  20.2 us
  transfers between devices with their start and end apart: 5, of which 4 were waited for; matrix products, arithmetic and copies ran while one was open for 2% of the time, Pallas kernels for 0%

commit v1 on v0

--- a/solution.py
+++ b/solution.py
@@ -1,7 +1,230 @@
 import jax
 import jax.numpy as jnp
 from jax import lax
+from jax.experimental import pallas as pl
+from jax.experimental.pallas import tpu as pltpu
+
 from jax.sharding import PartitionSpec as P
+
+MESH = pl.DeviceIdType.MESH
+F32, BF16 = jnp.float32, jnp.bfloat16
+WS, WM = 896, 256
+
+
+def spots():
+    s = lax.axis_index("seq")
+    return (s // 16, (s // 4) % 4, s % 4), lax.axis_index("ch")
+
+
+def peer(place, axis, step):
+    moved = [(place[i] + step) % 4 if i == axis else place[i] for i in range(3)]
+    return moved[0] * 16 + moved[1] * 4 + moved[2]
+
+
+def wide_start(i):
+    return pl.multiple_of(jnp.minimum(i * WS, 3456 - WS), 128)
+
+
+def grads_kernel(
+    n2t, cott, n1t, d_gate, d_lift, hidden, mixed_r,
+    o_gate, o_lift, o_down, o_in, o_out,
+    s_left, s_right, s_bsend, s_bland, s_csend, s_cland, s_dsend, s_dland,
+    m_left, m_right, m_bsend, m_bland, m_csend, m_cland, m_dsend, m_dland,
+    l_send, l_recv, f_send, f_recv, r_send, r_recv,
+    b_send, b_recv, c_send, c_recv, d_send, d_recv, own_sem,
+):
+    place, core = spots()
+    barrier = pltpu.get_barrier_semaphore()
+    for axis in range(3):
+        for step in range(1, 4):
+            pl.semaphore_signal(barrier, inc=1, device_id=(peer(place, axis, step), core), device_id_type=MESH)
+    pl.semaphore_signal(barrier, inc=1, device_id=(lax.axis_index("seq"), 1 - core), device_id_type=MESH)
+    pl.semaphore_wait(barrier, 10)
+
+    def push(src, dst, send, recv, axis, step):
+        copy = pltpu.make_async_remote_copy(
+            src_ref=src, dst_ref=dst, send_sem=send, recv_sem=recv,
+            device_id=(peer(place, axis, step), core), device_id_type=MESH)
+        copy.start()
+        return copy
+
+    def cross(src, dst, send, recv):
+        copy = pltpu.make_async_remote_copy(
+            src_ref=src, dst_ref=dst, send_sem=send, recv_sem=recv,
+            device_id=(lax.axis_index("seq"), 1 - core), device_id_type=MESH)
+        copy.start()
+        return copy
+
+    half = pl.ds(pl.multiple_of(core * 768, 768), 768)
+    bufs = (
+        (WS, s_left, s_right, s_bsend, s_bland, s_csend, s_cland, s_dsend, s_dland),
+        (WM, m_left, m_right, m_bsend, m_bland, m_csend, m_cland, m_dsend, m_dland),
+    )
+
+    def start_a(job, k):
+        width, left, right = bufs[job][:3]
+        me = place[k]
+        sent, own = [], []
+        for step in range(4):
+            target = (me + step) % 4
+            lanes = pl.ds(128 * step, 128)
+            if job == 0:
+                src_l = (n2t, n2t, cott)[k]
+                src_r = (d_gate, d_lift, hidden)[k].at[:, pl.ds(wide_start(target), WS)]
+            else:
+                src_l = n1t.at[jnp.where(target == 3, 1, 0)]
+                src_r = mixed_r.at[k, :, pl.ds(pl.multiple_of(target * WM, WM), WM)]
+            if step == 0:
+                a = pltpu.make_async_copy(src_l, left.at[k, :, lanes], own_sem.at[job, k, 0])
+                b = pltpu.make_async_copy(src_r, right.at[k, pl.ds(0, 128), :], own_sem.at[job, k, 1])
+                a.start()
+                b.start()
+                own += [a, b]
+            else:
+                sent.append((
+                    push(src_l.at[half, :], left.at[k, half, lanes], l_send.at[job, k, step - 1], l_recv.at[job, k, step - 1], k, step),
+                    push(src_r, right.at[k, pl.ds(128 * step, 128), :], r_send.at[job, k, step - 1], r_recv.at[job, k, step - 1], k, step),
+                ))
+        return sent, own
+
+    def forward_a(job, k, started):
+        left = bufs[job][1]
+        out = []
+        for step, (lc, rc) in zip(range(1, 4), started[0]):
+            lc.wait()
+            view = left.at[k, half, pl.ds(128 * step, 128)]
+            out.append(cross(view, view, f_send.at[job, k, step - 1], f_recv.at[job, k, step - 1]))
+        return out
+
+    def finish_a(started, forwarded):
+        for c in started[1]:
+            c.wait()
+        for lc, rc in started[0]:
+            rc.wait()
+        for c in forwarded:
+            c.wait()
+
+    def start_b(job, k):
+        width, left, right, bsend, bland = bufs[job][:5]
+
+        def slab(x, carry):
+            acc = jnp.dot(left[k, pl.ds(pl.multiple_of(x * 384, 384), 384), :], right[k], preferred_element_type=F32)
+            for j in range(4):
+                if k == 0:
+                    bsend[k, j, x] = acc[96 * j:96 * j + 96].astype(BF16)
+                elif k == 1:
+                    bsend[k, j, x] = jnp.concatenate([acc[96 * y + 24 * j:96 * y + 24 * j + 24] for y in range(4)], axis=0).astype(BF16)
+                else:
+                    bsend[k, x, j] = acc[96 * j:96 * j + 96].astype(BF16)
+            return carry
+
+        lax.fori_loop(0, 4, slab, 0)
+        axis = (k + 1) % 3
+        return [
+            push(bsend.at[k, (place[axis] + step) % 4], bland.at[k, step - 1], b_send.at[job, k, step - 1], b_recv.at[job, k, step - 1], axis, step)
+            for step in range(1, 4)
+        ]
+
+    def start_c(job, k, started):
+        width, _, _, bsend, bland, csend, cland = bufs[job][:7]
+        for c in started:
+            c.wait()
+        me = place[(k + 1) % 3]
+
+        def summed(q):
+            return (bsend[k, me, q].astype(F32) + bland[k, 0, q].astype(F32)
+                    + bland[k, 1, q].astype(F32) + bland[k, 2, q].astype(F32))
+
+        if k == 0:
+            for p in range(2):
+                a, b = summed(2 * p), summed(2 * p + 1)
+                for j in range(4):
+                    csend[k, j, 48 * p:48 * p + 48] = jnp.concatenate([a[24 * j:24 * j + 24], b[24 * j:24 * j + 24]], axis=0).astype(BF16)
+        else:
+            for q in range(4):
+                csend[k, q] = summed(q).astype(BF16)
+        axis = (k + 2) % 3
+        return [
+            push(csend.at[k, (place[axis] + step) % 4], cland.at[k, step - 1], c_send.at[job, k, step - 1], c_recv.at[job, k, step - 1], axis, step)
+            for step in range(1, 4)
+        ]
+
+    def start_d(job, k, started):
+        width, _, _, _, _, csend, cland, dsend, dland = bufs[job]
+        for c in started:
+            c.wait()
+        total = (csend[k, place[(k + 2) % 3]].astype(F32) + cland[k, 0].astype(F32)
+                 + cland[k, 1].astype(F32) + cland[k, 2].astype(F32))
+        for j in range(4):
+            dsend[k, j] = total[24 * j:24 * j + 24]
+        dland[k, 0] = dsend[k, place[k]]
+        return [
+            push(dsend.at[k, (place[k] + step) % 4], dland.at[k, step], d_send.at[job, k, step - 1], d_recv.at[job, k, step - 1], k, step)
+            for step in range(1, 4)
+        ]
+
+    def finish(job, k, started):
+        dland = bufs[job][8]
+        for c in started:
+            c.wait()
+        me = place[k]
+        for i in range(4):
+            slot = (me - i + 4) % 4
+            if job == 0:
+                out = (o_gate, o_lift, o_down)[k]
+                if i < 3:
+                    out[:, WS * i:WS * i + WS] = dland[k, slot]
+                else:
+                    out[:, WS * 3:3456] = dland[k, slot, :, 128:WS]
+            elif i < 3:
+                o_in[k, :, WM * i:WM * i + WM] = dland[k, slot]
+            else:
+                o_out[:, WM * k:WM * k + WM] = dland[k, slot]
+
+    a = {(j, k): start_a(j, k) for j in range(2) for k in range(3)}
+    b, c, d = {}, {}, {}
+    for j in range(2):
+        f = {k: forward_a(j, k, a[j, k]) for k in range(3)}
+        for k in range(3):
+            finish_a(a[j, k], f[k])
+            b[j, k] = start_b(j, k)
+    for j in range(2):
+        for k in range(3):
+            c[j, k] = start_c(j, k, b[j, k])
+    for j in range(2):
+        for k in range(3):
+            d[j, k] = start_d(j, k, c[j, k])
+    for j in range(2):
+        for k in range(3):
+            finish(j, k, d[j, k])
+
+
+def job_scratch(w):
+    return [
+        pltpu.VMEM((3, 1536, 512), BF16),
+        pltpu.VMEM((3, 512, w), BF16),
+        pltpu.VMEM((3, 4, 4, 96, w), BF16),
+        pltpu.VMEM((3, 3, 4, 96, w), BF16),
+        pltpu.VMEM((3, 4, 96, w), BF16),
+        pltpu.VMEM((3, 3, 96, w), BF16),
+        pltpu.VMEM((3, 4, 24, w), F32),
+        pltpu.VMEM((3, 4, 24, w), F32),
+    ]
+
+
+def weight_grads(n2t, cott, n1t, d_gate, d_lift, hidden, mixed_r):
+    vm = pl.BlockSpec(memory_space=pltpu.VMEM)
+    dma = pltpu.SemaphoreType.DMA
+    return pl.pallas_call(
+        grads_kernel,
+        out_shape=[jax.ShapeDtypeStruct(s, F32) for s in ((24, 3456), (24, 3456), (24, 3456), (3, 24, 768), (24, 768))],
+        in_specs=[vm] * 7,
+        out_specs=[vm] * 5,
+        scratch_shapes=job_scratch(WS) + job_scratch(WM) + [dma((2, 3, 3))] * 12 + [dma((2, 3, 2))],
+        compiler_params=pltpu.CompilerParams(collective_id=1, has_side_effects=True, vmem_limit_bytes=62 << 20),
+        name="weight_grads",
+    )(n2t, cott, n1t, d_gate, d_lift, hidden, mixed_r)
+
 
 BLK = 128
 
@@ -51,12 +274,6 @@
 def norm_back(grad_normed, normed, scale, gain):
     scaled = grad_normed * gain
     return scale * (scaled - normed * jnp.mean(scaled * normed, axis=1, keepdims=True))
-
-
-def outer_all(left, right):
-    return lax.dot_general(
-        left, right, (((0,), (0,)), ((), ())), preferred_element_type=jnp.float32
-    )
 
 
 def on_device(
@@ -184,33 +401,20 @@
     input_grad = (middle_grad + norm_back(mixer_in_grad, normed_a, scale_a, mixgain)).astype(
         jnp.bfloat16
     )
-    gate_term = outer_all(glu_in, gate_act)
-    lift_term = outer_all(glu_in, lift_act)
-    down_term = outer_all(cotangent, hidden)
-    proj_term = jnp.einsum("tr,kte->rke", mixer_in, proj_grads, preferred_element_type=jnp.float32)
-    out_term = outer_all(mixed_grad, gated)
-    reduced = lax.psum_scatter(
-        jnp.concatenate(
-            [
-                jnp.concatenate([proj_term.reshape(width, 3 * channels), out_term], axis=1),
-                jnp.concatenate([gate_term, lift_term, down_term], axis=1),
-            ],
-            axis=1,
-        ),
-        "seq",
-        scatter_dimension=0,
-        tiled=True,
-    )
-    mixer_part = reduced[:, : 4 * channels]
-    swiglu_part = reduced[:, 4 * channels :]
-    rows_out = mixer_part.shape[0]
-    inproj_grad = jnp.transpose(
-        mixer_part[:, : 3 * channels].reshape(rows_out, 3, channels), (1, 0, 2)
-    )
-    outproj_grad = mixer_part[:, 3 * channels :].T
-    gate_grad = swiglu_part[:, :hidden_units]
-    lift_grad = swiglu_part[:, hidden_units : 2 * hidden_units]
-    down_grad = swiglu_part[:, 2 * hidden_units :].T
+    mixed_right = jnp.stack(
+        [jnp.concatenate([proj_grads[k], gated[:, 256 * k : 256 * k + 256]], axis=1) for k in range(3)]
+    )
+    gate_grad, lift_grad, down_rows, inproj_grad, out_rows = weight_grads(
+        glu_in.T,
+        cotangent.T,
+        jnp.stack([mixer_in.T, mixed_grad.T]),
+        gate_act,
+        lift_act,
+        hidden,
+        mixed_right,
+    )
+    down_grad = down_rows.T
+    outproj_grad = out_rows.T
     mix_half = lax.dynamic_slice_in_dim(mixgain_term, ch_index * channels, channels, 0)
     glu_half = lax.dynamic_slice_in_dim(glugain_term, ch_index * channels, channels, 0)
     mixgain_grad, glugain_grad, taps_grad = together(

time: 882 us -> 249 us (0.28)
  waiting for transfers between devices: 664 us -> 13.2 us
  Pallas kernels: 0 us -> 100 us
  matrix products: 89.6 us -> 45.8 us
  local copies, waits for them, and re-layouts: 47.5 us -> 20.7 us
  between operations: 18.6 us -> 4.59 us
    unnamed x2 -> x0, waiting for transfers between devices: 623 us -> none
    pallas_call x0 -> x1, Pallas kernels: none -> 100 us  [weight_grads(): pl.pallas_call(grads_kernel, out_shape=[jax.ShapeDtypeStruct(s, F32) for...]
    dot_general x5 -> x0, matrix products: 39.1 us -> none  [the longest x4 31.3 us: outer_all(): lax.dot_general(left, right, (((0,), (0,)), ((), ())), preferred_element_...]
    all_to_all x4 -> x3, waiting for transfers between devices: 41 us -> 13.2 us  [from_everyone(): return lax.all_to_all(copies, axis, split_axis=0, concat_axis=0, tiled=True)]
    reshape x2 -> x0, local copies, waits for them, and re-layouts: 15.3 us -> none  [the longest x1 15.2 us: on_device(): proj_term.reshape(width, 3 * channels)]
    unnamed x91 -> x73, local copies, waits for them, and re-layouts: 20.2 us -> 8.53 us
    all_to_all x4 -> x3, starting transfers between devices: 26.5 us -> 23 us  [from_everyone(): return lax.all_to_all(copies, axis, split_axis=0, concat_axis=0, tiled=True)]
    all_to_all x3 -> x4, blocking collectives: 15.5 us -> 18.9 us  [from_everyone(): return lax.all_to_all(copies, axis, split_axis=0, concat_axis=0, tiled=True)]
  transfers between devices with their start and end apart: 5 -> 3, of which waited for: 4 -> 2; matrix products, arithmetic and copies ran while one was open for 2% -> 4% of each run, Pallas kernels for 0% -> 40%
where the time goes in v1:
time: 249 us; the launch traced here: 247 us
  Pallas kernels  100 us (40%)
  matrix products  45.8 us (18%)
  starting transfers between devices  23 us (9%)
  other arithmetic  20.8 us (8%)
  local copies, waits for them, and re-layouts  20.7 us (8%)
  blocking collectives  18.9 us (8%)
  waiting for transfers between devices  13.2 us (5%)
  between operations  4.59 us (2%)
    pallas_call x1, Pallas kernels, weight_grads(): pl.pallas_call(grads_kernel, out_shape=[jax.ShapeDtypeStruct(s, F32) for...  100 us
    all_to_all x3, starting transfers between devices, from_everyone(): return lax.all_to_all(copies, axis, split_axis=0, concat_axis=0, tiled=True)  23 us
    all_to_all x4, blocking collectives, from_everyone(): return lax.all_to_all(copies, axis, split_axis=0, concat_axis=0, tiled=True)  18.9 us
    all_to_all x3, waiting for transfers between devices, from_everyone(): return lax.all_to_all(copies, axis, split_axis=0, concat_axis=0, tiled=True)  13.2 us
    dot_general x1, matrix products, on_device(): jnp.dot(cotangent, down_weight.T, preferred_element_type=jnp.float32)  8.84 us
    unnamed x73, local copies, waits for them, and re-layouts  8.53 us
    dot_general x1, matrix products, on_device(): jnp.dot(gate_act, gate_weight.T, preferred_element_type=jnp.float32)  8.2 us
    dot_general x1, matrix products, on_device(): lift_pre = jnp.dot(glu_in, lift_weight, preferred_element_type=jnp.float32)  5.89 us
  transfers between devices with their start and end apart: 3, of which 2 were waited for; matrix products, arithmetic and copies ran while one was open for 4% of the time, Pallas kernels for 40%

profile of v1, /device:TPU:0, one launch (start us, length us, event | category | flops | bytes accessed | tf_op | source)
XLA Modules:
  0.0 247.2 jit_solution(747127414908937427)
XLA Ops:
  0.6 1.2 copy.40
  2.1 4.3 %convolution_bitcast_fusion.1 = f32[3,128,768]{2,1,0:T(8,128)S(1)} fusion(bf16[3,1536,768]{2,1,0:T(8,128)(2,1)} %param.17, bf16[128,1536]{0,1:T(8,128)(2,1)S(1)} %copy.40, f32[1536]{0:T(1024)} %param.16, f32[128]{0:T(128)S(1)} %add_rsqrt_fusion.1), kind=kOutput, calls=%fused_computation.13 | convolution fusion | flops 906756096 | bytes 8657408 | tf_op jit(solution)/shard_map/td,kde->kte/dot_general | solution.py:319
  6.5 0.8 broadcast_in_dim.96
  7.3 11.5 %all-to-all-start = ((bf16[64,1,2,768]{3,2,1,0:T(2,128)(2,1)}), bf16[64,1,2,768]{3,2,1,0:T(2,128)(2,1)S(1)}, u32[]{:S(2)}, u32[]{:S(2)}) async-start(bf16[64,1,2,768]{3,2,1,0:T(2,128)(2,1)} %broadcast_in_dim.96), calls=%async_computation | async-start | bytes 393216 | tf_op jit(solution)/shard_map/all_to_all | solution.py:237
  23.9 5.0 %all-to-all-done = bf16[64,1,2,768]{3,2,1,0:T(2,128)(2,1)S(1)} async-done(((bf16[64,1,2,768]{3,2,1,0:T(2,128)(2,1)}), bf16[64,1,2,768]{3,2,1,0:T(2,128)(2,1)S(1)}, u32[]{:S(2)}, u32[]{:S(2)}) %all-to-all-start) | async-done | bytes 196640 | tf_op jit(solution)/shard_map/all_to_all | solution.py:237
  29.0 0.9 fusion.23
  29.9 0.8 copy-done
  31.4 5.8 %all_to_all.36 = f32[2,128,1536]{2,1,0:T(8,128)} all-to-all(f32[2,128,1536]{2,1,0:T(8,128)S(1)} %broadcast_in_dim.99), channel_id=1, replica_groups=mesh['seq'=64,'ch'=2] {'ch'}, dimensions={0} | all-to-all | bytes 3145728 | tf_op jit(solution)/shard_map/all_to_all | solution.py:237
  37.2 1.6 reduce_sum.137
  38.8 1.2 copy.42
  40.0 1.5 multiply_reduce_fusion.2
  41.5 5.9 %fusion.40 = f32[128,3456]{1,0:T(8,128)S(1)} fusion(bf16[1536,3456]{1,0:T(8,128)(2,1)} %param.22, f32[128,1536]{0,1:T(8,128)S(1)} %get-tuple-element.108, f32[1536]{0:T(1024)S(1)} %copy-done.12, f32[128]{0:T(128)S(1)} %add_rsqrt_fusion), kind=kOutput, calls=%fused_computation.100 | convolution fusion | flops 1359544320 | bytes 13179392 | tf_op jit(solution)/shard_map/dot_general | solution.py:343
  47.6 1.7 fusion.39
  49.3 8.8 %multiply_convert_fusion = (bf16[128,3456]{1,0:T(8,128)(2,1)S(1)}, bf16[128,3456]{1,0:T(8,128)(2,1)S(1)}, bf16[128,3456]{1,0:T(8,128)(2,1)}) fusion(f32[128,3456]{1,0:T(8,128)S(1)} %fusion.39, f32[128,3456]{1,0:T(8,128)S(1)} %fusion.40, bf16[128,1536]{1,0:T(8,128)(2,1)S(1)} %copy-done.14, bf16[3456,1536]{1,0:T(8,128)(2,1)} %param.23), kind=kOutput, calls=%fused_computation.5 | convolution fusion | flops 1365590016 | bytes 17203200 | tf_op jit(solution)/shard_map/dot_general | solution.py:352
  58.2 8.2 %fusion.41 = f32[128,1536]{1,0:T(8,128)S(1)} fusion(bf16[128,3456]{1,0:T(8,128)(2,1)S(1)} %get-tuple-element.112.d_gate, bf16[1536,3456]{1,0:T(8,128)(2,1)} %param.21), kind=kOutput, calls=%fused_computation.101 | convolution fusion | flops 1358954496 | bytes 12288000 | tf_op jit(solution)/shard_map/dot_general | solution.py:359
  66.4 3.5 %fusion = bf16[128,1536]{1,0:T(8,128)(2,1)S(1)} fusion(f32[128,1536]{1,0:T(8,128)S(1)} %fusion.41, bf16[128,3456]{1,0:T(8,128)(2,1)S(1)} %get-tuple-element.111.d_lift, bf16[1536,3456]{1,0:T(8,128)(2,1)S(1)} %bitcast.99), kind=kOutput, calls=%fused_computation.2 | convolution fusion | flops 1359347712 | bytes 12681216 | tf_op jit(solution)/shard_map/dot_general | solution.py:360
  70.0 4.4 %all_to_all.37 = bf16[2,128,1536]{2,1,0:T(8,128)(2,1)S(1)} all-to-all(bf16[2,128,1536]{2,1,0:T(8,128)(2,1)S(1)} %broadcast_in_dim.101), channel_id=1, replica_groups=mesh['seq'=64,'ch'=2] {'ch'}, dimensions={0} | all-to-all | bytes 1572864 | tf_op jit(solution)/shard_map/all_to_all | solution.py:237
  74.3 1.0 convert_reduce_fusion.1
  75.4 2.3 copy.45
  77.7 1.7 multiply_reduce_fusion
  79.4 5.7 %convolution_convert_fusion = bf16[128,1536]{1,0:T(8,128)(2,1)S(1)} fusion(bf16[128,3456]{1,0:T(8,128)(2,1)S(1)} %copy-done.5, bf16[3456,1536]{1,0:T(8,128)(2,1)} %param.23), kind=kOutput, calls=%fused_computation.4 | convolution fusion | flops 1359151104 | bytes 11894784 | tf_op jit(solution)/shard_map/dot_general | solution.py:348
  85.2 4.4 %all_to_all.38 = bf16[2,128,1536]{2,1,0:T(8,128)(2,1)S(1)} all-to-all(bf16[2,128,1536]{2,1,0:T(8,128)(2,1)S(1)} %broadcast_in_dim.100), channel_id=1, replica_groups=mesh['seq'=64,'ch'=2] {'ch'}, dimensions={0} | all-to-all | bytes 1572864 | tf_op jit(solution)/shard_map/all_to_all | solution.py:237
  89.5 1.0 convert_reduce_fusion.2
  90.5 2.3 copy.43
  92.8 2.7 %convert_bitcast_fusion = (bf16[1,1536,128]{2,1,0:T(8,128)(2,1)}, f32[128,1536]{0,1:T(8,128)S(1)}, bf16[128,1536]{0,1:T(8,128)(2,1)}) fusion(f32[128]{0:T(128)S(1)} %broadcast_multiply_fusion.1, f32[128,1536]{0,1:T(8,128)S(1)} %get-tuple-element.108, f32[128,1536]{0,1:T(8,128)} %copy.45, f32[1536]{0:T(1024)S(1)} %copy-done.12, f32[128]{0:T(128)S(1)} %add_rsqrt_fusion, ...), kind=kLoop, calls=%fused_computation.68 | loop fusion | flops 1966080 | bytes 4332544 | tf_op jit(solution)/shard_map/stack | solution.py:410
  95.6 1.7 fusion.22
  98.2 0.9 broadcast_in_dim.106
  99.1 5.6 %all-to-all-start.4 = ((f32[64,1,2,768]{3,2,1,0:T(2,128)}), f32[64,1,2,768]{3,2,1,0:T(2,128)}, u32[]{:S(2)}, u32[]{:S(2)}) async-start(f32[64,1,2,768]{3,2,1,0:T(2,128)} %broadcast_in_dim.106), calls=%async_computation.4 | async-start | bytes 786432 | tf_op jit(solution)/shard_map/all_to_all | solution.py:237
  104.8 0.9 copy.51
  105.7 1.2 fusion.24
  106.9 0.7 copy-done.11
  107.7 1.0 fusion.59.n2t
  108.7 8.2 %all-to-all-done.4 = f32[64,1,2,768]{3,2,1,0:T(2,128)} async-done(((f32[64,1,2,768]{3,2,1,0:T(2,128)}), f32[64,1,2,768]{3,2,1,0:T(2,128)}, u32[]{:S(2)}, u32[]{:S(2)}) %all-to-all-start.4) | async-done | bytes 393248 | tf_op jit(solution)/shard_map/all_to_all | solution.py:237
  116.9 0.7 select_bitcast_fusion
  117.7 5.5 %fusion.1 = bf16[128,1536]{1,0:T(8,128)(2,1)S(1)} fusion(bf16[3,1536,768]{2,1,0:T(8,128)(2,1)} %param.17, bf16[1,128,768]{2,1,0:T(8,128)(2,1)S(1)} %get-tuple-element.115, bf16[1,128,768]{2,1,0:T(8,128)(2,1)} %bitcast.105, bf16[1,128,768]{2,1,0:T(8,128)(2,1)S(1)} %get-tuple-element.114), kind=kOutput, calls=%fused_computation.3 | convolution fusion | flops 906756096 | bytes 8060928 | tf_op jit(solution)/shard_map/kte,kde->td/dot_general | solution.py:395
  123.3 4.4 %all_to_all.39 = bf16[2,128,1536]{2,1,0:T(8,128)(2,1)S(1)} all-to-all(bf16[2,128,1536]{2,1,0:T(8,128)(2,1)S(1)} %broadcast_in_dim.109), channel_id=1, replica_groups=mesh['seq'=64,'ch'=2] {'ch'}, dimensions={0} | all-to-all | bytes 1572864 | tf_op jit(solution)/shard_map/all_to_all | solution.py:237
  128.6 1.5 broadcast_in_dim.110
  130.1 5.9 %all-to-all-start.6 = ((f32[64,1,3840]{2,1,0:T(1,128)}), f32[64,1,3840]{2,1,0:T(1,128)}, u32[]{:S(2)}, u32[]{:S(2)}) async-start(f32[64,1,3840]{2,1,0:T(1,128)} %broadcast_in_dim.110), calls=%async_computation.6 | async-start | bytes 1966080 | tf_op jit(solution)/shard_map/all_to_all | solution.py:237
  136.1 1.0 pad_maximum_fusion.1.mixed_r
  137.1 0.9 pad_maximum_fusion.n1t
  138.0 100.1 %weight_grads.1 = (f32[24,3456]{1,0:T(8,128)}, f32[24,3456]{1,0:T(8,128)}, f32[24,3456]{1,0:T(8,128)}, f32[3,24,768]{2,1,0:T(8,128)}, f32[24,768]{1,0:T(8,128)}) custom-call(bf16[1536,128]{1,0:T(8,128)(2,1)} %fusion.59.n2t, bf16[1536,128]{1,0:T(8,128)(2,1)} %bitcast.102, bf16[2,1536,128]{2,1,0:T(8,128)(2,1)} %pad_maximum_fusion.n1t, ...), custom_call_target="tpu_custom_call" | custom-call | tf_op jit(solution)/shard_map/weight_grads/pallas_call | solution.py:218
  238.2 1.5 fusion.12
  239.7 0.9 copy.52
  240.6 1.8 reduce_sum.149
  243.6 0.7 copy.64
  245.0 0.7 copy.66
  245.7 0.7 copy.67
  246.4 0.7 copy.68
  (110 shorter events, 7.2 us)
Async XLA Ops:
  2.1 16.7 %copy-start.24 = (s32[64]{0:T(128)S(1)}, s32[64]{0:T(128)}, u32[]{:S(2)}) copy-start(s32[64]{0:T(128)} %param.15) | copy-start | bytes 772
  2.1 21.2 %copy-start.25 = (s32[4]{0:T(128)S(1)}, s32[4]{0:T(128)}, u32[]{:S(2)}) copy-start(s32[4]{0:T(128)} %param.14) | copy-start | bytes 52
  2.1 21.4 %copy-start.23 = (f32[3,768]{1,0:T(4,128)S(1)}, f32[3,768]{1,0:T(4,128)}, u32[]{:S(2)}) copy-start(f32[3,768]{1,0:T(4,128)} %param.18) | copy-start | bytes 27652
  2.1 21.4 %copy-start.13 = (bf16[128,1536]{1,0:T(8,128)(2,1)S(1)}, bf16[128,1536]{1,0:T(8,128)(2,1)}, u32[]{:S(2)}) copy-start(bf16[128,1536]{1,0:T(8,128)(2,1)} %param.13) | copy-start | bytes 1179652
  7.3 21.6 %all-to-all-start = ((bf16[64,1,2,768]{3,2,1,0:T(2,128)(2,1)}), bf16[64,1,2,768]{3,2,1,0:T(2,128)(2,1)S(1)}, u32[]{:S(2)}, u32[]{:S(2)}) async-start(bf16[64,1,2,768]{3,2,1,0:T(2,128)(2,1)} %broadcast_in_dim.96), calls=%async_computation | async-start | bytes 393216 | tf_op jit(solution)/shard_map/all_to_all | solution.py:237
  23.8 69.0 %copy-start.8 = (bf16[128,1536]{0,1:T(8,128)(2,1)}, bf16[128,1536]{0,1:T(8,128)(2,1)S(1)}, u32[]{:S(2)}) copy-start(bf16[128,1536]{0,1:T(8,128)(2,1)S(1)} %copy.44) | copy-start | bytes 1179652
  28.9 1.8 copy-start
  38.8 2.7 %copy-start.12 = (f32[1536]{0:T(1024)S(1)}, f32[1536]{0:T(1024)}, u32[]{:S(2)}) copy-start(f32[1536]{0:T(1024)} %param.20) | copy-start | bytes 18436
  40.0 7.4 %slice-start.3 = ((s8[10616832]{0:T(1024)(128)(4,1)}), s8[4194304]{0:T(1024)(128)(4,1)S(1)}, s32[]{:S(2)}) async-start(s8[10616832]{0:T(1024)(128)(4,1)} %bitcast.100), calls=%async_computation.10 | async-start | bytes 8388608
  41.5 5.9 %slice-start.4 = ((s8[10616832]{0:T(1024)(128)(4,1)}), s8[4194304]{0:T(1024)(128)(4,1)S(1)}, s32[]{:S(2)}) async-start(s8[10616832]{0:T(1024)(128)(4,1)} %bitcast.100), calls=%async_computation.11 | async-start | bytes 8388608
  41.5 6.1 %slice-start.5 = ((s8[10616832]{0:T(1024)(128)(4,1)}), s8[2228224]{0:T(1024)(128)(4,1)S(1)}, s32[]{:S(2)}) async-start(s8[10616832]{0:T(1024)(128)(4,1)} %bitcast.100), calls=%async_computation.12 | async-start | bytes 4456448
  47.6 1.7 copy-start.14
  49.3 17.1 %slice-start = ((s8[10616832]{0:T(1024)(128)(4,1)}), s8[4194304]{0:T(1024)(128)(4,1)S(1)}, s32[]{:S(2)}) async-start(s8[10616832]{0:T(1024)(128)(4,1)} %bitcast.98), calls=%async_computation.7 | async-start | bytes 8388608
  49.3 17.1 %slice-start.1 = ((s8[10616832]{0:T(1024)(128)(4,1)}), s8[2228224]{0:T(1024)(128)(4,1)S(1)}, s32[]{:S(2)}) async-start(s8[10616832]{0:T(1024)(128)(4,1)} %bitcast.98), calls=%async_computation.8 | async-start | bytes 4456448
  58.2 8.2 %copy-start.7 = (bf16[128,3456]{1,0:T(8,128)(2,1)}, bf16[128,3456]{1,0:T(8,128)(2,1)S(1)}, u32[]{:S(2)}) copy-start(bf16[128,3456]{1,0:T(8,128)(2,1)S(1)} %get-tuple-element.112.d_gate) | copy-start | bytes 2654212
  58.2 8.2 %copy-start.6 = (bf16[128,3456]{1,0:T(8,128)(2,1)}, bf16[128,3456]{1,0:T(8,128)(2,1)S(1)}, u32[]{:S(2)}) copy-start(bf16[128,3456]{1,0:T(8,128)(2,1)S(1)} %get-tuple-element.111.d_lift) | copy-start | bytes 2654212
  58.2 8.2 %slice-start.2 = ((s8[10616832]{0:T(1024)(128)(4,1)}), s8[4194304]{0:T(1024)(128)(4,1)S(1)}, s32[]{:S(2)}) async-start(s8[10616832]{0:T(1024)(128)(4,1)} %bitcast.98), calls=%async_computation.9 | async-start | bytes 8388608
  77.7 1.7 copy-start.5
  92.8 2.7 %copy-start.1 = (bf16[768,1536]{1,0:T(8,128)(2,1)S(1)}, bf16[768,1536]{1,0:T(8,128)(2,1)}, u32[]{:S(2)}) copy-start(bf16[768,1536]{1,0:T(8,128)(2,1)} %param.19) | copy-start | bytes 7077892
  95.6 1.7 copy-start.2
  97.5 7.3 %copy-start.10 = (bf16[128,1536]{0,1:T(8,128)(2,1)S(1)}, bf16[128,1536]{0,1:T(8,128)(2,1)}, u32[]{:S(2)}) copy-start(bf16[128,1536]{0,1:T(8,128)(2,1)} %get-tuple-element.116) | copy-start | bytes 1179652
  99.1 17.8 %all-to-all-start.4 = ((f32[64,1,2,768]{3,2,1,0:T(2,128)}), f32[64,1,2,768]{3,2,1,0:T(2,128)}, u32[]{:S(2)}, u32[]{:S(2)}) async-start(f32[64,1,2,768]{3,2,1,0:T(2,128)} %broadcast_in_dim.106), calls=%async_computation.4 | async-start | bytes 786432 | tf_op jit(solution)/shard_map/all_to_all | solution.py:237
  106.9 0.7 copy-start.11
  123.2 4.8 %copy-start.21 = (f32[1536]{0:T(1024)S(1)}, f32[1536]{0:T(1024)}, u32[]{:S(2)}) copy-start(f32[1536]{0:T(1024)} %param.16) | copy-start | bytes 18436
  128.0 8.1 %copy-start.4 = (f32[128,1536]{0,1:T(8,128)}, f32[128,1536]{0,1:T(8,128)S(1)}, u32[]{:S(2)}) copy-start(f32[128,1536]{0,1:T(8,128)S(1)} %copy.46) | copy-start | bytes 2359300
  128.0 8.0 %copy-start.18 = (bf16[128,256]{1,0:T(8,128)(2,1)S(1)}, bf16[128,256]{1,0:T(8,128)(2,1)}, u32[]{:S(2)}) copy-start(bf16[128,256]{1,0:T(8,128)(2,1)} %get-tuple-element.121) | copy-start | bytes 196612
  128.0 8.0 %copy-start.19 = (bf16[128,256]{1,0:T(8,128)(2,1)S(1)}, bf16[128,256]{1,0:T(8,128)(2,1)}, u32[]{:S(2)}) copy-start(bf16[128,256]{1,0:T(8,128)(2,1)} %get-tuple-element.122) | copy-start | bytes 196612
  130.1 7.0 %copy-start.9 = (bf16[1,1536,128]{2,1,0:T(8,128)(2,1)S(1)}, bf16[1,1536,128]{2,1,0:T(8,128)(2,1)}, u32[]{:S(2)}) copy-start(bf16[1,1536,128]{2,1,0:T(8,128)(2,1)} %get-tuple-element.104) | copy-start | bytes 1179652
  130.1 110.5 %all-to-all-start.6 = ((f32[64,1,3840]{2,1,0:T(1,128)}), f32[64,1,3840]{2,1,0:T(1,128)}, u32[]{:S(2)}, u32[]{:S(2)}) async-start(f32[64,1,3840]{2,1,0:T(1,128)} %broadcast_in_dim.110), calls=%async_computation.6 | async-start | bytes 1966080 | tf_op jit(solution)/shard_map/all_to_all | solution.py:237
  138.0 100.1 %copy-start.3 = (f32[128,1536]{0,1:T(8,128)S(1)}, f32[128,1536]{0,1:T(8,128)}, u32[]{:S(2)}) copy-start(f32[128,1536]{0,1:T(8,128)} %copy-done.2) | copy-start | bytes 2359300
  238.1 5.5 %copy-start.20 = (f32[3,24,768]{2,1,0:T(8,128)S(1)}, f32[3,24,768]{2,1,0:T(8,128)}, u32[]{:S(2)}) copy-start(f32[3,24,768]{2,1,0:T(8,128)} %get-tuple-element.147) | copy-start | bytes 663556
  238.2 6.2 %copy-start.22 = (f32[24,768]{1,0:T(8,128)S(1)}, f32[24,768]{1,0:T(8,128)}, u32[]{:S(2)}) copy-start(f32[24,768]{1,0:T(8,128)} %get-tuple-element.16) | copy-start | bytes 221188
  238.2 6.8 %copy-start.17 = (f32[24,3456]{1,0:T(8,128)S(1)}, f32[24,3456]{1,0:T(8,128)}, u32[]{:S(2)}) copy-start(f32[24,3456]{1,0:T(8,128)} %get-tuple-element.151) | copy-start | bytes 995332
  238.2 7.5 %copy-start.16 = (f32[24,3456]{1,0:T(8,128)S(1)}, f32[24,3456]{1,0:T(8,128)}, u32[]{:S(2)}) copy-start(f32[24,3456]{1,0:T(8,128)} %get-tuple-element.152) | copy-start | bytes 995332
  239.7 6.7 %copy-start.15 = (f32[24,3456]{1,0:T(8,128)S(1)}, f32[24,3456]{1,0:T(8,128)}, u32[]{:S(2)}) copy-start(f32[24,3456]{1,0:T(8,128)} %get-tuple-element.19) | copy-start | bytes 995332

commit v2 on v0

v2 whole, which is shorter than its diff:
```python
import jax
import jax.numpy as jnp
from jax import lax
from jax.experimental import pallas as pl
from jax.experimental.pallas import tpu as pltpu
from jax.sharding import PartitionSpec as P

MESH = pl.DeviceIdType.MESH
F32, BF16 = jnp.float32, jnp.bfloat16
BLK, D, HALF, FF = 128, 1536, 768, 3456
WS, WM, TILE = 896, 256, 384
TILES = FF // TILE
EPS = 1e-05
ROUTES = ((2, 1, 0), (0, 2, 1), (1, 0, 2))
READY = ((0, 3), (3, 5), (5, 7), (7, 9))


def dot_nt(a, b):
    return lax.dot_general(a, b, (((1,), (1,)), ((), ())), preferred_element_type=F32)


def dot_nn(a, b):
    return jnp.dot(a, b, preferred_element_type=F32)


def slice_start(i):
    return pl.multiple_of(jnp.minimum(i * WS, FF - WS), 128)


def layer_kernel(
    seq_lengths, block_slots, mixgain, glugain, taps,
    tokens, cotangent, inproj, outproj, gate_w, lift_w, down_w,
    o_layer, o_input, o_gains, o_gate, o_lift, o_down, o_in, o_out,
    tok_v, cot_v, n1_v, b_v, c_v, x_v, v_v, u_v, y_v, h2_v, n2_v, glu_v, dn2_v,
    col, down_ring, out_v, act, mixed_r, s_src, m_src,
    xh_send, xh_recv, tails, heads, gain_land,
    s_left, s_right, s_bsend, s_bland, s_cland, s_dsend, s_dland, m_left, m_right, m_dsend, m_dland,
    load_sem, col_sem, down_sem, x_send, x_recv, halo_send, halo_recv, gain_send, gain_recv,
    l_send, l_recv, f_send, f_recv, r_send, r_recv,
    b_send, b_recv, c_send, c_recv, d_send, d_recv, own_sem,
):
    seq, core = lax.axis_index("seq"), lax.axis_index("ch")
    place = (seq // 16, (seq // 4) % 4, seq % 4)

    def peer(axis, step):
        at = [(place[i] + step) % 4 if i == axis else place[i] for i in range(3)]
        return at[0] * 16 + at[1] * 4 + at[2]

    def local(src, dst, sem):
        return pltpu.make_async_copy(src, dst, sem)

    def link(src, dst, send, recv, axis, step):
        return pltpu.make_async_remote_copy(
            src_ref=src, dst_ref=dst, send_sem=send, recv_sem=recv,
            device_id=(peer(axis, step), core), device_id_type=MESH)

    def cross(src, dst, send, recv):
        return pltpu.make_async_remote_copy(
            src_ref=src, dst_ref=dst, send_sem=send, recv_sem=recv,
            device_id=(seq, 1 - core), device_id_type=MESH)

    def started(copies):
        for c in copies:
            c.start()
        return copies

    def waited(copies):
        for c in copies:
            c.wait()

    tok_load = local(tokens, tok_v, load_sem.at[0])
    cot_load = local(cotangent, cot_v, load_sem.at[1])
    out_load = local(outproj, out_v, load_sem.at[2])
    in_loads = [local(inproj.at[k], col.at[k], col_sem.at[k, 0]) for k in range(3)]
    tok_load.start()
    in_loads[0].start()
    in_loads[2].start()
    in_loads[1].start()

    def pair_loads(j):
        slot = (j + 3) % 4
        lanes = pl.ds(pl.multiple_of(j * TILE, 128), TILE)
        return [
            local(gate_w.at[:, lanes], col.at[slot, :, pl.ds(0, TILE)], col_sem.at[slot, 0]),
            local(lift_w.at[:, lanes], col.at[slot, :, pl.ds(TILE, TILE)], col_sem.at[slot, 1]),
        ]

    def down_load(j):
        slot = j % 3
        return local(down_w.at[pl.ds(pl.multiple_of(j * TILE, 128), TILE), :], down_ring.at[slot], down_sem.at[slot])

    barrier = pltpu.get_barrier_semaphore()
    for axis in range(3):
        for step in range(1, 4):
            pl.semaphore_signal(barrier, inc=1, device_id=(peer(axis, step), core), device_id_type=MESH)
    pl.semaphore_signal(barrier, inc=1, device_id=(seq, 1 - core), device_id_type=MESH)

    block = jnp.int32(0)
    for i in range(64):
        block = jnp.where(block_slots[i] == seq, i, block)
    before = block_slots[jnp.maximum(block - 1, 0)]
    after = block_slots[jnp.minimum(block + 1, 63)]
    has_after = (block < 63).astype(F32)
    rows = lax.broadcasted_iota(jnp.int32, (BLK, 1), 0)
    positions = block * BLK + rows
    start = jnp.zeros((BLK, 1), jnp.int32)
    offset = jnp.int32(0)
    for i in range(4):
        start = jnp.where(offset <= positions, offset, start)
        offset = offset + seq_lengths[i]
    mask1 = (positions - 1 >= start).astype(F32)
    mask2 = (positions - 2 >= start).astype(F32)

    def halo_links(land, job, phase):
        out = []
        for k in range(3):
            where = [pl.ds(0, 4) if axis in ROUTES[k][:phase] else pl.ds(place[axis], 1) for axis in range(3)]
            view = land.at[k, where[0], where[1], where[2]]
            axis = ROUTES[k][phase]
            for step in range(1, 4):
                out.append(link(view, view, halo_send.at[job, phase, k, step - 1], halo_recv.at[job, phase, k, step - 1], axis, step))
        return out

    def halo_rows(land, slot):
        at = (slot // 16, (slot // 4) % 4, slot % 4)
        return jnp.concatenate([land[k, at[0], at[1], at[2]] for k in range(3)], axis=1)

    def put_halo(land, two):
        for k in range(3):
            land[k, place[0], place[1], place[2]] = two[:, 256 * k:256 * k + 256]

    tok_load.wait()
    resid = tok_v[...].astype(F32)
    scale_a = lax.rsqrt(jnp.mean(resid * resid, axis=1, keepdims=True) + EPS)
    n1 = (resid * scale_a * mixgain[...]).astype(BF16)
    n1_v[...] = n1
    in_loads[0].wait()
    b_v[...] = dot_nn(n1_v[...], col[0])
    in_loads[2].wait()
    x_v[...] = dot_nn(n1_v[...], col[2])
    v_v[...] = (b_v[...] * x_v[...]).astype(BF16).astype(F32)
    put_halo(tails, v_v[BLK - 2:BLK, :])
    pl.semaphore_wait(barrier, 10)
    halo = started(halo_links(tails, 0, 0))
    started([cot_load, out_load])
    started(pair_loads(0))
    for j in range(3):
        down_load(j).start()
    in_loads[1].wait()
    c_v[...] = dot_nn(n1_v[...], col[1])
    for j in range(1, 4):
        started(pair_loads(j))
    waited(halo)
    halo = started(halo_links(tails, 0, 1))
    m_src[0] = n1_v[...].T
    cot_load.wait()
    s_src[1] = cot_v[...].T
    waited(halo)
    halo = started(halo_links(tails, 0, 2))

    half = pl.ds(pl.multiple_of(core * HALF, HALF), HALF)

    def left_link(job, k, src, step):
        left = (s_left, m_left)[job]
        return link(src.at[half, :], left.at[k, half, pl.ds(128 * step, 128)],
                    l_send.at[job, k, step - 1], l_recv.at[job, k, step - 1], k, step)

    def send_left_s(k):
        src = s_src.at[1 if k == 2 else 0]
        local(src, s_left.at[k, :, pl.ds(0, 128)], own_sem.at[0, k, 0]).start()
        for step in range(1, 4):
            left_link(0, k, src, step).start()

    def send_left_m(k, which):
        for step in range(1, 4):
            @pl.when(((place[k] + step) % 4 == 3) == (which == 1))
            def _():
                left_link(1, k, m_src.at[which], step).start()

    send_left_s(2)
    for k in range(3):
        send_left_m(k, 0)

    waited(halo)
    carried = halo_rows(tails, before)
    row_is0, row_is1 = rows == 0, rows == 1
    tap0, tap1, tap2 = taps[0:1, :], taps[1:2, :], taps[2:3, :]

    def shifted():
        v = v_v[...]
        one = jnp.where(row_is0, carried[1:2], pltpu.roll(v, 1, 0)) * mask1
        two = jnp.where(row_is0, carried[0:1], jnp.where(row_is1, carried[1:2], pltpu.roll(v, 2, 0))) * mask2
        return v, one, two

    v0, v1, v2 = shifted()
    u_v[...] = tap0 * v0 + tap1 * v1 + tap2 * v2
    y_v[...] = (c_v[...] * u_v[...]).astype(BF16)
    out_load.wait()
    dn2_v[...] = dot_nn(y_v[...], out_v[...])
    swap = cross(dn2_v, h2_v, x_send.at[0], x_recv.at[0])
    swap.start()
    swap.wait()
    h2_v[...] = tok_v[...].astype(F32) + (dn2_v[...] + h2_v[...])
    h2 = h2_v[...]
    scale_b = lax.rsqrt(jnp.mean(h2 * h2, axis=1, keepdims=True) + EPS)
    n2_v[...] = (h2 * scale_b * glugain[...]).astype(BF16)
    s_src[0] = n2_v[...].T
    send_left_s(0)
    send_left_s(1)

    glu_v[...] = jnp.zeros_like(glu_v)
    dn2_v[...] = jnp.zeros_like(dn2_v)

    def tile(j, carry):
        slot = (j + 3) % 4
        lanes = pl.ds(pl.multiple_of(j * TILE, 128), TILE)
        waited(pair_loads(j))
        both = dot_nn(n2_v[...], col[slot])
        gate_pre, lift_pre = both[:, :TILE], both[:, TILE:]
        down_load(j).wait()
        hidden_grad = dot_nt(cot_v[...], down_ring[j % 3])
        sig = jax.nn.sigmoid(gate_pre)
        silu = gate_pre * sig
        hidden = (silu * lift_pre).astype(BF16)
        d_lift = (hidden_grad * silu).astype(BF16)
        d_gate = (hidden_grad * lift_pre * sig * (1.0 + gate_pre * (1.0 - sig))).astype(BF16)
        act[0, :, lanes] = d_gate
        act[1, :, lanes] = d_lift
        act[2, :, lanes] = hidden
        glu_v[...] += dot_nn(hidden, down_ring[j % 3])
        dn2_v[...] += dot_nt(jnp.concatenate([d_gate, d_lift], axis=1), col[slot])

        @pl.when(j + 4 < TILES)
        def _():
            started(pair_loads(j + 4))

        @pl.when(j + 3 < TILES)
        def _():
            down_load(j + 3).start()

        return carry

    def right_link(job, k, src, step):
        right = (s_right, m_right)[job]
        return link(src, right.at[k, pl.ds(pl.multiple_of(128 * step, 128), 128), :],
                    r_send.at[job, k, step - 1], r_recv.at[job, k, step - 1], k, step)

    def s_piece(k, i):
        return act.at[k, :, pl.ds(slice_start(i), WS)]

    for i, (first, end) in enumerate(READY):
        lax.fori_loop(first, end, tile, 0)
        for k in range(3):
            step = (i - place[k] + 4) % 4

            @pl.when(step != 0)
            def _():
                right_link(0, k, s_piece(k, i), step).start()

    own = {}
    for k in range(3):
        own[0, k] = local(s_piece(k, place[k]), s_right.at[k, pl.ds(0, 128), :], own_sem.at[0, k, 1])
        own[0, k].start()
    started(in_loads)

    xh_send[0] = dn2_v[...].astype(BF16)
    swap_dn2 = cross(xh_send.at[0], xh_recv.at[0], x_send.at[1], x_recv.at[1])
    swap_dn2.start()
    xh_send[1] = glu_v[...].astype(BF16)
    swap_glu = cross(xh_send.at[1], xh_recv.at[1], x_send.at[2], x_recv.at[2])
    swap_glu.start()
    swap_dn2.wait()
    h2 = h2_v[...]
    z2 = h2 * scale_b
    dn2 = xh_send[0].astype(F32) + xh_recv[0].astype(F32)
    glu_term = jnp.sum(dn2 * z2, axis=0, keepdims=True)
    scaled = dn2 * glugain[...]
    glu_v[...] = cot_v[...].astype(F32) + scale_b * (scaled - z2 * jnp.mean(scaled * z2, axis=1, keepdims=True))
    n2_v[...] = glu_v[...].astype(BF16)
    m_src[1] = n2_v[...].T
    for k in range(3):
        send_left_m(k, 1)
        local(m_src.at[jnp.where(place[k] == 3, 1, 0)], m_left.at[k, :, pl.ds(0, 128)], own_sem.at[1, k, 0]).start()
    dy = dot_nt(n2_v[...], out_v[...])
    d_c = (dy * u_v[...]).astype(BF16)
    du = dy * c_v[...]
    v0, v1, v2 = shifted()
    tap_terms = [jnp.sum(du * v, axis=0, keepdims=True) for v in (v0, v1, v2)]
    w1, w2 = tap1 * (du * mask1), tap2 * (du * mask2)
    put_halo(heads, jnp.concatenate([w2[0:1], w1[0:1] + w2[1:2]], axis=0))
    halo = started(halo_links(heads, 1, 0))
    dv = tap0 * du + jnp.where(rows < 127, pltpu.roll(w1, 127, 0), 0.0) + jnp.where(rows < 126, pltpu.roll(w2, 126, 0), 0.0)
    u_v[...] = dv
    y_out = y_v[...]
    for k in range(3):
        mixed_r[k, :, HALF:] = y_out[:, 256 * k:256 * k + 256]
    mixed_r[1, :, :HALF] = d_c
    swap_glu.wait()
    o_layer[...] = (h2_v[...] + (xh_send[1].astype(F32) + xh_recv[1].astype(F32))).astype(BF16)

    lefts, rights, dsends, dlands = (s_left, m_left), (s_right, m_right), (s_dsend, m_dsend), (s_dland, m_dland)

    def b_out(job, k, j, row=0, count=384):
        if job == 0:
            return s_bsend.at[k, j, pl.ds(row, count), :]
        return col.at[3, pl.ds(pl.multiple_of(384 * j + row, 96), count), pl.ds(WM * k, WM)]

    def b_in(job, k, i, row=0, count=384):
        if job == 0:
            return s_bland.at[k, i, pl.ds(row, count), :]
        return down_ring.at[i, pl.ds(row, count), pl.ds(WM * k, WM)]

    def c_out(job, k, j, row=0, count=96):
        return rights[job].at[k, pl.ds(pl.multiple_of(96 * j + row, 48), count), :]

    def c_in(job, k, i):
        if job == 0:
            return s_cland.at[k, i]
        return down_ring.at[i, pl.ds(0, 96), pl.ds(HALF + WM * k, WM)]

    def forward_left(job, k):
        left = lefts[job]
        out = []
        for step in range(1, 4):
            left_link(job, k, m_src.at[0], step).wait()
            view = left.at[k, half, pl.ds(128 * step, 128)]
            out.append(cross(view, view, f_send.at[job, k, step - 1], f_recv.at[job, k, step - 1]))
            out[-1].start()
        return out

    def finish_a(job, k, forwarded):
        local(m_src.at[0], lefts[job].at[k, :, pl.ds(0, 128)], own_sem.at[job, k, 0]).wait()
        own[job, k].wait()
        for step in range(1, 4):
            src = s_piece(k, 0) if job == 0 else mixed_r.at[k, :, pl.ds(0, WM)]
            right_link(job, k, src, step).wait()
        waited(forwarded)

    def start_b(job, k):
        left, right = lefts[job], rights[job]

        def slab(x, carry):
            acc = dot_nn(left[k, pl.ds(pl.multiple_of(x * 384, 384), 384), :], right[k])
            for j in range(4):
                if k == 0:
                    b_out(job, k, j, 96 * x, 96)[...] = acc[96 * j:96 * j + 96].astype(BF16)
                elif k == 1:
                    parts = [acc[96 * y + 24 * j:96 * y + 24 * j + 24] for y in range(4)]
                    b_out(job, k, j, 96 * x, 96)[...] = jnp.concatenate(parts, axis=0).astype(BF16)
                else:
                    b_out(job, k, x, 96 * j, 96)[...] = acc[96 * j:96 * j + 96].astype(BF16)
            return carry

        lax.fori_loop(0, 4, slab, 0)
        axis = (k + 1) % 3
        return started([
            link(b_out(job, k, (place[axis] + step) % 4), b_in(job, k, step - 1),
                 b_send.at[job, k, step - 1], b_recv.at[job, k, step - 1], axis, step)
            for step in range(1, 4)])

    def start_c(job, k, copies):
        waited(copies)
        me = place[(k + 1) % 3]

        def summed(q):
            total = b_out(job, k, me, 96 * q, 96)[...].astype(F32)
            for i in range(3):
                total = total + b_in(job, k, i, 96 * q, 96)[...].astype(F32)
            return total

        if k == 0:
            for p in range(2):
                a, b = summed(2 * p), summed(2 * p + 1)
                for j in range(4):
                    both = jnp.concatenate([a[24 * j:24 * j + 24], b[24 * j:24 * j + 24]], axis=0)
                    c_out(job, k, j, 48 * p, 48)[...] = both.astype(BF16)
        else:
            for q in range(4):
                c_out(job, k, q)[...] = summed(q).astype(BF16)
        axis = (k + 2) % 3
        return started([
            link(c_out(job, k, (place[axis] + step) % 4), c_in(job, k, step - 1),
                 c_send.at[job, k, step - 1], c_recv.at[job, k, step - 1], axis, step)
            for step in range(1, 4)])

    def start_d(job, k, copies):
        dsend, dland = dsends[job], dlands[job]
        waited(copies)
        total = c_out(job, k, place[(k + 2) % 3])[...].astype(F32)
        for i in range(3):
            total = total + c_in(job, k, i)[...].astype(F32)
        pad = jnp.zeros((8, total.shape[1]), F32)
        for j in range(4):
            dsend[k, j] = jnp.concatenate([total[24 * j:24 * j + 24], pad], axis=0).astype(BF16)
        dland[k, 0] = dsend[k, place[k]]
        return started([
            link(dsend.at[k, (place[k] + step) % 4], dland.at[k, step],
                 d_send.at[job, k, step - 1], d_recv.at[job, k, step - 1], k, step)
            for step in range(1, 4)])

    def finish(job, k, copies):
        dland = dlands[job]
        waited(copies)
        for i in range(4):
            piece = dland[k, (place[k] - i + 4) % 4].astype(F32)[:24]
            if job == 0:
                out = (o_gate, o_lift, o_down)[k]
                if i < 3:
                    out[:, WS * i:WS * i + WS] = piece
                else:
                    out[:, WS * 3:FF] = piece[:, 4 * WS - FF:]
            elif i < 3:
                o_in[k, :, WM * i:WM * i + WM] = piece
            else:
                o_out[:, WM * k:WM * k + WM] = piece

    def gain_links(axis):
        view = gain_land.at[axis, place[axis]]
        return [link(view, view, gain_send.at[axis, step - 1], gain_recv.at[axis, step - 1], axis, step) for step in range(1, 4)]

    def gain_sum(axis):
        return (gain_land[axis, 0] + gain_land[axis, 1]) + (gain_land[axis, 2] + gain_land[axis, 3])

    b, c, d = {}, {}, {}
    fwd = [forward_left(0, k) for k in range(3)]
    waited(halo)
    halo = started(halo_links(heads, 1, 1))
    finish_a(0, 0, fwd[0])
    b[0, 0] = start_b(0, 0)
    waited(halo)
    halo = started(halo_links(heads, 1, 2))
    finish_a(0, 1, fwd[1])
    b[0, 1] = start_b(0, 1)
    finish_a(0, 2, fwd[2])
    b[0, 2] = start_b(0, 2)

    waited(halo)
    incoming = halo_rows(heads, after) * has_after
    dv = u_v[...] + jnp.where(rows == 126, incoming[0:1], jnp.where(rows == 127, incoming[1:2], 0.0))
    mixed_r[0, :, :HALF] = (dv * x_v[...]).astype(BF16)
    mixed_r[2, :, :HALF] = (dv * b_v[...]).astype(BF16)

    def m_piece(k, i):
        return mixed_r.at[k, :, pl.ds(pl.multiple_of(i * WM, WM), WM)]

    for k in range(3):
        for step in range(1, 4):
            right_link(1, k, m_piece(k, (place[k] + step) % 4), step).start()
        own[1, k] = local(m_piece(k, place[k]), m_right.at[k, pl.ds(0, 128), :], own_sem.at[1, k, 1])
        own[1, k].start()
    waited(in_loads)
    for k in range(3):
        part = dot_nt(mixed_r[k, :, :HALF], col[k])
        if k == 0:
            dn2_v[...] = part
        else:
            dn2_v[...] += part
    xh_send[2] = dn2_v[...].astype(BF16)
    swap = cross(xh_send.at[2], xh_recv.at[2], x_send.at[3], x_recv.at[3])
    swap.start()
    fwd = [forward_left(1, k) for k in range(3)]
    swap.wait()
    dn1 = xh_send[2].astype(F32) + xh_recv[2].astype(F32)
    z1 = tok_v[...].astype(F32) * scale_a
    mix_term = jnp.sum(dn1 * z1, axis=0, keepdims=True)
    scaled = dn1 * mixgain[...]
    o_input[...] = (glu_v[...] + scale_a * (scaled - z1 * jnp.mean(scaled * z1, axis=1, keepdims=True))).astype(BF16)

    def my_half(row):
        return jnp.where(core == 0, row[:, :HALF], row[:, HALF:])

    gain_land[0, place[0]] = jnp.concatenate(
        [my_half(mix_term), my_half(glu_term), *tap_terms, jnp.zeros((3, HALF), F32)], axis=0)
    gains = started(gain_links(0))
    for k in range(3):
        finish_a(1, k, fwd[k])
        b[1, k] = start_b(1, k)
    waited(gains)
    gain_land[1, place[1]] = gain_sum(0)
    gains = started(gain_links(1))
    for k in range(3):
        c[0, k] = start_c(0, k, b[0, k])
    waited(gains)
    gain_land[2, place[2]] = gain_sum(1)
    gains = started(gain_links(2))
    for k in range(3):
        c[1, k] = start_c(1, k, b[1, k])
    waited(gains)
    o_gains[...] = gain_sum(2)
    for job in range(2):
        for k in range(3):
            d[job, k] = start_d(job, k, c[job, k])
    for job in range(2):
        for k in range(3):
            finish(job, k, d[job, k])


def run_layer(seq_lengths, block_slots, mixgain, glugain, taps, tokens, cotangent, inproj, outproj, gate_w, lift_w, down_w):
    vm = pl.BlockSpec(memory_space=pltpu.VMEM)
    sm = pl.BlockSpec(memory_space=pltpu.SMEM)
    hbm = pl.BlockSpec(memory_space=pl.ANY)
    dma = pltpu.SemaphoreType.DMA
    shape = jax.ShapeDtypeStruct
    full16, full32, half32 = pltpu.VMEM((BLK, D), BF16), pltpu.VMEM((BLK, D), F32), pltpu.VMEM((BLK, HALF), F32)
    return pl.pallas_call(
        layer_kernel,
        out_shape=[shape((BLK, D), BF16), shape((BLK, D), BF16), shape((8, HALF), F32)]
        + [shape(s, F32) for s in ((24, FF), (24, FF), (24, FF), (3, 24, HALF), (24, HALF))],
        in_specs=[sm, sm, vm, vm, vm] + [hbm] * 7,
        out_specs=[vm] * 8,
        scratch_shapes=[
            full16, full16, full16,
            half32, half32, half32, half32, half32, pltpu.VMEM((BLK, HALF), BF16),
            full32, full16, full32, full32,
            pltpu.VMEM((4, D, HALF), BF16), pltpu.VMEM((3, TILE, D), BF16), pltpu.VMEM((HALF, D), BF16),
            pltpu.VMEM((3, BLK, FF), BF16), pltpu.VMEM((3, BLK, 4 * WM), BF16),
            pltpu.VMEM((2, D, BLK), BF16), pltpu.VMEM((2, D, BLK), BF16),
            pltpu.VMEM((3, BLK, D), BF16), pltpu.VMEM((3, BLK, D), BF16),
            pltpu.VMEM((3, 4, 4, 4, 2, 256), F32), pltpu.VMEM((3, 4, 4, 4, 2, 256), F32),
            pltpu.VMEM((3, 4, 8, HALF), F32),
            pltpu.VMEM((3, D, 512), BF16), pltpu.VMEM((3, 512, WS), BF16), pltpu.VMEM((3, 4, 384, WS), BF16),
            pltpu.VMEM((3, 3, 384, WS), BF16), pltpu.VMEM((3, 3, 96, WS), BF16),
            pltpu.VMEM((3, 4, 32, WS), BF16), pltpu.VMEM((3, 4, 32, WS), BF16),
            pltpu.VMEM((3, D, 512), BF16), pltpu.VMEM((3, 512, WM), BF16),
            pltpu.VMEM((3, 4, 32, WM), BF16), pltpu.VMEM((3, 4, 32, WM), BF16),
        ]
        + [dma((3,)), dma((4, 2)), dma((3,)), dma((4,)), dma((4,)),
           dma((2, 3, 3, 3)), dma((2, 3, 3, 3)), dma((3, 3)), dma((3, 3))]
        + [dma((2, 3, 3))] * 12 + [dma((2, 3, 2))],
        compiler_params=pltpu.CompilerParams(collective_id=1, has_side_effects=True, vmem_limit_bytes=LIMIT),
        name="layer",
    )(seq_lengths, block_slots, mixgain, glugain, taps, tokens, cotangent, inproj, outproj, gate_w, lift_w, down_w)


LIMIT = 64 * 1024 * 1024 - 256 * 1024


def on_device(
    tokens, cotangent, seq_lengths, block_slots, mixgain, inproj, conv_taps, outproj, glugain, gate_weight, lift_weight, down_weight
):
    layer_out, input_grad, gains, gate_grad, lift_grad, down_rows, inproj_grad, out_rows = run_layer(
        seq_lengths, block_slots, mixgain[None, :], glugain[None, :], conv_taps,
        tokens, cotangent, inproj, outproj, gate_weight, lift_weight, down_weight,
    )
    return (
        layer_out, input_grad, gains[0], inproj_grad, gains[2:5], out_rows.T, gains[1], gate_grad, lift_grad, down_rows.T,
    )


def solution(mesh):
    in_specs = (
        P("seq", None), P("seq", None), P(), P(), P(), P(None, None, "ch"), P(None, "ch"), P("ch", None),
        P(), P(None, "ch"), P(None, "ch"), P("ch", None),
    )
    out_specs = (
        P("seq", None), P("seq", None), P("ch"), P(None, "seq", "ch"), P(None, "ch"), P("ch", "seq"),
        P("ch"), P("seq", "ch"), P("seq", "ch"), P("ch", "seq"),
    )
    return jax.shard_map(on_device, mesh=mesh, in_specs=in_specs, out_specs=out_specs, check_vma=False)
```

time: 882 us -> 178 us (0.20)
  waiting for transfers between devices: 664 us -> 0 us
  Pallas kernels: 0 us -> 160 us
  matrix products: 89.6 us -> 0 us
  local copies, waits for them, and re-layouts: 47.5 us -> 17.2 us
  starting transfers between devices: 26.6 us -> 0 us
  other arithmetic: 19.8 us -> 0 us
  between operations: 18.6 us -> 0.66 us
  blocking collectives: 15.5 us -> 0 us
    unnamed x2 -> x0, waiting for transfers between devices: 623 us -> none
    pallas_call x0 -> x1, Pallas kernels: none -> 160 us  [run_layer(): pl.pallas_call(layer_kernel, out_shape=[shape((BLK, D), BF16), shape((BLK...]
    dot_general x15 -> x0, matrix products: 89.6 us -> none  [the longest x4 31.3 us: outer_all(): lax.dot_general(left, right, (((0,), (0,)), ((), ())), preferred_element_...]
    all_to_all x4 -> x0, waiting for transfers between devices: 41 us -> none  [from_everyone(): return lax.all_to_all(copies, axis, split_axis=0, concat_axis=0, tiled=True)]
    all_to_all x4 -> x0, starting transfers between devices: 26.5 us -> none  [from_everyone(): return lax.all_to_all(copies, axis, split_axis=0, concat_axis=0, tiled=True)]
    reshape x3 -> x0, local copies, waits for them, and re-layouts: 15.9 us -> none  [the longest x1 15.2 us: on_device(): proj_term.reshape(width, 3 * channels)]
    all_to_all x3 -> x0, blocking collectives: 15.5 us -> none  [from_everyone(): return lax.all_to_all(copies, axis, split_axis=0, concat_axis=0, tiled=True)]
    reduce_sum x10 -> x0, other arithmetic: 10.7 us -> none  [the longest x2 3.37 us: over_copies(): return jnp.sum(everything, axis=0)]
  transfers between devices with their start and end apart: 5 -> 0, of which waited for: 4 -> 0; matrix products, arithmetic and copies ran while one was open for 2% -> 0% of each run, Pallas kernels for 0% -> 0%
where the time goes in v2:
time: 178 us
  Pallas kernels  160 us (90%)
  local copies, waits for them, and re-layouts  17.2 us (10%)
    pallas_call x1, Pallas kernels, run_layer(): pl.pallas_call(layer_kernel, out_shape=[shape((BLK, D), BF16), shape((BLK...  160 us
    unnamed x7, local copies, waits for them, and re-layouts  11.8 us

profile of v2, /device:TPU:0, one launch (start us, length us, event | category | flops | bytes accessed | tf_op | source)
XLA Modules:
  0.0 177.8 jit_solution(6277566230965214004)
XLA Ops:
  0.6 1.3 broadcast_in_dim.6.mixgain
  1.9 1.3 broadcast_in_dim.7.glugain
  3.2 159.9 %layer.1 = (bf16[128,1536]{1,0:T(8,128)(2,1)}, bf16[128,1536]{1,0:T(8,128)(2,1)}, f32[8,768]{1,0:T(8,128)}, f32[24,3456]{1,0:T(8,128)}, f32[24,3456]{1,0:T(8,128...) custom-call(s32[4]{0:T(128)} %seq_lengths.1, s32[64]{0:T(128)} %block_slots.1, ...), custom_call_target="tpu_custom_call" | custom-call | tf_op jit(solution)/shard_map/layer/pallas_call | solution.py:505
  163.2 1.4 slice_reduce_fusion
  164.6 1.3 slice.10
  165.9 1.8 copy.29
  167.7 1.8 copy.30
  169.5 1.6 copy.31
  171.1 1.5 copy.32
  172.6 1.7 copy.33
  174.4 1.7 copy.34
  176.1 1.7 copy.35

commit v3 on v2

v3 whole, which is shorter than its diff:
```python
import jax
import jax.numpy as jnp
from jax import lax
from jax.experimental import pallas as pl
from jax.experimental.pallas import tpu as pltpu
from jax.sharding import PartitionSpec as P

MESH = pl.DeviceIdType.MESH
F32, BF16 = jnp.float32, jnp.bfloat16
BLK, D, HALF, FF = 128, 1536, 768, 3456
WS, WM = 896, 256
STEPS, SPAN = 7, 512
EPS = 1e-05
LIMIT = 64 * 1024 * 1024 - 256 * 1024
ROUTES = ((2, 1, 0), (0, 2, 1), (1, 0, 2))
GROUPS = ((0, 256), (256, 256), (512, 256), (768, 128))


def dot_nt(a, b):
    return lax.dot_general(a, b, (((1,), (1,)), ((), ())), preferred_element_type=F32)


def dot_nn(a, b):
    return jnp.dot(a, b, preferred_element_type=F32)


def block_of(i, s):
    return min(7 * i, 20) + s


def layer_kernel(
    seq_lengths, block_slots, mixgain_1d, glugain_1d, taps,
    tokens, cotangent, inproj, outproj, gate_w, lift_w, down_w,
    o_layer, o_input, o_gains, o_gate, o_lift, o_down, o_in, o_out,
    mixgain, glugain, tok_v, cot_v, n_v, b_v, c_v, x_v, v_v, u_v, y_v, h2_v, glu_v, dn2_v,
    col, down_ring, out_v, act, mixed_r, s_src, m_src, xh_send, xh_recv, tails, heads, gain_land,
    s_left, s_right, s_bsend, s_bland, s_cland, s_dsend, s_dland, m_left, m_right, m_dsend, m_dland,
    load_sem, col_sem, down_sem, store_sem, x_send, x_recv, halo_send, halo_recv, gain_send, gain_recv,
    l_send, l_recv, f_send, f_recv, r_send, r_recv,
    b_send, b_recv, c_send, c_recv, d_send, d_recv, own_left, own_right,
):
    seq, core = lax.axis_index("seq"), lax.axis_index("ch")
    place = (seq // 16, (seq // 4) % 4, seq % 4)

    def peer(axis, step):
        at = [(place[i] + step) % 4 if i == axis else place[i] for i in range(3)]
        return at[0] * 16 + at[1] * 4 + at[2]

    def local(src, dst, sem):
        return pltpu.make_async_copy(src, dst, sem)

    def link(src, dst, send, recv, axis, step):
        return pltpu.make_async_remote_copy(
            src_ref=src, dst_ref=dst, send_sem=send, recv_sem=recv,
            device_id=(peer(axis, step), core), device_id_type=MESH)

    def cross(src, dst, send, recv):
        return pltpu.make_async_remote_copy(
            src_ref=src, dst_ref=dst, send_sem=send, recv_sem=recv,
            device_id=(seq, 1 - core), device_id_type=MESH)

    def started(copies):
        for c in copies:
            c.start()
        return copies

    def waited(copies):
        for c in copies:
            c.wait()

    tok_load = local(tokens, tok_v, load_sem.at[0])
    cot_load = local(cotangent, cot_v, load_sem.at[1])
    out_load = local(outproj, out_v, load_sem.at[2])
    gain_loads = [local(mixgain_1d, mixgain.at[0], load_sem.at[3]), local(glugain_1d, glugain.at[0], load_sem.at[4])]
    in_loads = [local(inproj.at[k], col.at[k, :, pl.ds(0, HALF)], col_sem.at[k, 0]) for k in range(3)]
    tok_load.start()
    started(gain_loads)
    in_loads[0].start()
    in_loads[2].start()
    in_loads[1].start()

    def pair_loads(s):
        slot = (s + 1) % 3
        out = []
        for m, w in enumerate((gate_w, lift_w)):
            for i in range(4):
                lanes = pl.ds(128 * block_of(i, s), 128)
                out.append(local(w.at[:, lanes], col.at[slot, :, pl.ds(SPAN * m + 128 * i, 128)], col_sem.at[slot, 4 * m + i]))
        return out

    def down_loads(s):
        slot = s % 3
        return [
            local(down_w.at[pl.ds(128 * block_of(i, s), 128), :], down_ring.at[slot, pl.ds(128 * i, 128), :], down_sem.at[slot, i])
            for i in range(4)]

    barrier = pltpu.get_barrier_semaphore()
    for axis in range(3):
        for step in range(1, 4):
            pl.semaphore_signal(barrier, inc=1, device_id=(peer(axis, step), core), device_id_type=MESH)
    pl.semaphore_signal(barrier, inc=1, device_id=(seq, 1 - core), device_id_type=MESH)

    block = jnp.int32(0)
    for i in range(64):
        block = jnp.where(block_slots[i] == seq, i, block)
    before = block_slots[jnp.maximum(block - 1, 0)]
    after = block_slots[jnp.minimum(block + 1, 63)]
    has_after = (block < 63).astype(F32)
    rows = lax.broadcasted_iota(jnp.int32, (BLK, 1), 0)
    positions = block * BLK + rows
    start = jnp.zeros((BLK, 1), jnp.int32)
    offset = jnp.int32(0)
    for i in range(4):
        start = jnp.where(offset <= positions, offset, start)
        offset = offset + seq_lengths[i]
    mask1 = (positions - 1 >= start).astype(F32)
    mask2 = (positions - 2 >= start).astype(F32)

    def halo_links(land, job, phase):
        out = []
        for k in range(3):
            where = [pl.ds(0, 4) if axis in ROUTES[k][:phase] else pl.ds(place[axis], 1) for axis in range(3)]
            view = land.at[k, where[0], where[1], where[2]]
            axis = ROUTES[k][phase]
            for step in range(1, 4):
                out.append(link(view, view, halo_send.at[job, phase, k, step - 1], halo_recv.at[job, phase, k, step - 1], axis, step))
        return out

    def halo_rows(land, slot):
        at = (slot // 16, (slot // 4) % 4, slot % 4)
        return jnp.concatenate([land[k, at[0], at[1], at[2]] for k in range(3)], axis=1)

    def put_halo(land, two):
        width = two.shape[1] // 3
        for k in range(3):
            land[k, place[0], place[1], place[2]] = two[:, width * k:width * k + width]

    def first_norm(values):
        scale = lax.rsqrt(jnp.mean(values * values, axis=1, keepdims=True) + EPS)
        return scale, values * scale * mixgain[...]

    tok_load.wait()
    put_halo(tails, tok_v[BLK - 16:BLK, :].astype(F32)[14:16])
    pl.semaphore_wait(barrier, 10)
    halo = started(halo_links(tails, 0, 0))
    waited(gain_loads)
    scale_a, n1 = first_norm(tok_v[...].astype(F32))
    n_v[...] = n1.astype(BF16)
    in_loads[0].wait()
    b_v[...] = dot_nn(n_v[...], col[0, :, :HALF])
    waited(halo)
    halo = started(halo_links(tails, 0, 1))
    started([cot_load, out_load])
    for s in range(3):
        started(down_loads(s))
    in_loads[2].wait()
    x_v[...] = dot_nn(n_v[...], col[2, :, :HALF])
    v_v[...] = (b_v[...] * x_v[...]).astype(BF16).astype(F32)
    in_loads[1].wait()
    c_v[...] = dot_nn(n_v[...], col[1, :, :HALF])
    started(pair_loads(0))
    waited(halo)
    halo = started(halo_links(tails, 0, 2))
    m_src[0] = n_v[...].T
    cot_load.wait()
    s_src[1] = cot_v[...].T

    half = pl.ds(pl.multiple_of(core * HALF, HALF), HALF)

    def left_link(job, k, src, step):
        left = (s_left, m_left)[job]
        return link(src.at[half, :], left.at[k, half, pl.ds(128 * step, 128)],
                    l_send.at[job, k, step - 1], l_recv.at[job, k, step - 1], k, step)

    def send_left_s(k):
        src = s_src.at[1 if k == 2 else 0]
        local(src, s_left.at[k, :, pl.ds(0, 128)], own_left.at[0, k]).start()
        for step in range(1, 4):
            left_link(0, k, src, step).start()

    def send_left_m(k, which):
        for step in range(1, 4):
            @pl.when(((place[k] + step) % 4 == 3) == (which == 1))
            def _():
                left_link(1, k, m_src.at[which], step).start()

    def forward_left(job, k):
        left = (s_left, m_left)[job]
        out = []
        for step in range(1, 4):
            left_link(job, k, m_src.at[0], step).wait()
            view = left.at[k, half, pl.ds(128 * step, 128)]
            out.append(cross(view, view, f_send.at[job, k, step - 1], f_recv.at[job, k, step - 1]))
            out[-1].start()
        return out

    send_left_s(2)
    for k in range(3):
        send_left_m(k, 0)

    waited(halo)
    last_two = jnp.concatenate([halo_rows(tails, before), jnp.zeros((14, D), F32)], axis=0)
    edge = first_norm(last_two)[1].astype(BF16)
    carried = (dot_nn(edge, col[0, :, :HALF]) * dot_nn(edge, col[2, :, :HALF])).astype(BF16).astype(F32)
    for s in range(1, 3):
        started(pair_loads(s))
    row_is0, row_is1 = rows == 0, rows == 1
    tap0, tap1, tap2 = taps[0:1, :], taps[1:2, :], taps[2:3, :]

    def shifted():
        v = v_v[...]
        one = jnp.where(row_is0, carried[1:2], pltpu.roll(v, 1, 0)) * mask1
        two = jnp.where(row_is0, carried[0:1], jnp.where(row_is1, carried[1:2], pltpu.roll(v, 2, 0))) * mask2
        return v, one, two

    v0, v1, v2 = shifted()
    u_v[...] = tap0 * v0 + tap1 * v1 + tap2 * v2
    y_v[...] = (c_v[...] * u_v[...]).astype(BF16)
    out_load.wait()
    dn2_v[...] = dot_nn(y_v[...], out_v[...])
    swap = cross(dn2_v, h2_v, x_send.at[0], x_recv.at[0])
    swap.start()
    swap.wait()
    h2_v[...] = tok_v[...].astype(F32) + (dn2_v[...] + h2_v[...])
    h2 = h2_v[...]
    scale_b = lax.rsqrt(jnp.mean(h2 * h2, axis=1, keepdims=True) + EPS)
    n_v[...] = (h2 * scale_b * glugain[...]).astype(BF16)
    s_src[0] = n_v[...].T
    send_left_s(0)
    send_left_s(1)

    lefts, rights, dsends, dlands = (s_left, m_left), (s_right, m_right), (s_dsend, m_dsend), (s_dland, m_dland)

    def right_piece(job, k, i, g):
        if job == 0:
            return act.at[k, i, :, pl.ds(*GROUPS[g])]
        return mixed_r.at[k, :, pl.ds(pl.multiple_of(i * WM, WM), WM)]

    def right_links(job, k, g):
        lanes = pl.ds(*GROUPS[g])
        return [
            link(right_piece(job, k, (place[k] + step) % 4, g), rights[job].at[k, pl.ds(128 * step, 128), lanes],
                 r_send.at[job, k, g, step - 1], r_recv.at[job, k, g, step - 1], k, step)
            for step in range(1, 4)]

    def right_own(job, k, g):
        return local(right_piece(job, k, place[k], g), rights[job].at[k, pl.ds(0, 128), pl.ds(*GROUPS[g])], own_right.at[job, k, g])

    def send_right(job, g):
        for k in range(3):
            right_own(job, k, g).start()
            started(right_links(job, k, g))

    def b_out(job, k, j, g, row=0, count=384):
        lanes = pl.ds(*GROUPS[g])
        if job == 0:
            return s_bsend.at[k, j, pl.ds(row, count), lanes]
        return col.at[0, pl.ds(pl.multiple_of(384 * j + row, 96), count), pl.ds(WM * k, WM)]

    def b_in(job, k, i, g, row=0, count=384):
        if job == 0:
            return s_bland.at[k, i, pl.ds(row, count), pl.ds(*GROUPS[g])]
        return down_ring.at[i, pl.ds(row, count), pl.ds(WM * k, WM)]

    def c_out(job, k, j, g, row=0, count=96):
        return rights[job].at[k, pl.ds(pl.multiple_of(96 * j + row, 48), count), pl.ds(*GROUPS[g])]

    def c_in(job, k, i, g):
        if job == 0:
            return s_cland.at[k, i, :, pl.ds(*GROUPS[g])]
        return down_ring.at[i, pl.ds(0, 96), pl.ds(HALF + WM * k, WM)]

    def b_links(job, k, g):
        axis = (k + 1) % 3
        return [
            link(b_out(job, k, (place[axis] + step) % 4, g), b_in(job, k, step - 1, g),
                 b_send.at[job, k, g, step - 1], b_recv.at[job, k, g, step - 1], axis, step)
            for step in range(1, 4)]

    def c_links(job, k, g):
        axis = (k + 2) % 3
        return [
            link(c_out(job, k, (place[axis] + step) % 4, g), c_in(job, k, step - 1, g),
                 c_send.at[job, k, g, step - 1], c_recv.at[job, k, g, step - 1], axis, step)
            for step in range(1, 4)]

    def start_b(job, k, g):
        right_own(job, k, g).wait()
        waited(right_links(job, k, g))
        lanes = pl.ds(*GROUPS[g])

        def slab(x, carry):
            acc = dot_nn(lefts[job][k, pl.ds(pl.multiple_of(x * 384, 384), 384), :], rights[job][k, :, lanes])
            for j in range(4):
                if k == 0:
                    b_out(job, k, j, g, 96 * x, 96)[...] = acc[96 * j:96 * j + 96].astype(BF16)
                elif k == 1:
                    parts = [acc[96 * y + 24 * j:96 * y + 24 * j + 24] for y in range(4)]
                    b_out(job, k, j, g, 96 * x, 96)[...] = jnp.concatenate(parts, axis=0).astype(BF16)
                else:
                    b_out(job, k, x, g, 96 * j, 96)[...] = acc[96 * j:96 * j + 96].astype(BF16)
            return carry

        lax.fori_loop(0, 4, slab, 0)
        started(b_links(job, k, g))

    def start_c(job, k, g):
        waited(b_links(job, k, g))
        me = place[(k + 1) % 3]

        def summed(q):
            total = b_out(job, k, me, g, 96 * q, 96)[...].astype(F32)
            for i in range(3):
                total = total + b_in(job, k, i, g, 96 * q, 96)[...].astype(F32)
            return total

        if k == 0:
            for p in range(2):
                a, b = summed(2 * p), summed(2 * p + 1)
                for j in range(4):
                    both = jnp.concatenate([a[24 * j:24 * j + 24], b[24 * j:24 * j + 24]], axis=0)
                    c_out(job, k, j, g, 48 * p, 48)[...] = both.astype(BF16)
        else:
            for q in range(4):
                c_out(job, k, q, g)[...] = summed(q).astype(BF16)
        started(c_links(job, k, g))

    def d_links(job, k):
        return [
            link(dsends[job].at[k, (place[k] + step) % 4], dlands[job].at[k, step],
                 d_send.at[job, k, step - 1], d_recv.at[job, k, step - 1], k, step)
            for step in range(1, 4)]

    def start_d(job, k):
        dsend, dland = dsends[job], dlands[job]
        for g in range(4 if job == 0 else 1):
            first, width = GROUPS[g]
            waited(c_links(job, k, g))
            total = c_out(job, k, place[(k + 2) % 3], g)[...].astype(F32)
            for i in range(3):
                total = total + c_in(job, k, i, g)[...].astype(F32)
            pad = jnp.zeros((8, width), F32)
            for j in range(4):
                dsend[k, j, :, first:first + width] = jnp.concatenate([total[24 * j:24 * j + 24], pad], axis=0).astype(BF16)
        dland[k, 0] = dsend[k, place[k]]
        started(d_links(job, k))

    def finish(job, k):
        waited(d_links(job, k))
        stage = (h2_v, glu_v, dn2_v)[k]
        out = []
        for i in range(4):
            piece = dlands[job][k, (place[k] - i + 4) % 4].astype(F32)[:24]
            at = pl.ds(32 * i, 24)
            if job == 0:
                stage[32 * i:32 * i + 24, :WS] = piece
                skip = 0 if i < 3 else 4 * WS - FF
                src = stage.at[at, pl.ds(skip, WS - skip)]
                dst = (o_gate, o_lift, o_down)[k].at[:, pl.ds(WS * i, WS - skip)]
            else:
                stage[32 * i:32 * i + 24, 1024:1024 + WM] = piece
                src = stage.at[at, pl.ds(1024, WM)]
                dst = o_in.at[k, :, pl.ds(WM * i, WM)] if i < 3 else o_out.at[:, pl.ds(WM * k, WM)]
            out.append(local(src, dst, store_sem.at[job, k, i]))
        return started(out)

    glu_v[...] = jnp.zeros_like(glu_v)
    dn2_v[...] = jnp.zeros_like(dn2_v)

    def swiglu_step(s):
        slot = (s + 1) % 3
        waited(pair_loads(s))
        both = dot_nn(n_v[...], col[slot])
        gate_pre, lift_pre = both[:, :SPAN], both[:, SPAN:]
        waited(down_loads(s))
        hidden_grad = dot_nt(cot_v[...], down_ring[s % 3])
        sig = jax.nn.sigmoid(gate_pre)
        silu = gate_pre * sig
        hidden = (silu * lift_pre).astype(BF16)
        d_lift = (hidden_grad * silu).astype(BF16)
        d_gate = (hidden_grad * lift_pre * sig * (1.0 + gate_pre * (1.0 - sig))).astype(BF16)
        for i in range(4):
            for k, values in enumerate((d_gate, d_lift, hidden)):
                act[k, i, :, 128 * s:128 * s + 128] = values[:, 128 * i:128 * i + 128]

        def once(values):
            if s < STEPS - 1:
                return values
            return jnp.concatenate([values[:, :256], jnp.zeros((BLK, 128), BF16), values[:, 384:]], axis=1)

        glu_v[...] += dot_nn(once(hidden), down_ring[s % 3])
        dn2_v[...] += dot_nt(jnp.concatenate([once(d_gate), once(d_lift)], axis=1), col[slot])
        if s + 3 < STEPS:
            started(pair_loads(s + 3))
            started(down_loads(s + 3))

    def left_ready(job, fwd):
        for k in range(3):
            local(m_src.at[0], lefts[job].at[k, :, pl.ds(0, 128)], own_left.at[job, k]).wait()
            waited(fwd[k])

    for s in range(2):
        swiglu_step(s)
    send_right(0, 0)
    swiglu_step(2)
    fwd = [forward_left(0, k) for k in range(3)]
    swiglu_step(3)
    send_right(0, 1)
    left_ready(0, fwd)
    for k in range(3):
        start_b(0, k, 0)
    swiglu_step(4)
    swiglu_step(5)
    send_right(0, 2)
    for k in range(3):
        start_b(0, k, 1)
    swiglu_step(6)
    send_right(0, 3)
    started(in_loads)

    xh_send[0] = dn2_v[...].astype(BF16)
    swap_dn2 = cross(xh_send.at[0], xh_recv.at[0], x_send.at[1], x_recv.at[1])
    swap_dn2.start()
    xh_send[1] = glu_v[...].astype(BF16)
    swap_glu = cross(xh_send.at[1], xh_recv.at[1], x_send.at[2], x_recv.at[2])
    swap_glu.start()
    swap_dn2.wait()
    h2 = h2_v[...]
    z2 = h2 * scale_b
    dn2 = xh_send[0].astype(F32) + xh_recv[0].astype(F32)
    glu_term = jnp.sum(dn2 * z2, axis=0, keepdims=True)
    scaled = dn2 * glugain[...]
    glu_v[...] = cot_v[...].astype(F32) + scale_b * (scaled - z2 * jnp.mean(scaled * z2, axis=1, keepdims=True))
    n_v[...] = glu_v[...].astype(BF16)
    dy = dot_nt(n_v[...], out_v[...])
    d_c = (dy * u_v[...]).astype(BF16)
    du = dy * c_v[...]
    v0, v1, v2 = shifted()
    tap_terms = [jnp.sum(du * v, axis=0, keepdims=True) for v in (v0, v1, v2)]
    w1, w2 = tap1 * (du * mask1), tap2 * (du * mask2)
    put_halo(heads, jnp.concatenate([w2[0:1], w1[0:1] + w2[1:2]], axis=0))
    halo = started(halo_links(heads, 1, 0))
    u_v[...] = (tap0 * du + jnp.where(rows < 127, pltpu.roll(w1, 127, 0), 0.0)
                + jnp.where(rows < 126, pltpu.roll(w2, 126, 0), 0.0))
    m_src[1] = n_v[...].T
    for k in range(3):
        send_left_m(k, 1)
        local(m_src.at[jnp.where(place[k] == 3, 1, 0)], m_left.at[k, :, pl.ds(0, 128)], own_left.at[1, k]).start()
    y_out = y_v[...]
    for k in range(3):
        mixed_r[k, :, HALF:] = y_out[:, 256 * k:256 * k + 256]
    mixed_r[1, :, :HALF] = d_c
    swap_glu.wait()
    xh_send[1] = (h2_v[...] + (xh_send[1].astype(F32) + xh_recv[1].astype(F32))).astype(BF16)
    stores = started([local(xh_send.at[1], o_layer, load_sem.at[5])])
    start_b(0, 0, 2)
    waited(halo)
    halo = started(halo_links(heads, 1, 1))
    start_b(0, 1, 2)
    start_b(0, 2, 2)
    waited(halo)
    halo = started(halo_links(heads, 1, 2))
    for k in range(3):
        start_b(0, k, 3)

    waited(halo)
    incoming = halo_rows(heads, after) * has_after
    dv = u_v[...] + jnp.where(rows == 126, incoming[0:1], jnp.where(rows == 127, incoming[1:2], 0.0))
    mixed_r[0, :, :HALF] = (dv * x_v[...]).astype(BF16)
    mixed_r[2, :, :HALF] = (dv * b_v[...]).astype(BF16)
    send_right(1, 0)
    waited(in_loads)
    for k in range(3):
        part = dot_nt(mixed_r[k, :, :HALF], col[k, :, :HALF])
        if k == 0:
            dn2_v[...] = part
        else:
            dn2_v[...] += part
    xh_send[2] = dn2_v[...].astype(BF16)
    swap = cross(xh_send.at[2], xh_recv.at[2], x_send.at[3], x_recv.at[3])
    swap.start()
    fwd = [forward_left(1, k) for k in range(3)]
    swap.wait()
    dn1 = xh_send[2].astype(F32) + xh_recv[2].astype(F32)
    z1 = tok_v[...].astype(F32) * scale_a
    mix_term = jnp.sum(dn1 * z1, axis=0, keepdims=True)
    scaled = dn1 * mixgain[...]
    xh_send[2] = (glu_v[...] + scale_a * (scaled - z1 * jnp.mean(scaled * z1, axis=1, keepdims=True))).astype(BF16)
    stores += started([local(xh_send.at[2], o_input, load_sem.at[6])])

    def my_half(row):
        return jnp.where(core == 0, row[:, :HALF], row[:, HALF:])

    def gain_links(axis):
        view = gain_land.at[axis, place[axis]]
        return [link(view, view, gain_send.at[axis, step - 1], gain_recv.at[axis, step - 1], axis, step) for step in range(1, 4)]

    def gain_sum(axis):
        return (gain_land[axis, 0] + gain_land[axis, 1]) + (gain_land[axis, 2] + gain_land[axis, 3])

    gain_land[0, place[0]] = jnp.concatenate(
        [my_half(mix_term), my_half(glu_term), *tap_terms, jnp.zeros((3, HALF), F32)], axis=0)
    gains = started(gain_links(0))
    left_ready(1, fwd)
    for k in range(3):
        start_b(1, k, 0)
    for g in range(2):
        for k in range(3):
            start_c(0, k, g)
    waited(gains)
    gain_land[1, place[1]] = gain_sum(0)
    gains = started(gain_links(1))
    for g in range(2, 4):
        for k in range(3):
            start_c(0, k, g)
    waited(gains)
    gain_land[2, place[2]] = gain_sum(1)
    gains = started(gain_links(2))
    for k in range(3):
        start_c(1, k, 0)
    waited(gains)
    v_v[0:8, :] = gain_sum(2)
    stores += started([local(v_v.at[pl.ds(0, 8), :], o_gains, load_sem.at[7])])
    for job in range(2):
        for k in range(3):
            start_d(job, k)
    for job in range(2):
        for k in range(3):
            stores += finish(job, k)
    waited(stores)


def run_layer(seq_lengths, block_slots, mixgain, glugain, taps, tokens, cotangent, inproj, outproj, gate_w, lift_w, down_w):
    vm = pl.BlockSpec(memory_space=pltpu.VMEM)
    sm = pl.BlockSpec(memory_space=pltpu.SMEM)
    hbm = pl.BlockSpec(memory_space=pl.ANY)
    dma = pltpu.SemaphoreType.DMA
    shape = jax.ShapeDtypeStruct
    row, full16, full32, half32 = (
        pltpu.VMEM((1, D), F32), pltpu.VMEM((BLK, D), BF16), pltpu.VMEM((BLK, D), F32), pltpu.VMEM((BLK, HALF), F32))
    return pl.pallas_call(
        layer_kernel,
        out_shape=[shape((BLK, D), BF16), shape((BLK, D), BF16), shape((8, HALF), F32)]
        + [shape(s, F32) for s in ((24, FF), (24, FF), (24, FF), (3, 24, HALF), (24, HALF))],
        in_specs=[sm, sm, hbm, hbm, vm] + [hbm] * 7,
        out_specs=[hbm] * 8,
        scratch_shapes=[
            row, row, full16, full16, full16,
            half32, half32, half32, half32, half32, pltpu.VMEM((BLK, HALF), BF16),
            full32, full32, full32,
            pltpu.VMEM((3, D, 2 * SPAN), BF16), pltpu.VMEM((3, SPAN, D), BF16), pltpu.VMEM((HALF, D), BF16),
            pltpu.VMEM((3, 4, BLK, WS), BF16), pltpu.VMEM((3, BLK, 4 * WM), BF16),
            pltpu.VMEM((2, D, BLK), BF16), pltpu.VMEM((2, D, BLK), BF16),
            pltpu.VMEM((3, BLK, D), BF16), pltpu.VMEM((3, BLK, D), BF16),
            pltpu.VMEM((3, 4, 4, 4, 2, 512), F32), pltpu.VMEM((3, 4, 4, 4, 2, 256), F32),
            pltpu.VMEM((3, 4, 8, HALF), F32),
            pltpu.VMEM((3, D, 512), BF16), pltpu.VMEM((3, 512, WS), BF16), pltpu.VMEM((3, 4, 384, WS), BF16),
            pltpu.VMEM((3, 3, 384, WS), BF16), pltpu.VMEM((3, 3, 96, WS), BF16),
            pltpu.VMEM((3, 4, 32, WS), BF16), pltpu.VMEM((3, 4, 32, WS), BF16),
            pltpu.VMEM((3, D, 512), BF16), pltpu.VMEM((3, 512, WM), BF16),
            pltpu.VMEM((3, 4, 32, WM), BF16), pltpu.VMEM((3, 4, 32, WM), BF16),
            dma((8,)), dma((3, 8)), dma((3, 4)), dma((2, 3, 4)), dma((4,)), dma((4,)),
            dma((2, 3, 3, 3)), dma((2, 3, 3, 3)), dma((3, 3)), dma((3, 3)),
        ]
        + [dma((2, 3, 3))] * 4 + [dma((2, 3, 4, 3))] * 6 + [dma((2, 3, 3))] * 2 + [dma((2, 3)), dma((2, 3, 4))],
        compiler_params=pltpu.CompilerParams(collective_id=1, has_side_effects=True, vmem_limit_bytes=LIMIT),
        name="layer",
    )(seq_lengths, block_slots, mixgain, glugain, taps, tokens, cotangent, inproj, outproj, gate_w, lift_w, down_w)


def place_kernel(*refs):
    ins, outs, held, in_sems, out_sems = refs[:8], refs[8:18], refs[18:26], refs[26], refs[27]
    loads = [pltpu.make_async_copy(a, b, in_sems.at[i]) for i, (a, b) in enumerate(zip(ins, held))]
    for c in loads:
        c.start()
    gains = held[2]
    parts = [held[0], held[1], gains.at[0], gains.at[1], gains.at[pl.ds(2, 3)], *held[3:]]
    stores = []
    for i, (a, b) in enumerate(zip(parts, outs)):
        if i not in (3, 4):
            loads[i if i < 3 else i - 2].wait()
        stores.append(pltpu.make_async_copy(a, b, out_sems.at[i]))
        stores[-1].start()
    for c in stores:
        c.wait()


def place_outputs(results):
    hbm = pl.BlockSpec(memory_space=pl.ANY)
    shape = jax.ShapeDtypeStruct
    return pl.pallas_call(
        place_kernel,
        out_shape=[shape((BLK, D), BF16), shape((BLK, D), BF16), shape((HALF,), F32), shape((HALF,), F32), shape((3, HALF), F32)]
        + [shape(s, F32) for s in ((24, FF), (24, FF), (24, FF), (3, 24, HALF), (24, HALF))],
        in_specs=[hbm] * 8,
        out_specs=[hbm] * 10,
        scratch_shapes=[pltpu.VMEM(r.shape, r.dtype) for r in results] + [pltpu.SemaphoreType.DMA((8,)), pltpu.SemaphoreType.DMA((10,))],
        name="place",
    )(*results)


def on_device(
    tokens, cotangent, seq_lengths, block_slots, mixgain, inproj, conv_taps, outproj, glugain, gate_weight, lift_weight, down_weight
):
    results = run_layer(
        seq_lengths, block_slots, mixgain, glugain, conv_taps,
        tokens, cotangent, inproj, outproj, gate_weight, lift_weight, down_weight,
    )
    layer_out, input_grad, mixgain_grad, glugain_grad, taps_grad, gate_grad, lift_grad, down_rows, inproj_grad, out_rows = place_outputs(results)
    return (
        layer_out, input_grad, mixgain_grad, inproj_grad, taps_grad, out_rows.T, glugain_grad, gate_grad, lift_grad, down_rows.T,
    )


def solution(mesh):
    in_specs = (
        P("seq", None), P("seq", None), P(), P(), P(), P(None, None, "ch"), P(None, "ch"), P("ch", None),
        P(), P(None, "ch"), P(None, "ch"), P("ch", None),
    )
    out_specs = (
        P("seq", None), P("seq", None), P("ch"), P(None, "seq", "ch"), P(None, "ch"), P("ch", "seq"),
        P("ch"), P("seq", "ch"), P("seq", "ch"), P("ch", "seq"),
    )
    return jax.shard_map(on_device, mesh=mesh, in_specs=in_specs, out_specs=out_specs, check_vma=False)
```

time: 178 us -> 140 us (0.79)
  Pallas kernels: 160 us -> 139 us
  local copies, waits for them, and re-layouts: 17.2 us -> 0 us
    pallas_call x1, Pallas kernels: 160 us -> 136 us  [run_layer(): pl.pallas_call(layer_kernel, out_shape=[shape((BLK, D), BF16), shape((BLK...]
    unnamed x7 -> x0, local copies, waits for them, and re-layouts: 11.8 us -> none
    slice x2 -> x0, local copies, waits for them, and re-layouts: 2.77 us -> none  [the longest x1 1.43 us: on_device(): gains[1]]
    broadcast_in_dim x2 -> x0, local copies, waits for them, and re-layouts: 2.59 us -> none  [the longest x1 1.3 us: on_device(): mixgain[None, :]]
    pallas_call x0 -> x1, Pallas kernels: none -> 2.46 us  [place_outputs(): pl.pallas_call(place_kernel, out_shape=[shape((BLK, D), BF16), shape((BLK...]
where the time goes in v3:
time: 140 us
  Pallas kernels  139 us (99%)
    pallas_call x1, Pallas kernels, run_layer(): pl.pallas_call(layer_kernel, out_shape=[shape((BLK, D), BF16), shape((BLK...  136 us

profile of v3, /device:TPU:0, one launch (start us, length us, event | category | flops | bytes accessed | tf_op | source)
XLA Modules:
  0.0 139.8 jit_solution(17532643024873844343)
XLA Ops:
  0.6 136.5 %layer.1 = (bf16[128,1536]{1,0:T(8,128)(2,1)}, bf16[128,1536]{1,0:T(8,128)(2,1)}, f32[8,768]{1,0:T(8,128)}, f32[24,3456]{1,0:T(8,128)}, f32[24,3456]{1,0:T(8,128...) custom-call(s32[4]{0:T(128)} %seq_lengths.1, s32[64]{0:T(128)} %block_slots.1, f32[1536]{0:T(1024)} %mixgain_1d.1, ...), custom_call_target="tpu_custom_call" | custom-call | tf_op jit(solution)/shard_map/layer/pallas_call | solution.py:541
  137.1 2.5 %place.1 = (bf16[128,1536]{1,0:T(8,128)(2,1)}, bf16[128,1536]{1,0:T(8,128)(2,1)}, f32[768]{0:T(1024)}, f32[768]{0:T(1024)}, f32[3,768]{1,0:T(4,128)}, /*index=5*...) custom-call(bf16[128,1536]{1,0:T(8,128)(2,1)} %get-tuple-element.28.refs_0, ...), custom_call_target="tpu_custom_call" | custom-call | tf_op jit(solution)/shard_map/place/pallas_call | solution.py:591

commit v4 on v3

--- a/solution.py
+++ b/solution.py
@@ -20,6 +20,10 @@
     return lax.dot_general(a, b, (((1,), (1,)), ((), ())), preferred_element_type=F32)
 
 
+def outer(a, b):
+    return lax.dot_general(a, b, (((0,), (0,)), ((), ())), preferred_element_type=F32)
+
+
 def dot_nn(a, b):
     return jnp.dot(a, b, preferred_element_type=F32)
 
@@ -33,11 +37,11 @@
     tokens, cotangent, inproj, outproj, gate_w, lift_w, down_w,
     o_layer, o_input, o_gains, o_gate, o_lift, o_down, o_in, o_out,
     mixgain, glugain, tok_v, cot_v, n_v, b_v, c_v, x_v, v_v, u_v, y_v, h2_v, glu_v, dn2_v,
-    col, down_ring, out_v, act, mixed_r, s_src, m_src, xh_send, xh_recv, tails, heads, gain_land,
+    col, down_ring, out_v, da_v, act, mixed_r, s_src, m_src, e_src, eb_v, ex_v, er_src, e_left, e_right, xh_send, xh_recv, tails, heads, gain_land,
     s_left, s_right, s_bsend, s_bland, s_cland, s_dsend, s_dland, m_left, m_right, m_dsend, m_dland,
     load_sem, col_sem, down_sem, store_sem, x_send, x_recv, halo_send, halo_recv, gain_send, gain_recv,
     l_send, l_recv, f_send, f_recv, r_send, r_recv,
-    b_send, b_recv, c_send, c_recv, d_send, d_recv, own_left, own_right,
+    b_send, b_recv, c_send, c_recv, d_send, d_recv, own_left, own_right, e_send, e_recv, own_edge,
 ):
     seq, core = lax.axis_index("seq"), lax.axis_index("ch")
     place = (seq // 16, (seq // 4) % 4, seq % 4)
@@ -88,8 +92,8 @@
                 out.append(local(w.at[:, lanes], col.at[slot, :, pl.ds(SPAN * m + 128 * i, 128)], col_sem.at[slot, 4 * m + i]))
         return out
 
-    def down_loads(s):
-        slot = s % 3
+    def down_loads(t):
+        s, slot = t % STEPS, t % 3
         return [
             local(down_w.at[pl.ds(128 * block_of(i, s), 128), :], down_ring.at[slot, pl.ds(128 * i, 128), :], down_sem.at[slot, i])
             for i in range(4)]
@@ -148,22 +152,29 @@
     n_v[...] = n1.astype(BF16)
     in_loads[0].wait()
     b_v[...] = dot_nn(n_v[...], col[0, :, :HALF])
+    started([cot_load])
+    for s in range(3):
+        started(down_loads(s))
     waited(halo)
     halo = started(halo_links(tails, 0, 1))
-    started([cot_load, out_load])
-    for s in range(3):
-        started(down_loads(s))
     in_loads[2].wait()
     x_v[...] = dot_nn(n_v[...], col[2, :, :HALF])
     v_v[...] = (b_v[...] * x_v[...]).astype(BF16).astype(F32)
     in_loads[1].wait()
     c_v[...] = dot_nn(n_v[...], col[1, :, :HALF])
     started(pair_loads(0))
+    cot_load.wait()
+
+    def hidden_grads(first, end):
+        for s in range(first, end):
+            waited(down_loads(s))
+            da_v[s] = dot_nt(cot_v[...], down_ring[s % 3])
+            started(down_loads(s + 3))
+
     waited(halo)
     halo = started(halo_links(tails, 0, 2))
+    s_src[1] = cot_v[...].T
     m_src[0] = n_v[...].T
-    cot_load.wait()
-    s_src[1] = cot_v[...].T
 
     half = pl.ds(pl.multiple_of(core * HALF, HALF), HALF)
 
@@ -197,11 +208,36 @@
     send_left_s(2)
     for k in range(3):
         send_left_m(k, 0)
+    started([out_load])
+    hidden_grads(0, STEPS)
 
     waited(halo)
     last_two = jnp.concatenate([halo_rows(tails, before), jnp.zeros((14, D), F32)], axis=0)
     edge = first_norm(last_two)[1].astype(BF16)
-    carried = (dot_nn(edge, col[0, :, :HALF]) * dot_nn(edge, col[2, :, :HALF])).astype(BF16).astype(F32)
+    edge_b, edge_x = dot_nn(edge, col[0, :, :HALF]), dot_nn(edge, col[2, :, :HALF])
+    carried = (edge_b * edge_x).astype(BF16).astype(F32)
+    e_src[...] = edge
+    eb_v[...] = edge_b
+    ex_v[...] = edge_x
+
+    def edge_left_links(n):
+        return [
+            link(e_src, e_left.at[n, pl.ds(16 * step, 16), :], e_send.at[0, n, step - 1], e_recv.at[0, n, step - 1], 2 * n, step)
+            for step in range(1, 4)]
+
+    def edge_piece(n, i):
+        return er_src.at[n, :, pl.ds(pl.multiple_of(i * WM, WM), WM)]
+
+    def edge_right_links(n):
+        return [
+            link(edge_piece(n, (place[2 * n] + step) % 4), e_right.at[n, pl.ds(16 * step, 16), :],
+                 e_send.at[1, n, step - 1], e_recv.at[1, n, step - 1], 2 * n, step)
+            for step in range(1, 4)]
+
+    def edge_own(n):
+        return [
+            local(e_src, e_left.at[n, pl.ds(0, 16), :], own_edge.at[0, n]),
+            local(edge_piece(n, place[2 * n]), e_right.at[n, pl.ds(0, 16), :], own_edge.at[1, n])]
     for s in range(1, 3):
         started(pair_loads(s))
     row_is0, row_is1 = rows == 0, rows == 1
@@ -255,7 +291,7 @@
         lanes = pl.ds(*GROUPS[g])
         if job == 0:
             return s_bsend.at[k, j, pl.ds(row, count), lanes]
-        return col.at[0, pl.ds(pl.multiple_of(384 * j + row, 96), count), pl.ds(WM * k, WM)]
+        return col.at[1, pl.ds(pl.multiple_of(384 * j + row, 96), count), pl.ds(WM * k, WM)]
 
     def b_in(job, k, i, g, row=0, count=384):
         if job == 0:
@@ -270,12 +306,21 @@
             return s_cland.at[k, i, :, pl.ds(*GROUPS[g])]
         return down_ring.at[i, pl.ds(0, 96), pl.ds(HALF + WM * k, WM)]
 
-    def b_links(job, k, g):
+    LOW, HIGH = 0, 192
+
+    def b_links(job, k, g, which):
         axis = (k + 1) % 3
-        return [
-            link(b_out(job, k, (place[axis] + step) % 4, g), b_in(job, k, step - 1, g),
-                 b_send.at[job, k, g, step - 1], b_recv.at[job, k, g, step - 1], axis, step)
-            for step in range(1, 4)]
+        me = place[axis]
+        opposite, ahead, behind = (me + 2) % 4, (me + 1) % 4, (me + 3) % 4
+        table = (
+            (opposite, LOW, 2, 1), (ahead, HIGH, 0, 1), (opposite, HIGH, 2, 3),
+            (behind, LOW, 1, 3), (ahead, LOW, 0, 1), (behind, HIGH, 1, 3))
+        out = []
+        for n in which:
+            part, row, land, step = table[n]
+            out.append(link(b_out(job, k, part, g, row, 192), b_in(job, k, land, g, row, 192),
+                            b_send.at[job, k, g, n], b_recv.at[job, k, g, n], axis, step))
+        return out
 
     def c_links(job, k, g):
         axis = (k + 2) % 3
@@ -288,29 +333,49 @@
         right_own(job, k, g).wait()
         waited(right_links(job, k, g))
         lanes = pl.ds(*GROUPS[g])
+        edges = job == 1 and k != 1
+        if edges:
+            for c in edge_own(k // 2):
+                c.wait()
+            waited(edge_left_links(k // 2))
+            waited(edge_right_links(k // 2))
 
         def slab(x, carry):
-            acc = dot_nn(lefts[job][k, pl.ds(pl.multiple_of(x * 384, 384), 384), :], rights[job][k, :, lanes])
-            for j in range(4):
-                if k == 0:
-                    b_out(job, k, j, g, 96 * x, 96)[...] = acc[96 * j:96 * j + 96].astype(BF16)
-                elif k == 1:
-                    parts = [acc[96 * y + 24 * j:96 * y + 24 * j + 24] for y in range(4)]
-                    b_out(job, k, j, g, 96 * x, 96)[...] = jnp.concatenate(parts, axis=0).astype(BF16)
-                else:
-                    b_out(job, k, x, g, 96 * j, 96)[...] = acc[96 * j:96 * j + 96].astype(BF16)
+            at = pl.ds(pl.multiple_of(x * HALF, HALF), HALF)
+            acc = dot_nn(lefts[job][k, at, :], rights[job][k, :, lanes])
+            if edges:
+                acc = acc + outer(e_left[k // 2, :, at], e_right[k // 2])
+            for h in range(2):
+                row = pl.multiple_of(192 * x + 96 * h, 96)
+                for j in range(4):
+                    base = 384 * h + 96 * j
+                    if k == 0:
+                        b_out(job, k, j, g, row, 96)[...] = acc[base:base + 96].astype(BF16)
+                    elif k == 1:
+                        parts = [acc[384 * h + 96 * y + 24 * j:384 * h + 96 * y + 24 * j + 24] for y in range(4)]
+                        b_out(job, k, j, g, row, 96)[...] = jnp.concatenate(parts, axis=0).astype(BF16)
+                    else:
+                        b_out(job, k, 2 * x + h, g, 96 * j, 96)[...] = acc[base:base + 96].astype(BF16)
             return carry
 
-        lax.fori_loop(0, 4, slab, 0)
-        started(b_links(job, k, g))
+        lax.fori_loop(0, 2, slab, 0)
+        started(b_links(job, k, g, range(4)))
+
+    def pass_on(job, k, g):
+        waited(b_links(job, k, g, (0, 2)))
+        me = place[(k + 1) % 3]
+        for step, row in ((1, LOW), (3, HIGH)):
+            own, via = b_out(job, k, (me + step) % 4, g, row, 192), b_in(job, k, 2, g, row, 192)
+            own[...] = (own[...].astype(F32) + via[...].astype(F32)).astype(BF16)
+        started(b_links(job, k, g, (4, 5)))
 
     def start_c(job, k, g):
-        waited(b_links(job, k, g))
+        waited(b_links(job, k, g, (1, 3, 4, 5)))
         me = place[(k + 1) % 3]
 
         def summed(q):
             total = b_out(job, k, me, g, 96 * q, 96)[...].astype(F32)
-            for i in range(3):
+            for i in range(2):
                 total = total + b_in(job, k, i, g, 96 * q, 96)[...].astype(F32)
             return total
 
@@ -372,8 +437,7 @@
         waited(pair_loads(s))
         both = dot_nn(n_v[...], col[slot])
         gate_pre, lift_pre = both[:, :SPAN], both[:, SPAN:]
-        waited(down_loads(s))
-        hidden_grad = dot_nt(cot_v[...], down_ring[s % 3])
+        hidden_grad = da_v[s]
         sig = jax.nn.sigmoid(gate_pre)
         silu = gate_pre * sig
         hidden = (silu * lift_pre).astype(BF16)
@@ -388,11 +452,12 @@
                 return values
             return jnp.concatenate([values[:, :256], jnp.zeros((BLK, 128), BF16), values[:, 384:]], axis=1)
 
-        glu_v[...] += dot_nn(once(hidden), down_ring[s % 3])
+        waited(down_loads(STEPS + s))
+        glu_v[...] += dot_nn(once(hidden), down_ring[(STEPS + s) % 3])
         dn2_v[...] += dot_nt(jnp.concatenate([once(d_gate), once(d_lift)], axis=1), col[slot])
         if s + 3 < STEPS:
             started(pair_loads(s + 3))
-            started(down_loads(s + 3))
+            started(down_loads(STEPS + s + 3))
 
     def left_ready(job, fwd):
         for k in range(3):
@@ -414,6 +479,8 @@
     send_right(0, 2)
     for k in range(3):
         start_b(0, k, 1)
+    for k in range(3):
+        pass_on(0, k, 0)
     swiglu_step(6)
     send_right(0, 3)
     started(in_loads)
@@ -438,37 +505,44 @@
     v0, v1, v2 = shifted()
     tap_terms = [jnp.sum(du * v, axis=0, keepdims=True) for v in (v0, v1, v2)]
     w1, w2 = tap1 * (du * mask1), tap2 * (du * mask2)
-    put_halo(heads, jnp.concatenate([w2[0:1], w1[0:1] + w2[1:2]], axis=0))
-    halo = started(halo_links(heads, 1, 0))
-    u_v[...] = (tap0 * du + jnp.where(rows < 127, pltpu.roll(w1, 127, 0), 0.0)
-                + jnp.where(rows < 126, pltpu.roll(w2, 126, 0), 0.0))
+    two = jnp.concatenate([w2[0:1], w1[0:1] + w2[1:2]], axis=0)
+    put_halo(heads, two)
+    dv = (tap0 * du + jnp.where(rows < 127, pltpu.roll(w1, 127, 0), 0.0)
+          + jnp.where(rows < 126, pltpu.roll(w2, 126, 0), 0.0))
+    mixed_r[0, :, :HALF] = (dv * x_v[...]).astype(BF16)
+    mixed_r[1, :, :HALF] = d_c
+    mixed_r[2, :, :HALF] = (dv * b_v[...]).astype(BF16)
+    y_out = y_v[...]
+    for k in range(3):
+        mixed_r[k, :, HALF:] = y_out[:, 256 * k:256 * k + 256]
+    share = jnp.concatenate([two, jnp.zeros((14, HALF), F32)], axis=0)
+    none = jnp.zeros((16, WM), BF16)
+    for n, other in enumerate((ex_v, eb_v)):
+        er_src[n] = jnp.concatenate([(share * other[...]).astype(BF16), none], axis=1)
+    send_right(1, 0)
+    for n in range(2):
+        started(edge_own(n))
+        started(edge_left_links(n))
+        started(edge_right_links(n))
     m_src[1] = n_v[...].T
     for k in range(3):
         send_left_m(k, 1)
         local(m_src.at[jnp.where(place[k] == 3, 1, 0)], m_left.at[k, :, pl.ds(0, 128)], own_left.at[1, k]).start()
-    y_out = y_v[...]
-    for k in range(3):
-        mixed_r[k, :, HALF:] = y_out[:, 256 * k:256 * k + 256]
-    mixed_r[1, :, :HALF] = d_c
+    halo = started(halo_links(heads, 1, 0))
     swap_glu.wait()
     xh_send[1] = (h2_v[...] + (xh_send[1].astype(F32) + xh_recv[1].astype(F32))).astype(BF16)
     stores = started([local(xh_send.at[1], o_layer, load_sem.at[5])])
-    start_b(0, 0, 2)
+    for k in range(3):
+        start_b(0, k, 2)
+    for k in range(3):
+        pass_on(0, k, 1)
     waited(halo)
     halo = started(halo_links(heads, 1, 1))
-    start_b(0, 1, 2)
-    start_b(0, 2, 2)
-    waited(halo)
-    halo = started(halo_links(heads, 1, 2))
     for k in range(3):
         start_b(0, k, 3)
-
-    waited(halo)
-    incoming = halo_rows(heads, after) * has_after
-    dv = u_v[...] + jnp.where(rows == 126, incoming[0:1], jnp.where(rows == 127, incoming[1:2], 0.0))
-    mixed_r[0, :, :HALF] = (dv * x_v[...]).astype(BF16)
-    mixed_r[2, :, :HALF] = (dv * b_v[...]).astype(BF16)
-    send_right(1, 0)
+    for k in range(3):
+        pass_on(0, k, 2)
+
     waited(in_loads)
     for k in range(3):
         part = dot_nt(mixed_r[k, :, :HALF], col[k, :, :HALF])
@@ -476,17 +550,35 @@
             dn2_v[...] = part
         else:
             dn2_v[...] += part
-    xh_send[2] = dn2_v[...].astype(BF16)
-    swap = cross(xh_send.at[2], xh_recv.at[2], x_send.at[3], x_recv.at[3])
+    waited(halo)
+    halo = started(halo_links(heads, 1, 2))
+    fwd = [forward_left(1, k) for k in range(3)]
+    left_ready(1, fwd)
+    for k in range(3):
+        start_b(1, k, 0)
+    for k in range(3):
+        pass_on(0, k, 3)
+    for k in range(3):
+        start_c(0, k, 0)
+    waited(halo)
+    incoming = jnp.concatenate([jnp.zeros((14, HALF), F32), halo_rows(heads, after) * has_after], axis=0)
+    extra = dot_nt((incoming * x_v[BLK - 16:, :]).astype(BF16), col[0, :, :HALF])
+    extra += dot_nt((incoming * b_v[BLK - 16:, :]).astype(BF16), col[2, :, :HALF])
+    dn2_v[BLK - 16:, :] += extra
+    xh_send[0] = dn2_v[...].astype(BF16)
+    swap = cross(xh_send.at[0], xh_recv.at[0], x_send.at[3], x_recv.at[3])
     swap.start()
-    fwd = [forward_left(1, k) for k in range(3)]
+    for k in range(3):
+        pass_on(1, k, 0)
+    for k in range(3):
+        start_c(0, k, 1)
     swap.wait()
-    dn1 = xh_send[2].astype(F32) + xh_recv[2].astype(F32)
+    dn1 = xh_send[0].astype(F32) + xh_recv[0].astype(F32)
     z1 = tok_v[...].astype(F32) * scale_a
     mix_term = jnp.sum(dn1 * z1, axis=0, keepdims=True)
     scaled = dn1 * mixgain[...]
-    xh_send[2] = (glu_v[...] + scale_a * (scaled - z1 * jnp.mean(scaled * z1, axis=1, keepdims=True))).astype(BF16)
-    stores += started([local(xh_send.at[2], o_input, load_sem.at[6])])
+    xh_send[0] = (glu_v[...] + scale_a * (scaled - z1 * jnp.mean(scaled * z1, axis=1, keepdims=True))).astype(BF16)
+    stores += started([local(xh_send.at[0], o_input, load_sem.at[6])])
 
     def my_half(row):
         return jnp.where(core == 0, row[:, :HALF], row[:, HALF:])
@@ -501,29 +593,25 @@
     gain_land[0, place[0]] = jnp.concatenate(
         [my_half(mix_term), my_half(glu_term), *tap_terms, jnp.zeros((3, HALF), F32)], axis=0)
     gains = started(gain_links(0))
-    left_ready(1, fwd)
-    for k in range(3):
-        start_b(1, k, 0)
-    for g in range(2):
-        for k in range(3):
-            start_c(0, k, g)
+    for k in range(3):
+        start_c(0, k, 2)
     waited(gains)
     gain_land[1, place[1]] = gain_sum(0)
     gains = started(gain_links(1))
-    for g in range(2, 4):
-        for k in range(3):
-            start_c(0, k, g)
+    for k in range(3):
+        start_c(0, k, 3)
+    for k in range(3):
+        start_c(1, k, 0)
     waited(gains)
     gain_land[2, place[2]] = gain_sum(1)
     gains = started(gain_links(2))
     for k in range(3):
-        start_c(1, k, 0)
+        start_d(0, k)
     waited(gains)
     v_v[0:8, :] = gain_sum(2)
     stores += started([local(v_v.at[pl.ds(0, 8), :], o_gains, load_sem.at[7])])
-    for job in range(2):
-        for k in range(3):
-            start_d(job, k)
+    for k in range(3):
+        start_d(1, k)
     for job in range(2):
         for k in range(3):
             stores += finish(job, k)
@@ -549,9 +637,11 @@
             half32, half32, half32, half32, half32, pltpu.VMEM((BLK, HALF), BF16),
             full32, full32, full32,
             pltpu.VMEM((3, D, 2 * SPAN), BF16), pltpu.VMEM((3, SPAN, D), BF16), pltpu.VMEM((HALF, D), BF16),
-            pltpu.VMEM((3, 4, BLK, WS), BF16), pltpu.VMEM((3, BLK, 4 * WM), BF16),
+            pltpu.VMEM((STEPS, BLK, SPAN), F32), pltpu.VMEM((3, 4, BLK, WS), BF16), pltpu.VMEM((3, BLK, 4 * WM), BF16),
             pltpu.VMEM((2, D, BLK), BF16), pltpu.VMEM((2, D, BLK), BF16),
-            pltpu.VMEM((3, BLK, D), BF16), pltpu.VMEM((3, BLK, D), BF16),
+            pltpu.VMEM((16, D), BF16), pltpu.VMEM((16, HALF), F32), pltpu.VMEM((16, HALF), F32),
+            pltpu.VMEM((2, 16, 4 * WM), BF16), pltpu.VMEM((2, 64, D), BF16), pltpu.VMEM((2, 64, WM), BF16),
+            pltpu.VMEM((2, BLK, D), BF16), pltpu.VMEM((2, BLK, D), BF16),
             pltpu.VMEM((3, 4, 4, 4, 2, 512), F32), pltpu.VMEM((3, 4, 4, 4, 2, 256), F32),
             pltpu.VMEM((3, 4, 8, HALF), F32),
             pltpu.VMEM((3, D, 512), BF16), pltpu.VMEM((3, 512, WS), BF16), pltpu.VMEM((3, 4, 384, WS), BF16),
@@ -562,7 +652,8 @@
             dma((8,)), dma((3, 8)), dma((3, 4)), dma((2, 3, 4)), dma((4,)), dma((4,)),
             dma((2, 3, 3, 3)), dma((2, 3, 3, 3)), dma((3, 3)), dma((3, 3)),
         ]
-        + [dma((2, 3, 3))] * 4 + [dma((2, 3, 4, 3))] * 6 + [dma((2, 3, 3))] * 2 + [dma((2, 3)), dma((2, 3, 4))],
+        + [dma((2, 3, 3))] * 4 + [dma((2, 3, 4, 3))] * 2 + [dma((2, 3, 4, 6))] * 2 + [dma((2, 3, 4, 3))] * 2 + [dma((2, 3, 3))] * 2
+        + [dma((2, 3)), dma((2, 3, 4)), dma((2, 2, 3)), dma((2, 2, 3)), dma((2, 2))],
         compiler_params=pltpu.CompilerParams(collective_id=1, has_side_effects=True, vmem_limit_bytes=LIMIT),
         name="layer",
     )(seq_lengths, block_slots, mixgain, glugain, taps, tokens, cotangent, inproj, outproj, gate_w, lift_w, down_w)

time: 140 us -> 131 us (0.936)
  Pallas kernels: 139 us -> 130 us
    pallas_call x1, Pallas kernels: 136 us -> 127 us  [run_layer(): pl.pallas_call(layer_kernel, out_shape=[shape((BLK, D), BF16), shape((BLK...]
where the time goes in v4:
time: 131 us
  Pallas kernels  130 us (99%)
    pallas_call x1, Pallas kernels, run_layer(): pl.pallas_call(layer_kernel, out_shape=[shape((BLK, D), BF16), shape((BLK...  127 us

profile of v4, /device:TPU:0, one launch (start us, length us, event | category | flops | bytes accessed | tf_op | source)
XLA Modules:
  0.0 130.7 jit_solution(16918150263825050568)
XLA Ops:
  0.6 127.4 %layer.1 = (bf16[128,1536]{1,0:T(8,128)(2,1)}, bf16[128,1536]{1,0:T(8,128)(2,1)}, f32[8,768]{1,0:T(8,128)}, f32[24,3456]{1,0:T(8,128)}, f32[24,3456]{1,0:T(8,128...) custom-call(s32[4]{0:T(128)} %seq_lengths.1, s32[64]{0:T(128)} %block_slots.1, f32[1536]{0:T(1024)} %mixgain_1d.1, ...), custom_call_target="tpu_custom_call" | custom-call | tf_op jit(solution)/shard_map/layer/pallas_call | solution.py:629
  128.0 2.5 %place.1 = (bf16[128,1536]{1,0:T(8,128)(2,1)}, bf16[128,1536]{1,0:T(8,128)(2,1)}, f32[768]{0:T(1024)}, f32[768]{0:T(1024)}, f32[3,768]{1,0:T(4,128)}, /*index=5*...) custom-call(bf16[128,1536]{1,0:T(8,128)(2,1)} %get-tuple-element.28.refs_0, ...), custom_call_target="tpu_custom_call" | custom-call | tf_op jit(solution)/shard_map/place/pallas_call | solution.py:682

commit v5 on v4

--- a/solution.py
+++ b/solution.py
@@ -72,11 +72,17 @@
         for c in copies:
             c.wait()
 
+    def all_of(view, sem):
+        local(view, view, sem).wait()
+
+    def all_links(view, send, recv):
+        link(view, view, send, recv, 0, 1).wait()
+
     tok_load = local(tokens, tok_v, load_sem.at[0])
     cot_load = local(cotangent, cot_v, load_sem.at[1])
     out_load = local(outproj, out_v, load_sem.at[2])
     gain_loads = [local(mixgain_1d, mixgain.at[0], load_sem.at[3]), local(glugain_1d, glugain.at[0], load_sem.at[4])]
-    in_loads = [local(inproj.at[k], col.at[k, :, pl.ds(0, HALF)], col_sem.at[k, 0]) for k in range(3)]
+    in_loads = [local(inproj.at[k], col.at[k, :, pl.ds(0, HALF)], col_sem.at[3 + k]) for k in range(3)]
     tok_load.start()
     started(gain_loads)
     in_loads[0].start()
@@ -89,14 +95,20 @@
         for m, w in enumerate((gate_w, lift_w)):
             for i in range(4):
                 lanes = pl.ds(128 * block_of(i, s), 128)
-                out.append(local(w.at[:, lanes], col.at[slot, :, pl.ds(SPAN * m + 128 * i, 128)], col_sem.at[slot, 4 * m + i]))
+                out.append(local(w.at[:, lanes], col.at[slot, :, pl.ds(SPAN * m + 128 * i, 128)], col_sem.at[slot]))
         return out
 
     def down_loads(t):
         s, slot = t % STEPS, t % 3
         return [
-            local(down_w.at[pl.ds(128 * block_of(i, s), 128), :], down_ring.at[slot, pl.ds(128 * i, 128), :], down_sem.at[slot, i])
+            local(down_w.at[pl.ds(128 * block_of(i, s), 128), :], down_ring.at[slot, pl.ds(128 * i, 128), :], down_sem.at[slot])
             for i in range(4)]
+
+    def pair_ready(s):
+        all_of(col.at[(s + 1) % 3], col_sem.at[(s + 1) % 3])
+
+    def down_ready(t):
+        all_of(down_ring.at[t % 3], down_sem.at[t % 3])
 
     barrier = pltpu.get_barrier_semaphore()
     for axis in range(3):
@@ -127,8 +139,12 @@
             view = land.at[k, where[0], where[1], where[2]]
             axis = ROUTES[k][phase]
             for step in range(1, 4):
-                out.append(link(view, view, halo_send.at[job, phase, k, step - 1], halo_recv.at[job, phase, k, step - 1], axis, step))
+                out.append(link(view, view, halo_send.at[job, phase], halo_recv.at[job, phase], axis, step))
         return out
+
+    def halo_ready(land, job, phase):
+        view = (land.at[:, pl.ds(0, 3), 0, 0], land.at[:, pl.ds(0, 3), :, 0], land.at[:, pl.ds(0, 3)])[phase]
+        all_links(view, halo_send.at[job, phase], halo_recv.at[job, phase])
 
     def halo_rows(land, slot):
         at = (slot // 16, (slot // 4) % 4, slot % 4)
@@ -146,7 +162,7 @@
     tok_load.wait()
     put_halo(tails, tok_v[BLK - 16:BLK, :].astype(F32)[14:16])
     pl.semaphore_wait(barrier, 10)
-    halo = started(halo_links(tails, 0, 0))
+    started(halo_links(tails, 0, 0))
     waited(gain_loads)
     scale_a, n1 = first_norm(tok_v[...].astype(F32))
     n_v[...] = n1.astype(BF16)
@@ -155,8 +171,8 @@
     started([cot_load])
     for s in range(3):
         started(down_loads(s))
-    waited(halo)
-    halo = started(halo_links(tails, 0, 1))
+    halo_ready(tails, 0, 0)
+    started(halo_links(tails, 0, 1))
     in_loads[2].wait()
     x_v[...] = dot_nn(n_v[...], col[2, :, :HALF])
     v_v[...] = (b_v[...] * x_v[...]).astype(BF16).astype(F32)
@@ -167,12 +183,12 @@
 
     def hidden_grads(first, end):
         for s in range(first, end):
-            waited(down_loads(s))
+            down_ready(s)
             da_v[s] = dot_nt(cot_v[...], down_ring[s % 3])
             started(down_loads(s + 3))
 
-    waited(halo)
-    halo = started(halo_links(tails, 0, 2))
+    halo_ready(tails, 0, 1)
+    started(halo_links(tails, 0, 2))
     s_src[1] = cot_v[...].T
     m_src[0] = n_v[...].T
 
@@ -181,11 +197,11 @@
     def left_link(job, k, src, step):
         left = (s_left, m_left)[job]
         return link(src.at[half, :], left.at[k, half, pl.ds(128 * step, 128)],
-                    l_send.at[job, k, step - 1], l_recv.at[job, k, step - 1], k, step)
+                    l_send.at[job], l_recv.at[job], k, step)
 
     def send_left_s(k):
         src = s_src.at[1 if k == 2 else 0]
-        local(src, s_left.at[k, :, pl.ds(0, 128)], own_left.at[0, k]).start()
+        local(src, s_left.at[k, :, pl.ds(0, 128)], own_left.at[0]).start()
         for step in range(1, 4):
             left_link(0, k, src, step).start()
 
@@ -195,23 +211,20 @@
             def _():
                 left_link(1, k, m_src.at[which], step).start()
 
-    def forward_left(job, k):
-        left = (s_left, m_left)[job]
-        out = []
-        for step in range(1, 4):
-            left_link(job, k, m_src.at[0], step).wait()
-            view = left.at[k, half, pl.ds(128 * step, 128)]
-            out.append(cross(view, view, f_send.at[job, k, step - 1], f_recv.at[job, k, step - 1]))
-            out[-1].start()
-        return out
-
-    send_left_s(2)
-    for k in range(3):
-        send_left_m(k, 0)
+    def others(job):
+        return (s_left, m_left)[job].at[:, half, pl.ds(128, 384)]
+
+    def forward_left(job):
+        all_links(others(job), l_send.at[job], l_recv.at[job])
+        cross(others(job), others(job), f_send.at[job], f_recv.at[job]).start()
+
     started([out_load])
     hidden_grads(0, STEPS)
 
-    waited(halo)
+    halo_ready(tails, 0, 2)
+    send_left_s(2)
+    for k in range(3):
+        send_left_m(k, 0)
     last_two = jnp.concatenate([halo_rows(tails, before), jnp.zeros((14, D), F32)], axis=0)
     edge = first_norm(last_two)[1].astype(BF16)
     edge_b, edge_x = dot_nn(edge, col[0, :, :HALF]), dot_nn(edge, col[2, :, :HALF])
@@ -222,7 +235,7 @@
 
     def edge_left_links(n):
         return [
-            link(e_src, e_left.at[n, pl.ds(16 * step, 16), :], e_send.at[0, n, step - 1], e_recv.at[0, n, step - 1], 2 * n, step)
+            link(e_src, e_left.at[n, pl.ds(16 * step, 16), :], e_send.at[0], e_recv.at[0], 2 * n, step)
             for step in range(1, 4)]
 
     def edge_piece(n, i):
@@ -231,13 +244,13 @@
     def edge_right_links(n):
         return [
             link(edge_piece(n, (place[2 * n] + step) % 4), e_right.at[n, pl.ds(16 * step, 16), :],
-                 e_send.at[1, n, step - 1], e_recv.at[1, n, step - 1], 2 * n, step)
+                 e_send.at[1], e_recv.at[1], 2 * n, step)
             for step in range(1, 4)]
 
     def edge_own(n):
         return [
-            local(e_src, e_left.at[n, pl.ds(0, 16), :], own_edge.at[0, n]),
-            local(edge_piece(n, place[2 * n]), e_right.at[n, pl.ds(0, 16), :], own_edge.at[1, n])]
+            local(e_src, e_left.at[n, pl.ds(0, 16), :], own_edge.at[0]),
+            local(edge_piece(n, place[2 * n]), e_right.at[n, pl.ds(0, 16), :], own_edge.at[1])]
     for s in range(1, 3):
         started(pair_loads(s))
     row_is0, row_is1 = rows == 0, rows == 1
@@ -276,11 +289,11 @@
         lanes = pl.ds(*GROUPS[g])
         return [
             link(right_piece(job, k, (place[k] + step) % 4, g), rights[job].at[k, pl.ds(128 * step, 128), lanes],
-                 r_send.at[job, k, g, step - 1], r_recv.at[job, k, g, step - 1], k, step)
+                 r_send.at[4 * job + g], r_recv.at[4 * job + g], k, step)
             for step in range(1, 4)]
 
     def right_own(job, k, g):
-        return local(right_piece(job, k, place[k], g), rights[job].at[k, pl.ds(0, 128), pl.ds(*GROUPS[g])], own_right.at[job, k, g])
+        return local(right_piece(job, k, place[k], g), rights[job].at[k, pl.ds(0, 128), pl.ds(*GROUPS[g])], own_right.at[4 * job + g])
 
     def send_right(job, g):
         for k in range(3):
@@ -318,27 +331,32 @@
         out = []
         for n in which:
             part, row, land, step = table[n]
+            sem = 2 * (4 * job + g) + (land != 2)
             out.append(link(b_out(job, k, part, g, row, 192), b_in(job, k, land, g, row, 192),
-                            b_send.at[job, k, g, n], b_recv.at[job, k, g, n], axis, step))
+                            b_send.at[sem], b_recv.at[sem], axis, step))
         return out
 
     def c_links(job, k, g):
         axis = (k + 2) % 3
         return [
             link(c_out(job, k, (place[axis] + step) % 4, g), c_in(job, k, step - 1, g),
-                 c_send.at[job, k, g, step - 1], c_recv.at[job, k, g, step - 1], axis, step)
+                 c_send.at[4 * job + g], c_recv.at[4 * job + g], axis, step)
             for step in range(1, 4)]
 
+    def right_ready(job, g):
+        lanes, n = pl.ds(*GROUPS[g]), 4 * job + g
+        all_of(rights[job].at[:, pl.ds(0, 128), lanes], own_right.at[n])
+        all_links(rights[job].at[:, pl.ds(128, 384), lanes], r_send.at[n], r_recv.at[n])
+
+    def edges_ready():
+        all_of(e_left.at[:, pl.ds(0, 16), :], own_edge.at[0])
+        all_of(e_right.at[:, pl.ds(0, 16), :], own_edge.at[1])
+        all_links(e_left.at[:, pl.ds(16, 48), :], e_send.at[0], e_recv.at[0])
+        all_links(e_right.at[:, pl.ds(16, 48), :], e_send.at[1], e_recv.at[1])
+
     def start_b(job, k, g):
-        right_own(job, k, g).wait()
-        waited(right_links(job, k, g))
         lanes = pl.ds(*GROUPS[g])
         edges = job == 1 and k != 1
-        if edges:
-            for c in edge_own(k // 2):
-                c.wait()
-            waited(edge_left_links(k // 2))
-            waited(edge_right_links(k // 2))
 
         def slab(x, carry):
             at = pl.ds(pl.multiple_of(x * HALF, HALF), HALF)
@@ -361,16 +379,29 @@
         lax.fori_loop(0, 2, slab, 0)
         started(b_links(job, k, g, range(4)))
 
+    def b_ready(job, g, last):
+        sem = 2 * (4 * job + g) + last
+        if job == 0:
+            view = s_bland.at[:, pl.ds(0, 2) if last else pl.ds(2, 1), :, pl.ds(*GROUPS[g])]
+        else:
+            view = down_ring.at[pl.ds(0, 2) if last else pl.ds(2, 1), pl.ds(0, 384), pl.ds(0, HALF)]
+        all_links(view, b_send.at[sem], b_recv.at[sem])
+
     def pass_on(job, k, g):
-        waited(b_links(job, k, g, (0, 2)))
         me = place[(k + 1) % 3]
         for step, row in ((1, LOW), (3, HIGH)):
             own, via = b_out(job, k, (me + step) % 4, g, row, 192), b_in(job, k, 2, g, row, 192)
             own[...] = (own[...].astype(F32) + via[...].astype(F32)).astype(BF16)
         started(b_links(job, k, g, (4, 5)))
 
+    def c_ready(job, g):
+        if job == 0:
+            view = s_cland.at[:, :, :, pl.ds(*GROUPS[g])]
+        else:
+            view = down_ring.at[:, pl.ds(0, 96), pl.ds(HALF, HALF)]
+        all_links(view, c_send.at[4 * job + g], c_recv.at[4 * job + g])
+
     def start_c(job, k, g):
-        waited(b_links(job, k, g, (1, 3, 4, 5)))
         me = place[(k + 1) % 3]
 
         def summed(q):
@@ -393,14 +424,13 @@
     def d_links(job, k):
         return [
             link(dsends[job].at[k, (place[k] + step) % 4], dlands[job].at[k, step],
-                 d_send.at[job, k, step - 1], d_recv.at[job, k, step - 1], k, step)
+                 d_send.at[job], d_recv.at[job], k, step)
             for step in range(1, 4)]
 
     def start_d(job, k):
         dsend, dland = dsends[job], dlands[job]
         for g in range(4 if job == 0 else 1):
             first, width = GROUPS[g]
-            waited(c_links(job, k, g))
             total = c_out(job, k, place[(k + 2) % 3], g)[...].astype(F32)
             for i in range(3):
                 total = total + c_in(job, k, i, g)[...].astype(F32)
@@ -411,9 +441,7 @@
         started(d_links(job, k))
 
     def finish(job, k):
-        waited(d_links(job, k))
         stage = (h2_v, glu_v, dn2_v)[k]
-        out = []
         for i in range(4):
             piece = dlands[job][k, (place[k] - i + 4) % 4].astype(F32)[:24]
             at = pl.ds(32 * i, 24)
@@ -426,15 +454,14 @@
                 stage[32 * i:32 * i + 24, 1024:1024 + WM] = piece
                 src = stage.at[at, pl.ds(1024, WM)]
                 dst = o_in.at[k, :, pl.ds(WM * i, WM)] if i < 3 else o_out.at[:, pl.ds(WM * k, WM)]
-            out.append(local(src, dst, store_sem.at[job, k, i]))
-        return started(out)
+            local(src, dst, store_sem.at[k if job == 0 else 3 + (i == 3)]).start()
 
     glu_v[...] = jnp.zeros_like(glu_v)
     dn2_v[...] = jnp.zeros_like(dn2_v)
 
     def swiglu_step(s):
         slot = (s + 1) % 3
-        waited(pair_loads(s))
+        pair_ready(s)
         both = dot_nn(n_v[...], col[slot])
         gate_pre, lift_pre = both[:, :SPAN], both[:, SPAN:]
         hidden_grad = da_v[s]
@@ -452,33 +479,35 @@
                 return values
             return jnp.concatenate([values[:, :256], jnp.zeros((BLK, 128), BF16), values[:, 384:]], axis=1)
 
-        waited(down_loads(STEPS + s))
+        down_ready(STEPS + s)
         glu_v[...] += dot_nn(once(hidden), down_ring[(STEPS + s) % 3])
         dn2_v[...] += dot_nt(jnp.concatenate([once(d_gate), once(d_lift)], axis=1), col[slot])
         if s + 3 < STEPS:
             started(pair_loads(s + 3))
             started(down_loads(STEPS + s + 3))
 
-    def left_ready(job, fwd):
-        for k in range(3):
-            local(m_src.at[0], lefts[job].at[k, :, pl.ds(0, 128)], own_left.at[job, k]).wait()
-            waited(fwd[k])
+    def left_ready(job):
+        all_of(lefts[job].at[:, :, pl.ds(0, 128)], own_left.at[job])
+        cross(others(job), others(job), f_send.at[job], f_recv.at[job]).wait()
 
     for s in range(2):
         swiglu_step(s)
     send_right(0, 0)
     swiglu_step(2)
-    fwd = [forward_left(0, k) for k in range(3)]
+    forward_left(0)
     swiglu_step(3)
     send_right(0, 1)
-    left_ready(0, fwd)
+    left_ready(0)
+    right_ready(0, 0)
     for k in range(3):
         start_b(0, k, 0)
     swiglu_step(4)
     swiglu_step(5)
     send_right(0, 2)
+    right_ready(0, 1)
     for k in range(3):
         start_b(0, k, 1)
+    b_ready(0, 0, 0)
     for k in range(3):
         pass_on(0, k, 0)
     swiglu_step(6)
@@ -527,19 +556,23 @@
     m_src[1] = n_v[...].T
     for k in range(3):
         send_left_m(k, 1)
-        local(m_src.at[jnp.where(place[k] == 3, 1, 0)], m_left.at[k, :, pl.ds(0, 128)], own_left.at[1, k]).start()
-    halo = started(halo_links(heads, 1, 0))
+        local(m_src.at[jnp.where(place[k] == 3, 1, 0)], m_left.at[k, :, pl.ds(0, 128)], own_left.at[1]).start()
+    started(halo_links(heads, 1, 0))
     swap_glu.wait()
     xh_send[1] = (h2_v[...] + (xh_send[1].astype(F32) + xh_recv[1].astype(F32))).astype(BF16)
     stores = started([local(xh_send.at[1], o_layer, load_sem.at[5])])
+    right_ready(0, 2)
     for k in range(3):
         start_b(0, k, 2)
+    b_ready(0, 1, 0)
     for k in range(3):
         pass_on(0, k, 1)
-    waited(halo)
-    halo = started(halo_links(heads, 1, 1))
+    halo_ready(heads, 1, 0)
+    started(halo_links(heads, 1, 1))
+    right_ready(0, 3)
     for k in range(3):
         start_b(0, k, 3)
+    b_ready(0, 2, 0)
     for k in range(3):
         pass_on(0, k, 2)
 
@@ -550,17 +583,21 @@
             dn2_v[...] = part
         else:
             dn2_v[...] += part
-    waited(halo)
-    halo = started(halo_links(heads, 1, 2))
-    fwd = [forward_left(1, k) for k in range(3)]
-    left_ready(1, fwd)
+    halo_ready(heads, 1, 1)
+    started(halo_links(heads, 1, 2))
+    forward_left(1)
+    left_ready(1)
+    right_ready(1, 0)
+    edges_ready()
     for k in range(3):
         start_b(1, k, 0)
+    b_ready(0, 3, 0)
     for k in range(3):
         pass_on(0, k, 3)
+    b_ready(0, 0, 1)
     for k in range(3):
         start_c(0, k, 0)
-    waited(halo)
+    halo_ready(heads, 1, 2)
     incoming = jnp.concatenate([jnp.zeros((14, HALF), F32), halo_rows(heads, after) * has_after], axis=0)
     extra = dot_nt((incoming * x_v[BLK - 16:, :]).astype(BF16), col[0, :, :HALF])
     extra += dot_nt((incoming * b_v[BLK - 16:, :]).astype(BF16), col[2, :, :HALF])
@@ -568,8 +605,10 @@
     xh_send[0] = dn2_v[...].astype(BF16)
     swap = cross(xh_send.at[0], xh_recv.at[0], x_send.at[3], x_recv.at[3])
     swap.start()
+    b_ready(1, 0, 0)
     for k in range(3):
         pass_on(1, k, 0)
+    b_ready(0, 1, 1)
     for k in range(3):
         start_c(0, k, 1)
     swap.wait()
@@ -585,36 +624,43 @@
 
     def gain_links(axis):
         view = gain_land.at[axis, place[axis]]
-        return [link(view, view, gain_send.at[axis, step - 1], gain_recv.at[axis, step - 1], axis, step) for step in range(1, 4)]
+        return [link(view, view, gain_send.at[axis], gain_recv.at[axis], axis, step) for step in range(1, 4)]
 
     def gain_sum(axis):
+        all_links(gain_land.at[axis, pl.ds(0, 3)], gain_send.at[axis], gain_recv.at[axis])
         return (gain_land[axis, 0] + gain_land[axis, 1]) + (gain_land[axis, 2] + gain_land[axis, 3])
 
     gain_land[0, place[0]] = jnp.concatenate(
         [my_half(mix_term), my_half(glu_term), *tap_terms, jnp.zeros((3, HALF), F32)], axis=0)
-    gains = started(gain_links(0))
+    started(gain_links(0))
+    b_ready(0, 2, 1)
     for k in range(3):
         start_c(0, k, 2)
-    waited(gains)
     gain_land[1, place[1]] = gain_sum(0)
-    gains = started(gain_links(1))
+    started(gain_links(1))
+    b_ready(0, 3, 1)
     for k in range(3):
         start_c(0, k, 3)
+    b_ready(1, 0, 1)
     for k in range(3):
         start_c(1, k, 0)
-    waited(gains)
     gain_land[2, place[2]] = gain_sum(1)
-    gains = started(gain_links(2))
+    started(gain_links(2))
+    for g in range(4):
+        c_ready(0, g)
     for k in range(3):
         start_d(0, k)
-    waited(gains)
     v_v[0:8, :] = gain_sum(2)
     stores += started([local(v_v.at[pl.ds(0, 8), :], o_gains, load_sem.at[7])])
+    c_ready(1, 0)
     for k in range(3):
         start_d(1, k)
     for job in range(2):
+        all_links(dlands[job].at[:, pl.ds(1, 3)], d_send.at[job], d_recv.at[job])
         for k in range(3):
-            stores += finish(job, k)
+            finish(job, k)
+    for n, out in enumerate((o_gate, o_lift, o_down, o_in, o_out)):
+        all_of(out, store_sem.at[n])
     waited(stores)
 
 
@@ -649,11 +695,12 @@
             pltpu.VMEM((3, 4, 32, WS), BF16), pltpu.VMEM((3, 4, 32, WS), BF16),
             pltpu.VMEM((3, D, 512), BF16), pltpu.VMEM((3, 512, WM), BF16),
             pltpu.VMEM((3, 4, 32, WM), BF16), pltpu.VMEM((3, 4, 32, WM), BF16),
-            dma((8,)), dma((3, 8)), dma((3, 4)), dma((2, 3, 4)), dma((4,)), dma((4,)),
-            dma((2, 3, 3, 3)), dma((2, 3, 3, 3)), dma((3, 3)), dma((3, 3)),
-        ]
-        + [dma((2, 3, 3))] * 4 + [dma((2, 3, 4, 3))] * 2 + [dma((2, 3, 4, 6))] * 2 + [dma((2, 3, 4, 3))] * 2 + [dma((2, 3, 3))] * 2
-        + [dma((2, 3)), dma((2, 3, 4)), dma((2, 2, 3)), dma((2, 2, 3)), dma((2, 2))],
+            dma((8,)), dma((6,)), dma((3,)), dma((5,)), dma((4,)), dma((4,)),
+            dma((2, 3)), dma((2, 3)), dma((3,)), dma((3,)),
+            dma((2,)), dma((2,)), dma((2,)), dma((2,)), dma((5,)), dma((5,)),
+            dma((10,)), dma((10,)), dma((5,)), dma((5,)), dma((2,)), dma((2,)),
+            dma((2,)), dma((5,)), dma((2,)), dma((2,)), dma((2,)),
+        ],
         compiler_params=pltpu.CompilerParams(collective_id=1, has_side_effects=True, vmem_limit_bytes=LIMIT),
         name="layer",
     )(seq_lengths, block_slots, mixgain, glugain, taps, tokens, cotangent, inproj, outproj, gate_w, lift_w, down_w)

time: 131 us -> 124 us (0.947)
  Pallas kernels: 130 us -> 123 us
    pallas_call x1, Pallas kernels: 127 us -> 120 us  [run_layer(): pl.pallas_call(layer_kernel, out_shape=[shape((BLK, D), BF16), shape((BLK...]
where the time goes in v5:
time: 124 us
  Pallas kernels  123 us (99%)
    pallas_call x1, Pallas kernels, run_layer(): pl.pallas_call(layer_kernel, out_shape=[shape((BLK, D), BF16), shape((BLK...  120 us

profile of v5, /device:TPU:0, one launch (start us, length us, event | category | flops | bytes accessed | tf_op | source)
XLA Modules:
  0.0 123.7 jit_solution(7683846334403558675)
XLA Ops:
  0.6 120.4 %layer.1 = (bf16[128,1536]{1,0:T(8,128)(2,1)}, bf16[128,1536]{1,0:T(8,128)(2,1)}, f32[8,768]{1,0:T(8,128)}, f32[24,3456]{1,0:T(8,128)}, f32[24,3456]{1,0:T(8,128...) custom-call(s32[4]{0:T(128)} %seq_lengths.1, s32[64]{0:T(128)} %block_slots.1, f32[1536]{0:T(1024)} %mixgain_1d.1, ...), custom_call_target="tpu_custom_call" | custom-call | tf_op jit(solution)/shard_map/layer/pallas_call | solution.py:675
  121.0 2.5 %place.1 = (bf16[128,1536]{1,0:T(8,128)(2,1)}, bf16[128,1536]{1,0:T(8,128)(2,1)}, f32[768]{0:T(1024)}, f32[768]{0:T(1024)}, f32[3,768]{1,0:T(4,128)}, /*index=5*...) custom-call(bf16[128,1536]{1,0:T(8,128)(2,1)} %get-tuple-element.28.refs_0, ...), custom_call_target="tpu_custom_call" | custom-call | tf_op jit(solution)/shard_map/place/pallas_call | solution.py:729

commit v6 on v5

--- a/solution.py
+++ b/solution.py
@@ -13,7 +13,7 @@
 EPS = 1e-05
 LIMIT = 64 * 1024 * 1024 - 256 * 1024
 ROUTES = ((2, 1, 0), (0, 2, 1), (1, 0, 2))
-GROUPS = ((0, 256), (256, 256), (512, 256), (768, 128))
+GROUPS = (((0, 256), (256, 256), (512, 256), (768, 128)), ((0, 256),))
 
 
 def dot_nt(a, b):
@@ -28,8 +28,8 @@
     return jnp.dot(a, b, preferred_element_type=F32)
 
 
-def block_of(i, s):
-    return min(7 * i, 20) + s
+def span(s):
+    return min(SPAN, FF - SPAN * s)
 
 
 def layer_kernel(
@@ -37,11 +37,11 @@
     tokens, cotangent, inproj, outproj, gate_w, lift_w, down_w,
     o_layer, o_input, o_gains, o_gate, o_lift, o_down, o_in, o_out,
     mixgain, glugain, tok_v, cot_v, n_v, b_v, c_v, x_v, v_v, u_v, y_v, h2_v, glu_v, dn2_v,
-    col, down_ring, out_v, da_v, act, mixed_r, s_src, m_src, e_src, eb_v, ex_v, er_src, e_left, e_right, xh_send, xh_recv, tails, heads, gain_land,
+    col, down_ring, out_v, da_v, act, mixed_r, s_src, m_src, e_src, eb_v, ex_v, er_src, e_left, e_right, xh_send, xh_recv, xs_send, tails, heads, gain_land,
     s_left, s_right, s_bsend, s_bland, s_cland, s_dsend, s_dland, m_left, m_right, m_dsend, m_dland,
     load_sem, col_sem, down_sem, store_sem, x_send, x_recv, halo_send, halo_recv, gain_send, gain_recv,
     l_send, l_recv, f_send, f_recv, r_send, r_recv,
-    b_send, b_recv, c_send, c_recv, d_send, d_recv, own_left, own_right, e_send, e_recv, own_edge,
+    b_send, b_recv, c_send, c_recv, d_send, d_recv, e_send, e_recv, own_edge,
 ):
     seq, core = lax.axis_index("seq"), lax.axis_index("ch")
     place = (seq // 16, (seq // 4) % 4, seq % 4)
@@ -90,25 +90,20 @@
     in_loads[1].start()
 
     def pair_loads(s):
-        slot = (s + 1) % 3
-        out = []
-        for m, w in enumerate((gate_w, lift_w)):
-            for i in range(4):
-                lanes = pl.ds(128 * block_of(i, s), 128)
-                out.append(local(w.at[:, lanes], col.at[slot, :, pl.ds(SPAN * m + 128 * i, 128)], col_sem.at[slot]))
-        return out
+        slot, w = (s + 1) % 3, span(s)
+        return [
+            local(weight.at[:, pl.ds(SPAN * s, w)], col.at[slot, :, pl.ds(w * m, w)], col_sem.at[slot])
+            for m, weight in enumerate((gate_w, lift_w))]
 
     def down_loads(t):
         s, slot = t % STEPS, t % 3
-        return [
-            local(down_w.at[pl.ds(128 * block_of(i, s), 128), :], down_ring.at[slot, pl.ds(128 * i, 128), :], down_sem.at[slot])
-            for i in range(4)]
+        return [local(down_w.at[pl.ds(SPAN * s, span(s)), :], down_ring.at[slot, pl.ds(0, span(s)), :], down_sem.at[slot])]
 
     def pair_ready(s):
-        all_of(col.at[(s + 1) % 3], col_sem.at[(s + 1) % 3])
+        all_of(col.at[(s + 1) % 3, :, pl.ds(0, 2 * span(s))], col_sem.at[(s + 1) % 3])
 
     def down_ready(t):
-        all_of(down_ring.at[t % 3], down_sem.at[t % 3])
+        all_of(down_ring.at[t % 3, pl.ds(0, span(t % STEPS)), :], down_sem.at[t % 3])
 
     barrier = pltpu.get_barrier_semaphore()
     for axis in range(3):
@@ -184,7 +179,7 @@
     def hidden_grads(first, end):
         for s in range(first, end):
             down_ready(s)
-            da_v[s] = dot_nt(cot_v[...], down_ring[s % 3])
+            da_v[:, SPAN * s:SPAN * s + span(s)] = dot_nt(cot_v[...], down_ring[s % 3, :span(s), :])
             started(down_loads(s + 3))
 
     halo_ready(tails, 0, 1)
@@ -201,7 +196,7 @@
 
     def send_left_s(k):
         src = s_src.at[1 if k == 2 else 0]
-        local(src, s_left.at[k, :, pl.ds(0, 128)], own_left.at[0]).start()
+        s_left[k, :, :128] = src[...]
         for step in range(1, 4):
             left_link(0, k, src, step).start()
 
@@ -219,14 +214,16 @@
         cross(others(job), others(job), f_send.at[job], f_recv.at[job]).start()
 
     started([out_load])
-    hidden_grads(0, STEPS)
+    hidden_grads(0, 4)
 
     halo_ready(tails, 0, 2)
     send_left_s(2)
     for k in range(3):
         send_left_m(k, 0)
     last_two = jnp.concatenate([halo_rows(tails, before), jnp.zeros((14, D), F32)], axis=0)
-    edge = first_norm(last_two)[1].astype(BF16)
+    edge_scale, edge = first_norm(last_two)
+    xs_send[1] = last_two * edge_scale
+    edge = edge.astype(BF16)
     edge_b, edge_x = dot_nn(edge, col[0, :, :HALF]), dot_nn(edge, col[2, :, :HALF])
     carried = (edge_b * edge_x).astype(BF16).astype(F32)
     e_src[...] = edge
@@ -269,6 +266,7 @@
     dn2_v[...] = dot_nn(y_v[...], out_v[...])
     swap = cross(dn2_v, h2_v, x_send.at[0], x_recv.at[0])
     swap.start()
+    hidden_grads(4, 6)
     swap.wait()
     h2_v[...] = tok_v[...].astype(F32) + (dn2_v[...] + h2_v[...])
     h2 = h2_v[...]
@@ -282,41 +280,40 @@
 
     def right_piece(job, k, i, g):
         if job == 0:
-            return act.at[k, i, :, pl.ds(*GROUPS[g])]
+            return act.at[k, i, :, pl.ds(*GROUPS[0][g])]
         return mixed_r.at[k, :, pl.ds(pl.multiple_of(i * WM, WM), WM)]
 
     def right_links(job, k, g):
-        lanes = pl.ds(*GROUPS[g])
+        lanes = pl.ds(*GROUPS[job][g])
         return [
             link(right_piece(job, k, (place[k] + step) % 4, g), rights[job].at[k, pl.ds(128 * step, 128), lanes],
                  r_send.at[4 * job + g], r_recv.at[4 * job + g], k, step)
             for step in range(1, 4)]
 
-    def right_own(job, k, g):
-        return local(right_piece(job, k, place[k], g), rights[job].at[k, pl.ds(0, 128), pl.ds(*GROUPS[g])], own_right.at[4 * job + g])
-
     def send_right(job, g):
         for k in range(3):
-            right_own(job, k, g).start()
             started(right_links(job, k, g))
+        first, width = GROUPS[job][g]
+        for k in range(3):
+            rights[job][k, :128, first:first + width] = right_piece(job, k, place[k], g)[...]
 
     def b_out(job, k, j, g, row=0, count=384):
-        lanes = pl.ds(*GROUPS[g])
+        lanes = pl.ds(*GROUPS[job][g])
         if job == 0:
             return s_bsend.at[k, j, pl.ds(row, count), lanes]
         return col.at[1, pl.ds(pl.multiple_of(384 * j + row, 96), count), pl.ds(WM * k, WM)]
 
     def b_in(job, k, i, g, row=0, count=384):
         if job == 0:
-            return s_bland.at[k, i, pl.ds(row, count), pl.ds(*GROUPS[g])]
+            return s_bland.at[k, i, pl.ds(row, count), pl.ds(*GROUPS[job][g])]
         return down_ring.at[i, pl.ds(row, count), pl.ds(WM * k, WM)]
 
     def c_out(job, k, j, g, row=0, count=96):
-        return rights[job].at[k, pl.ds(pl.multiple_of(96 * j + row, 48), count), pl.ds(*GROUPS[g])]
+        return rights[job].at[k, pl.ds(pl.multiple_of(96 * j + row, 48), count), pl.ds(*GROUPS[job][g])]
 
     def c_in(job, k, i, g):
         if job == 0:
-            return s_cland.at[k, i, :, pl.ds(*GROUPS[g])]
+            return s_cland.at[k, i, :, pl.ds(*GROUPS[job][g])]
         return down_ring.at[i, pl.ds(0, 96), pl.ds(HALF + WM * k, WM)]
 
     LOW, HIGH = 0, 192
@@ -344,8 +341,7 @@
             for step in range(1, 4)]
 
     def right_ready(job, g):
-        lanes, n = pl.ds(*GROUPS[g]), 4 * job + g
-        all_of(rights[job].at[:, pl.ds(0, 128), lanes], own_right.at[n])
+        lanes, n = pl.ds(*GROUPS[job][g]), 4 * job + g
         all_links(rights[job].at[:, pl.ds(128, 384), lanes], r_send.at[n], r_recv.at[n])
 
     def edges_ready():
@@ -355,34 +351,32 @@
         all_links(e_right.at[:, pl.ds(16, 48), :], e_send.at[1], e_recv.at[1])
 
     def start_b(job, k, g):
-        lanes = pl.ds(*GROUPS[g])
+        lanes = pl.ds(*GROUPS[job][g])
         edges = job == 1 and k != 1
 
         def slab(x, carry):
-            at = pl.ds(pl.multiple_of(x * HALF, HALF), HALF)
+            at = pl.ds(pl.multiple_of(x * 384, 384), 384)
             acc = dot_nn(lefts[job][k, at, :], rights[job][k, :, lanes])
             if edges:
                 acc = acc + outer(e_left[k // 2, :, at], e_right[k // 2])
-            for h in range(2):
-                row = pl.multiple_of(192 * x + 96 * h, 96)
-                for j in range(4):
-                    base = 384 * h + 96 * j
-                    if k == 0:
-                        b_out(job, k, j, g, row, 96)[...] = acc[base:base + 96].astype(BF16)
-                    elif k == 1:
-                        parts = [acc[384 * h + 96 * y + 24 * j:384 * h + 96 * y + 24 * j + 24] for y in range(4)]
-                        b_out(job, k, j, g, row, 96)[...] = jnp.concatenate(parts, axis=0).astype(BF16)
-                    else:
-                        b_out(job, k, 2 * x + h, g, 96 * j, 96)[...] = acc[base:base + 96].astype(BF16)
+            row = pl.multiple_of(96 * x, 96)
+            for j in range(4):
+                if k == 0:
+                    b_out(job, k, j, g, row, 96)[...] = acc[96 * j:96 * j + 96].astype(BF16)
+                elif k == 1:
+                    parts = [acc[96 * y + 24 * j:96 * y + 24 * j + 24] for y in range(4)]
+                    b_out(job, k, j, g, row, 96)[...] = jnp.concatenate(parts, axis=0).astype(BF16)
+                else:
+                    b_out(job, k, x, g, 96 * j, 96)[...] = acc[96 * j:96 * j + 96].astype(BF16)
             return carry
 
-        lax.fori_loop(0, 2, slab, 0)
+        lax.fori_loop(0, 4, slab, 0)
         started(b_links(job, k, g, range(4)))
 
     def b_ready(job, g, last):
         sem = 2 * (4 * job + g) + last
         if job == 0:
-            view = s_bland.at[:, pl.ds(0, 2) if last else pl.ds(2, 1), :, pl.ds(*GROUPS[g])]
+            view = s_bland.at[:, pl.ds(0, 2) if last else pl.ds(2, 1), :, pl.ds(*GROUPS[job][g])]
         else:
             view = down_ring.at[pl.ds(0, 2) if last else pl.ds(2, 1), pl.ds(0, 384), pl.ds(0, HALF)]
         all_links(view, b_send.at[sem], b_recv.at[sem])
@@ -396,7 +390,7 @@
 
     def c_ready(job, g):
         if job == 0:
-            view = s_cland.at[:, :, :, pl.ds(*GROUPS[g])]
+            view = s_cland.at[:, :, :, pl.ds(*GROUPS[job][g])]
         else:
             view = down_ring.at[:, pl.ds(0, 96), pl.ds(HALF, HALF)]
         all_links(view, c_send.at[4 * job + g], c_recv.at[4 * job + g])
@@ -429,8 +423,7 @@
 
     def start_d(job, k):
         dsend, dland = dsends[job], dlands[job]
-        for g in range(4 if job == 0 else 1):
-            first, width = GROUPS[g]
+        for g, (first, width) in enumerate(GROUPS[job]):
             total = c_out(job, k, place[(k + 2) % 3], g)[...].astype(F32)
             for i in range(3):
                 total = total + c_in(job, k, i, g)[...].astype(F32)
@@ -441,20 +434,19 @@
         started(d_links(job, k))
 
     def finish(job, k):
-        stage = (h2_v, glu_v, dn2_v)[k]
-        for i in range(4):
-            piece = dlands[job][k, (place[k] - i + 4) % 4].astype(F32)[:24]
-            at = pl.ds(32 * i, 24)
-            if job == 0:
-                stage[32 * i:32 * i + 24, :WS] = piece
-                skip = 0 if i < 3 else 4 * WS - FF
-                src = stage.at[at, pl.ds(skip, WS - skip)]
-                dst = (o_gate, o_lift, o_down)[k].at[:, pl.ds(WS * i, WS - skip)]
-            else:
-                stage[32 * i:32 * i + 24, 1024:1024 + WM] = piece
-                src = stage.at[at, pl.ds(1024, WM)]
-                dst = o_in.at[k, :, pl.ds(WM * i, WM)] if i < 3 else o_out.at[:, pl.ds(WM * k, WM)]
-            local(src, dst, store_sem.at[k if job == 0 else 3 + (i == 3)]).start()
+        pieces = [dlands[job][k, (place[k] - i + 4) % 4].astype(F32)[:24] for i in range(4)]
+        if job == 0:
+            for i in range(4):
+                for s in range(STEPS):
+                    if SPAN * s + 128 * i < FF:
+                        da_v[32 * k:32 * k + 24, SPAN * s + 128 * i:SPAN * s + 128 * i + 128] = pieces[i][:, 128 * s:128 * s + 128]
+            local(da_v.at[pl.ds(32 * k, 24), :], (o_gate, o_lift, o_down)[k], store_sem.at[k]).start()
+        else:
+            stage = (h2_v, glu_v, dn2_v)[k]
+            for i in range(4):
+                stage[:24, WM * i:WM * i + WM] = pieces[i]
+            local(stage.at[pl.ds(0, 24), pl.ds(0, HALF)], o_in.at[k], store_sem.at[3]).start()
+            local(stage.at[pl.ds(0, 24), pl.ds(HALF, WM)], o_out.at[:, pl.ds(WM * k, WM)], store_sem.at[4]).start()
 
     glu_v[...] = jnp.zeros_like(glu_v)
     dn2_v[...] = jnp.zeros_like(dn2_v)
@@ -462,46 +454,42 @@
     def swiglu_step(s):
         slot = (s + 1) % 3
         pair_ready(s)
-        both = dot_nn(n_v[...], col[slot])
-        gate_pre, lift_pre = both[:, :SPAN], both[:, SPAN:]
-        hidden_grad = da_v[s]
+        w = span(s)
+        both = dot_nn(n_v[...], col[slot, :, :2 * w])
+        gate_pre, lift_pre = both[:, :w], both[:, w:]
+        hidden_grad = da_v[:, SPAN * s:SPAN * s + w]
         sig = jax.nn.sigmoid(gate_pre)
         silu = gate_pre * sig
         hidden = (silu * lift_pre).astype(BF16)
         d_lift = (hidden_grad * silu).astype(BF16)
         d_gate = (hidden_grad * lift_pre * sig * (1.0 + gate_pre * (1.0 - sig))).astype(BF16)
-        for i in range(4):
-            for k, values in enumerate((d_gate, d_lift, hidden)):
-                act[k, i, :, 128 * s:128 * s + 128] = values[:, 128 * i:128 * i + 128]
-
-        def once(values):
-            if s < STEPS - 1:
-                return values
-            return jnp.concatenate([values[:, :256], jnp.zeros((BLK, 128), BF16), values[:, 384:]], axis=1)
-
+        for k, values in enumerate((d_gate, d_lift, hidden)):
+            for i in range(4):
+                part = values[:, 128 * i:128 * i + 128] if 128 * i < w else jnp.zeros((BLK, 128), BF16)
+                act[k, i, :, 128 * s:128 * s + 128] = part
         down_ready(STEPS + s)
-        glu_v[...] += dot_nn(once(hidden), down_ring[(STEPS + s) % 3])
-        dn2_v[...] += dot_nt(jnp.concatenate([once(d_gate), once(d_lift)], axis=1), col[slot])
+        glu_v[...] += dot_nn(hidden, down_ring[(STEPS + s) % 3, :w, :])
+        dn2_v[...] += dot_nt(jnp.concatenate([d_gate, d_lift], axis=1), col[slot, :, :2 * w])
         if s + 3 < STEPS:
             started(pair_loads(s + 3))
             started(down_loads(STEPS + s + 3))
 
     def left_ready(job):
-        all_of(lefts[job].at[:, :, pl.ds(0, 128)], own_left.at[job])
         cross(others(job), others(job), f_send.at[job], f_recv.at[job]).wait()
 
+    hidden_grads(6, STEPS)
     for s in range(2):
         swiglu_step(s)
     send_right(0, 0)
-    swiglu_step(2)
+    for s in range(2, 4):
+        swiglu_step(s)
+    send_right(0, 1)
     forward_left(0)
-    swiglu_step(3)
-    send_right(0, 1)
+    swiglu_step(4)
     left_ready(0)
     right_ready(0, 0)
     for k in range(3):
         start_b(0, k, 0)
-    swiglu_step(4)
     swiglu_step(5)
     send_right(0, 2)
     right_ready(0, 1)
@@ -536,6 +524,7 @@
     w1, w2 = tap1 * (du * mask1), tap2 * (du * mask2)
     two = jnp.concatenate([w2[0:1], w1[0:1] + w2[1:2]], axis=0)
     put_halo(heads, two)
+    started(halo_links(heads, 1, 0))
     dv = (tap0 * du + jnp.where(rows < 127, pltpu.roll(w1, 127, 0), 0.0)
           + jnp.where(rows < 126, pltpu.roll(w2, 126, 0), 0.0))
     mixed_r[0, :, :HALF] = (dv * x_v[...]).astype(BF16)
@@ -556,25 +545,36 @@
     m_src[1] = n_v[...].T
     for k in range(3):
         send_left_m(k, 1)
-        local(m_src.at[jnp.where(place[k] == 3, 1, 0)], m_left.at[k, :, pl.ds(0, 128)], own_left.at[1]).start()
-    started(halo_links(heads, 1, 0))
+        m_left[k, :, :128] = m_src[jnp.where(place[k] == 3, 1, 0)]
+    b_ready(0, 1, 0)
+    for k in range(3):
+        pass_on(0, k, 1)
+    right_ready(0, 2)
+    for k in range(3):
+        start_b(0, k, 2)
     swap_glu.wait()
     xh_send[1] = (h2_v[...] + (xh_send[1].astype(F32) + xh_recv[1].astype(F32))).astype(BF16)
     stores = started([local(xh_send.at[1], o_layer, load_sem.at[5])])
-    right_ready(0, 2)
-    for k in range(3):
-        start_b(0, k, 2)
-    b_ready(0, 1, 0)
-    for k in range(3):
-        pass_on(0, k, 1)
-    halo_ready(heads, 1, 0)
-    started(halo_links(heads, 1, 1))
-    right_ready(0, 3)
-    for k in range(3):
-        start_b(0, k, 3)
-    b_ready(0, 2, 0)
-    for k in range(3):
-        pass_on(0, k, 2)
+    b_ready(0, 0, 1)
+    for k in range(3):
+        start_c(0, k, 0)
+
+    def my_half(row):
+        return jnp.where(core == 0, row[:, :HALF], row[:, HALF:])
+
+    def gain_links(axis):
+        view = gain_land.at[axis, place[axis]]
+        return [link(view, view, gain_send.at[axis], gain_recv.at[axis], axis, step) for step in range(1, 4)]
+
+    def gain_sum(axis):
+        all_links(gain_land.at[axis, pl.ds(0, 3)], gain_send.at[axis], gain_recv.at[axis])
+        return (gain_land[axis, 0] + gain_land[axis, 1]) + (gain_land[axis, 2] + gain_land[axis, 3])
+
+    def input_rows(dn1, first):
+        z1 = tok_v[first:, :].astype(F32) * scale_a[first:]
+        scaled = dn1 * mixgain[...]
+        n_v[first:, :] = (glu_v[first:, :] + scale_a[first:] * (scaled - z1 * jnp.mean(scaled * z1, axis=1, keepdims=True))).astype(BF16)
+        return z1
 
     waited(in_loads)
     for k in range(3):
@@ -583,75 +583,73 @@
             dn2_v[...] = part
         else:
             dn2_v[...] += part
+    ahead = dot_nt(er_src[0, :, :HALF], col[0, :, :HALF]) + dot_nt(er_src[1, :, :HALF], col[2, :, :HALF])
+    swap_dn1 = cross(dn2_v, da_v.at[:, pl.ds(0, D)], x_send.at[3], x_recv.at[3])
+    swap_dn1.start()
+    xs_send[0] = jnp.concatenate([jnp.sum(ahead * xs_send[1], axis=0, keepdims=True), jnp.zeros((15, D), F32)], axis=0)
+    swap_row = cross(xs_send.at[0], da_v.at[pl.ds(0, 16), pl.ds(D, D)], x_send.at[4], x_recv.at[4])
+    swap_row.start()
+    right_ready(0, 3)
+    for k in range(3):
+        start_b(0, k, 3)
+    halo_ready(heads, 1, 0)
+    started(halo_links(heads, 1, 1))
+    swap_dn1.wait()
+    swap_row.wait()
+    dn1 = dn2_v[...] + da_v[:, :D]
+    z1 = input_rows(dn1, 0)
+    mix_term = jnp.sum(dn1 * z1, axis=0, keepdims=True) + (xs_send[0, 0:1] + da_v[0:1, D:2 * D])
+    gain_land[0, place[0]] = jnp.concatenate(
+        [my_half(mix_term), my_half(glu_term), *tap_terms, jnp.zeros((3, HALF), F32)], axis=0)
+    started(gain_links(0))
+    forward_left(1)
+    b_ready(0, 2, 0)
+    for k in range(3):
+        pass_on(0, k, 2)
+    b_ready(0, 1, 1)
+    for k in range(3):
+        start_c(0, k, 1)
+    b_ready(0, 3, 0)
+    for k in range(3):
+        pass_on(0, k, 3)
     halo_ready(heads, 1, 1)
     started(halo_links(heads, 1, 2))
-    forward_left(1)
     left_ready(1)
     right_ready(1, 0)
     edges_ready()
     for k in range(3):
         start_b(1, k, 0)
-    b_ready(0, 3, 0)
-    for k in range(3):
-        pass_on(0, k, 3)
-    b_ready(0, 0, 1)
-    for k in range(3):
-        start_c(0, k, 0)
+    gain_land[1, place[1]] = gain_sum(0)
+    started(gain_links(1))
+    b_ready(0, 2, 1)
+    for k in range(3):
+        start_c(0, k, 2)
+    b_ready(1, 0, 0)
+    for k in range(3):
+        pass_on(1, k, 0)
+    b_ready(0, 3, 1)
+    for k in range(3):
+        start_c(0, k, 3)
+    gain_land[2, place[2]] = gain_sum(1)
+    started(gain_links(2))
     halo_ready(heads, 1, 2)
     incoming = jnp.concatenate([jnp.zeros((14, HALF), F32), halo_rows(heads, after) * has_after], axis=0)
-    extra = dot_nt((incoming * x_v[BLK - 16:, :]).astype(BF16), col[0, :, :HALF])
-    extra += dot_nt((incoming * b_v[BLK - 16:, :]).astype(BF16), col[2, :, :HALF])
-    dn2_v[BLK - 16:, :] += extra
-    xh_send[0] = dn2_v[...].astype(BF16)
-    swap = cross(xh_send.at[0], xh_recv.at[0], x_send.at[3], x_recv.at[3])
+    xs_send[1] = (dot_nt((incoming * x_v[BLK - 16:, :]).astype(BF16), col[0, :, :HALF])
+                  + dot_nt((incoming * b_v[BLK - 16:, :]).astype(BF16), col[2, :, :HALF]))
+    swap = cross(xs_send.at[1], da_v.at[pl.ds(16, 16), pl.ds(D, D)], x_send.at[5], x_recv.at[5])
     swap.start()
-    b_ready(1, 0, 0)
-    for k in range(3):
-        pass_on(1, k, 0)
-    b_ready(0, 1, 1)
-    for k in range(3):
-        start_c(0, k, 1)
+    b_ready(1, 0, 1)
+    for k in range(3):
+        start_c(1, k, 0)
     swap.wait()
-    dn1 = xh_send[0].astype(F32) + xh_recv[0].astype(F32)
-    z1 = tok_v[...].astype(F32) * scale_a
-    mix_term = jnp.sum(dn1 * z1, axis=0, keepdims=True)
-    scaled = dn1 * mixgain[...]
-    xh_send[0] = (glu_v[...] + scale_a * (scaled - z1 * jnp.mean(scaled * z1, axis=1, keepdims=True))).astype(BF16)
-    stores += started([local(xh_send.at[0], o_input, load_sem.at[6])])
-
-    def my_half(row):
-        return jnp.where(core == 0, row[:, :HALF], row[:, HALF:])
-
-    def gain_links(axis):
-        view = gain_land.at[axis, place[axis]]
-        return [link(view, view, gain_send.at[axis], gain_recv.at[axis], axis, step) for step in range(1, 4)]
-
-    def gain_sum(axis):
-        all_links(gain_land.at[axis, pl.ds(0, 3)], gain_send.at[axis], gain_recv.at[axis])
-        return (gain_land[axis, 0] + gain_land[axis, 1]) + (gain_land[axis, 2] + gain_land[axis, 3])
-
-    gain_land[0, place[0]] = jnp.concatenate(
-        [my_half(mix_term), my_half(glu_term), *tap_terms, jnp.zeros((3, HALF), F32)], axis=0)
-    started(gain_links(0))
-    b_ready(0, 2, 1)
-    for k in range(3):
-        start_c(0, k, 2)
-    gain_land[1, place[1]] = gain_sum(0)
-    started(gain_links(1))
-    b_ready(0, 3, 1)
-    for k in range(3):
-        start_c(0, k, 3)
-    b_ready(1, 0, 1)
-    for k in range(3):
-        start_c(1, k, 0)
-    gain_land[2, place[2]] = gain_sum(1)
-    started(gain_links(2))
+    input_rows((dn2_v[BLK - 16:, :] + da_v[BLK - 16:, :D]) + (xs_send[1] + da_v[16:32, D:2 * D]), BLK - 16)
+    stores += started([local(n_v, o_input, load_sem.at[6])])
+    v_v[0:8, :] = gain_sum(2)
+    stores += started([local(v_v.at[pl.ds(0, 8), :], o_gains, load_sem.at[7])])
     for g in range(4):
         c_ready(0, g)
     for k in range(3):
         start_d(0, k)
-    v_v[0:8, :] = gain_sum(2)
-    stores += started([local(v_v.at[pl.ds(0, 8), :], o_gains, load_sem.at[7])])
     c_ready(1, 0)
     for k in range(3):
         start_d(1, k)
@@ -683,11 +681,11 @@
             half32, half32, half32, half32, half32, pltpu.VMEM((BLK, HALF), BF16),
             full32, full32, full32,
             pltpu.VMEM((3, D, 2 * SPAN), BF16), pltpu.VMEM((3, SPAN, D), BF16), pltpu.VMEM((HALF, D), BF16),
-            pltpu.VMEM((STEPS, BLK, SPAN), F32), pltpu.VMEM((3, 4, BLK, WS), BF16), pltpu.VMEM((3, BLK, 4 * WM), BF16),
+            pltpu.VMEM((BLK, FF), F32), pltpu.VMEM((3, 4, BLK, WS), BF16), pltpu.VMEM((3, BLK, 4 * WM), BF16),
             pltpu.VMEM((2, D, BLK), BF16), pltpu.VMEM((2, D, BLK), BF16),
             pltpu.VMEM((16, D), BF16), pltpu.VMEM((16, HALF), F32), pltpu.VMEM((16, HALF), F32),
             pltpu.VMEM((2, 16, 4 * WM), BF16), pltpu.VMEM((2, 64, D), BF16), pltpu.VMEM((2, 64, WM), BF16),
-            pltpu.VMEM((2, BLK, D), BF16), pltpu.VMEM((2, BLK, D), BF16),
+            pltpu.VMEM((2, BLK, D), BF16), pltpu.VMEM((2, BLK, D), BF16), pltpu.VMEM((2, 16, D), F32),
             pltpu.VMEM((3, 4, 4, 4, 2, 512), F32), pltpu.VMEM((3, 4, 4, 4, 2, 256), F32),
             pltpu.VMEM((3, 4, 8, HALF), F32),
             pltpu.VMEM((3, D, 512), BF16), pltpu.VMEM((3, 512, WS), BF16), pltpu.VMEM((3, 4, 384, WS), BF16),
@@ -695,11 +693,11 @@
             pltpu.VMEM((3, 4, 32, WS), BF16), pltpu.VMEM((3, 4, 32, WS), BF16),
             pltpu.VMEM((3, D, 512), BF16), pltpu.VMEM((3, 512, WM), BF16),
             pltpu.VMEM((3, 4, 32, WM), BF16), pltpu.VMEM((3, 4, 32, WM), BF16),
-            dma((8,)), dma((6,)), dma((3,)), dma((5,)), dma((4,)), dma((4,)),
+            dma((8,)), dma((6,)), dma((3,)), dma((5,)), dma((6,)), dma((6,)),
             dma((2, 3)), dma((2, 3)), dma((3,)), dma((3,)),
             dma((2,)), dma((2,)), dma((2,)), dma((2,)), dma((5,)), dma((5,)),
             dma((10,)), dma((10,)), dma((5,)), dma((5,)), dma((2,)), dma((2,)),
-            dma((2,)), dma((5,)), dma((2,)), dma((2,)), dma((2,)),
+            dma((2,)), dma((2,)), dma((2,)),
         ],
         compiler_params=pltpu.CompilerParams(collective_id=1, has_side_effects=True, vmem_limit_bytes=LIMIT),
         name="layer",

time: 124 us -> 120 us (0.968)
  Pallas kernels: 123 us -> 119 us
    pallas_call x1, Pallas kernels: 120 us -> 116 us  [run_layer(): pl.pallas_call(layer_kernel, out_shape=[shape((BLK, D), BF16), shape((BLK...]
where the time goes in v6:
time: 120 us
  Pallas kernels  119 us (99%)
    pallas_call x1, Pallas kernels, run_layer(): pl.pallas_call(layer_kernel, out_shape=[shape((BLK, D), BF16), shape((BLK...  116 us
    pallas_call x1, Pallas kernels, place_outputs(): pl.pallas_call(place_kernel, out_shape=[shape((BLK, D), BF16), shape((BLK...  2.46 us

profile of v6, /device:TPU:0, one launch (start us, length us, event | category | flops | bytes accessed | tf_op | source)
XLA Modules:
  0.0 119.5 jit_solution(2431736947327664533)
XLA Ops:
  0.6 116.2 %layer.1 = (bf16[128,1536]{1,0:T(8,128)(2,1)}, bf16[128,1536]{1,0:T(8,128)(2,1)}, f32[8,768]{1,0:T(8,128)}, f32[24,3456]{1,0:T(8,128)}, f32[24,3456]{1,0:T(8,128...) custom-call(s32[4]{0:T(128)} %seq_lengths.1, s32[64]{0:T(128)} %block_slots.1, f32[1536]{0:T(1024)} %mixgain_1d.1, ...), custom_call_target="tpu_custom_call" | custom-call | tf_op jit(solution)/shard_map/layer/pallas_call | solution.py:673
  116.9 2.5 %place.1 = (bf16[128,1536]{1,0:T(8,128)(2,1)}, bf16[128,1536]{1,0:T(8,128)(2,1)}, f32[768]{0:T(1024)}, f32[768]{0:T(1024)}, f32[3,768]{1,0:T(4,128)}, /*index=5*...) custom-call(bf16[128,1536]{1,0:T(8,128)(2,1)} %get-tuple-element.28.refs_0, ...), custom_call_target="tpu_custom_call" | custom-call | tf_op jit(solution)/shard_map/place/pallas_call | solution.py:727

commit v7 on v6

--- a/solution.py
+++ b/solution.py
@@ -37,7 +37,7 @@
     tokens, cotangent, inproj, outproj, gate_w, lift_w, down_w,
     o_layer, o_input, o_gains, o_gate, o_lift, o_down, o_in, o_out,
     mixgain, glugain, tok_v, cot_v, n_v, b_v, c_v, x_v, v_v, u_v, y_v, h2_v, glu_v, dn2_v,
-    col, down_ring, out_v, da_v, act, mixed_r, s_src, m_src, e_src, eb_v, ex_v, er_src, e_left, e_right, xh_send, xh_recv, xs_send, tails, heads, gain_land,
+    col, down_ring, out_v, da_v, act, mixed_r, s_src, m_src, e_src, eb_v, ex_v, er_src, er_two, e_left, e_right, xh_send, xh_recv, xs_send, tails, heads, gain_land,
     s_left, s_right, s_bsend, s_bland, s_cland, s_dsend, s_dland, m_left, m_right, m_dsend, m_dland,
     load_sem, col_sem, down_sem, store_sem, x_send, x_recv, halo_send, halo_recv, gain_send, gain_recv,
     l_send, l_recv, f_send, f_recv, r_send, r_recv,
@@ -191,14 +191,23 @@
 
     def left_link(job, k, src, step):
         left = (s_left, m_left)[job]
+        sem = 1 if job == 1 else 2 + step // 2
         return link(src.at[half, :], left.at[k, half, pl.ds(128 * step, 128)],
-                    l_send.at[job], l_recv.at[job], k, step)
+                    l_send.at[sem], l_recv.at[sem], k, step)
 
     def send_left_s(k):
         src = s_src.at[1 if k == 2 else 0]
         s_left[k, :, :128] = src[...]
-        for step in range(1, 4):
+        for step in (1, 3):
             left_link(0, k, src, step).start()
+
+    def hand_on():
+        for n, step in enumerate((1, 3)):
+            all_links(s_left.at[:, half, pl.ds(128 * step, 128)], l_send.at[2 + n], l_recv.at[2 + n])
+            part = pl.ds(pl.multiple_of(core * HALF + 384 * n, 384), 384)
+            for k in range(3):
+                link(s_left.at[k, part, pl.ds(128 * step, 128)], s_left.at[k, part, pl.ds(256, 128)],
+                     l_send.at[0], l_recv.at[0], k, step).start()
 
     def send_left_m(k, which):
         for step in range(1, 4):
@@ -210,7 +219,10 @@
         return (s_left, m_left)[job].at[:, half, pl.ds(128, 384)]
 
     def forward_left(job):
-        all_links(others(job), l_send.at[job], l_recv.at[job])
+        if job == 0:
+            all_links(s_left.at[:, half, pl.ds(256, 128)], l_send.at[0], l_recv.at[0])
+        else:
+            all_links(others(1), l_send.at[1], l_recv.at[1])
         cross(others(job), others(job), f_send.at[job], f_recv.at[job]).start()
 
     started([out_load])
@@ -226,28 +238,28 @@
     edge = edge.astype(BF16)
     edge_b, edge_x = dot_nn(edge, col[0, :, :HALF]), dot_nn(edge, col[2, :, :HALF])
     carried = (edge_b * edge_x).astype(BF16).astype(F32)
-    e_src[...] = edge
+    e_src[...] = edge.astype(F32)[0:2]
     eb_v[...] = edge_b
     ex_v[...] = edge_x
 
     def edge_left_links(n):
         return [
-            link(e_src, e_left.at[n, pl.ds(16 * step, 16), :], e_send.at[0], e_recv.at[0], 2 * n, step)
+            link(e_src, e_left.at[n, step], e_send.at[0], e_recv.at[0], 2 * n, step)
             for step in range(1, 4)]
 
     def edge_piece(n, i):
-        return er_src.at[n, :, pl.ds(pl.multiple_of(i * WM, WM), WM)]
+        return er_two.at[n, :, pl.ds(pl.multiple_of(i * WM, WM), WM)]
 
     def edge_right_links(n):
         return [
-            link(edge_piece(n, (place[2 * n] + step) % 4), e_right.at[n, pl.ds(16 * step, 16), :],
+            link(edge_piece(n, (place[2 * n] + step) % 4), e_right.at[n, step],
                  e_send.at[1], e_recv.at[1], 2 * n, step)
             for step in range(1, 4)]
 
     def edge_own(n):
         return [
-            local(e_src, e_left.at[n, pl.ds(0, 16), :], own_edge.at[0]),
-            local(edge_piece(n, place[2 * n]), e_right.at[n, pl.ds(0, 16), :], own_edge.at[1])]
+            local(e_src, e_left.at[n, 0], own_edge.at[0]),
+            local(edge_piece(n, place[2 * n]), e_right.at[n, 0], own_edge.at[1])]
     for s in range(1, 3):
         started(pair_loads(s))
     row_is0, row_is1 = rows == 0, rows == 1
@@ -345,10 +357,13 @@
         all_links(rights[job].at[:, pl.ds(128, 384), lanes], r_send.at[n], r_recv.at[n])
 
     def edges_ready():
-        all_of(e_left.at[:, pl.ds(0, 16), :], own_edge.at[0])
-        all_of(e_right.at[:, pl.ds(0, 16), :], own_edge.at[1])
-        all_links(e_left.at[:, pl.ds(16, 48), :], e_send.at[0], e_recv.at[0])
-        all_links(e_right.at[:, pl.ds(16, 48), :], e_send.at[1], e_recv.at[1])
+        all_of(e_left.at[:, 0], own_edge.at[0])
+        all_of(e_right.at[:, 0], own_edge.at[1])
+        all_links(e_left.at[:, pl.ds(1, 3)], e_send.at[0], e_recv.at[0])
+        all_links(e_right.at[:, pl.ds(1, 3)], e_send.at[1], e_recv.at[1])
+
+    def edge_tile(parts):
+        return jnp.concatenate([*parts, jnp.zeros((8, parts[0].shape[1]), F32)], axis=0).astype(BF16)
 
     def start_b(job, k, g):
         lanes = pl.ds(*GROUPS[job][g])
@@ -358,7 +373,7 @@
             at = pl.ds(pl.multiple_of(x * 384, 384), 384)
             acc = dot_nn(lefts[job][k, at, :], rights[job][k, :, lanes])
             if edges:
-                acc = acc + outer(e_left[k // 2, :, at], e_right[k // 2])
+                acc = acc + outer(edge_tile([e_left[k // 2, i, :, at] for i in range(4)]), edge_tile([e_right[k // 2, i] for i in range(4)]))
             row = pl.multiple_of(96 * x, 96)
             for j in range(4):
                 if k == 0:
@@ -481,8 +496,9 @@
     for s in range(2):
         swiglu_step(s)
     send_right(0, 0)
-    for s in range(2, 4):
-        swiglu_step(s)
+    swiglu_step(2)
+    hand_on()
+    swiglu_step(3)
     send_right(0, 1)
     forward_left(0)
     swiglu_step(4)
@@ -537,6 +553,7 @@
     none = jnp.zeros((16, WM), BF16)
     for n, other in enumerate((ex_v, eb_v)):
         er_src[n] = jnp.concatenate([(share * other[...]).astype(BF16), none], axis=1)
+        er_two[n] = er_src[n].astype(F32)[0:2]
     send_right(1, 0)
     for n in range(2):
         started(edge_own(n))
@@ -592,8 +609,6 @@
     right_ready(0, 3)
     for k in range(3):
         start_b(0, k, 3)
-    halo_ready(heads, 1, 0)
-    started(halo_links(heads, 1, 1))
     swap_dn1.wait()
     swap_row.wait()
     dn1 = dn2_v[...] + da_v[:, :D]
@@ -603,6 +618,13 @@
         [my_half(mix_term), my_half(glu_term), *tap_terms, jnp.zeros((3, HALF), F32)], axis=0)
     started(gain_links(0))
     forward_left(1)
+    halo_ready(heads, 1, 0)
+    started(halo_links(heads, 1, 1))
+    left_ready(1)
+    right_ready(1, 0)
+    edges_ready()
+    for k in range(3):
+        start_b(1, k, 0)
     b_ready(0, 2, 0)
     for k in range(3):
         pass_on(0, k, 2)
@@ -614,19 +636,14 @@
         pass_on(0, k, 3)
     halo_ready(heads, 1, 1)
     started(halo_links(heads, 1, 2))
-    left_ready(1)
-    right_ready(1, 0)
-    edges_ready()
-    for k in range(3):
-        start_b(1, k, 0)
     gain_land[1, place[1]] = gain_sum(0)
     started(gain_links(1))
+    b_ready(1, 0, 0)
+    for k in range(3):
+        pass_on(1, k, 0)
     b_ready(0, 2, 1)
     for k in range(3):
         start_c(0, k, 2)
-    b_ready(1, 0, 0)
-    for k in range(3):
-        pass_on(1, k, 0)
     b_ready(0, 3, 1)
     for k in range(3):
         start_c(0, k, 3)
@@ -683,8 +700,8 @@
             pltpu.VMEM((3, D, 2 * SPAN), BF16), pltpu.VMEM((3, SPAN, D), BF16), pltpu.VMEM((HALF, D), BF16),
             pltpu.VMEM((BLK, FF), F32), pltpu.VMEM((3, 4, BLK, WS), BF16), pltpu.VMEM((3, BLK, 4 * WM), BF16),
             pltpu.VMEM((2, D, BLK), BF16), pltpu.VMEM((2, D, BLK), BF16),
-            pltpu.VMEM((16, D), BF16), pltpu.VMEM((16, HALF), F32), pltpu.VMEM((16, HALF), F32),
-            pltpu.VMEM((2, 16, 4 * WM), BF16), pltpu.VMEM((2, 64, D), BF16), pltpu.VMEM((2, 64, WM), BF16),
+            pltpu.VMEM((2, D), F32), pltpu.VMEM((16, HALF), F32), pltpu.VMEM((16, HALF), F32),
+            pltpu.VMEM((2, 16, 4 * WM), BF16), pltpu.VMEM((2, 2, 4 * WM), F32), pltpu.VMEM((2, 4, 2, D), F32), pltpu.VMEM((2, 4, 2, WM), F32),
             pltpu.VMEM((2, BLK, D), BF16), pltpu.VMEM((2, BLK, D), BF16), pltpu.VMEM((2, 16, D), F32),
             pltpu.VMEM((3, 4, 4, 4, 2, 512), F32), pltpu.VMEM((3, 4, 4, 4, 2, 256), F32),
             pltpu.VMEM((3, 4, 8, HALF), F32),
@@ -695,7 +712,7 @@
             pltpu.VMEM((3, 4, 32, WM), BF16), pltpu.VMEM((3, 4, 32, WM), BF16),
             dma((8,)), dma((6,)), dma((3,)), dma((5,)), dma((6,)), dma((6,)),
             dma((2, 3)), dma((2, 3)), dma((3,)), dma((3,)),
-            dma((2,)), dma((2,)), dma((2,)), dma((2,)), dma((5,)), dma((5,)),
+            dma((4,)), dma((4,)), dma((2,)), dma((2,)), dma((5,)), dma((5,)),
             dma((10,)), dma((10,)), dma((5,)), dma((5,)), dma((2,)), dma((2,)),
             dma((2,)), dma((2,)), dma((2,)),
         ],

time: 120 us -> 117 us (0.975)
  Pallas kernels: 119 us -> 116 us
    pallas_call x1, Pallas kernels: 116 us -> 114 us  [run_layer(): pl.pallas_call(layer_kernel, out_shape=[shape((BLK, D), BF16), shape((BLK...]
where the time goes in v7:
time: 117 us
  Pallas kernels  116 us (99%)
    pallas_call x1, Pallas kernels, run_layer(): pl.pallas_call(layer_kernel, out_shape=[shape((BLK, D), BF16), shape((BLK...  114 us
    pallas_call x1, Pallas kernels, place_outputs(): pl.pallas_call(place_kernel, out_shape=[shape((BLK, D), BF16), shape((BLK...  2.46 us

profile of v7, /device:TPU:0, one launch (start us, length us, event | category | flops | bytes accessed | tf_op | source)
XLA Modules:
  0.0 117.0 jit_solution(10030550344518304005)
XLA Ops:
  0.6 113.7 %layer.1 = (bf16[128,1536]{1,0:T(8,128)(2,1)}, bf16[128,1536]{1,0:T(8,128)(2,1)}, f32[8,768]{1,0:T(8,128)}, f32[24,3456]{1,0:T(8,128)}, f32[24,3456]{1,0:T(8,128...) custom-call(s32[4]{0:T(128)} %seq_lengths.1, s32[64]{0:T(128)} %block_slots.1, f32[1536]{0:T(1024)} %mixgain_1d.1, ...), custom_call_target="tpu_custom_call" | custom-call | tf_op jit(solution)/shard_map/layer/pallas_call | solution.py:690
  114.4 2.5 %place.1 = (bf16[128,1536]{1,0:T(8,128)(2,1)}, bf16[128,1536]{1,0:T(8,128)(2,1)}, f32[768]{0:T(1024)}, f32[768]{0:T(1024)}, f32[3,768]{1,0:T(4,128)}, /*index=5*...) custom-call(bf16[128,1536]{1,0:T(8,128)(2,1)} %get-tuple-element.28.refs_0, ...), custom_call_target="tpu_custom_call" | custom-call | tf_op jit(solution)/shard_map/place/pallas_call | solution.py:744

commit v8 on v7

--- a/solution.py
+++ b/solution.py
@@ -403,9 +403,31 @@
             own[...] = (own[...].astype(F32) + via[...].astype(F32)).astype(BF16)
         started(b_links(job, k, g, (4, 5)))
 
+    def c_halves(k, g, which):
+        axis = (k + 2) % 3
+        me = place[axis]
+        opposite, ahead, behind = (me + 2) % 4, (me + 1) % 4, (me + 3) % 4
+        table = ((opposite, 0, 2, 1), (ahead, 48, 0, 1), (opposite, 48, 2, 3), (behind, 0, 1, 3), (ahead, 0, 0, 1), (behind, 48, 1, 3))
+        out = []
+        for n in which:
+            part, row, land, step = table[n]
+            sem = 5 + g if land == 2 else g
+            out.append(link(c_out(0, k, part, g, row, 48), s_cland.at[k, land, pl.ds(row, 48), pl.ds(*GROUPS[0][g])],
+                            c_send.at[sem], c_recv.at[sem], axis, step))
+        return out
+
+    def pass_on_c(g):
+        lanes = pl.ds(*GROUPS[0][g])
+        all_links(s_cland.at[:, pl.ds(2, 1), :, lanes], c_send.at[5 + g], c_recv.at[5 + g])
+        for k in range(3):
+            for step, row in ((1, 0), (3, 48)):
+                mine, via = c_out(0, k, (place[(k + 2) % 3] + step) % 4, g, row, 48), s_cland.at[k, 2, pl.ds(row, 48), lanes]
+                mine[...] = (mine[...].astype(F32) + via[...].astype(F32)).astype(BF16)
+            started(c_halves(k, g, (4, 5)))
+
     def c_ready(job, g):
         if job == 0:
-            view = s_cland.at[:, :, :, pl.ds(*GROUPS[job][g])]
+            view = s_cland.at[:, pl.ds(0, 2 if g < 3 else 3), :, pl.ds(*GROUPS[job][g])]
         else:
             view = down_ring.at[:, pl.ds(0, 96), pl.ds(HALF, HALF)]
         all_links(view, c_send.at[4 * job + g], c_recv.at[4 * job + g])
@@ -428,7 +450,7 @@
         else:
             for q in range(4):
                 c_out(job, k, q, g)[...] = summed(q).astype(BF16)
-        started(c_links(job, k, g))
+        started(c_halves(k, g, range(4)) if job == 0 and g < 3 else c_links(job, k, g))
 
     def d_links(job, k):
         return [
@@ -440,7 +462,7 @@
         dsend, dland = dsends[job], dlands[job]
         for g, (first, width) in enumerate(GROUPS[job]):
             total = c_out(job, k, place[(k + 2) % 3], g)[...].astype(F32)
-            for i in range(3):
+            for i in range(2 if job == 0 and g < 3 else 3):
                 total = total + c_in(job, k, i, g)[...].astype(F32)
             pad = jnp.zeros((8, width), F32)
             for j in range(4):
@@ -634,6 +656,7 @@
     b_ready(0, 3, 0)
     for k in range(3):
         pass_on(0, k, 3)
+    pass_on_c(0)
     halo_ready(heads, 1, 1)
     started(halo_links(heads, 1, 2))
     gain_land[1, place[1]] = gain_sum(0)
@@ -641,6 +664,7 @@
     b_ready(1, 0, 0)
     for k in range(3):
         pass_on(1, k, 0)
+    pass_on_c(1)
     b_ready(0, 2, 1)
     for k in range(3):
         start_c(0, k, 2)
@@ -658,6 +682,7 @@
     b_ready(1, 0, 1)
     for k in range(3):
         start_c(1, k, 0)
+    pass_on_c(2)
     swap.wait()
     input_rows((dn2_v[BLK - 16:, :] + da_v[BLK - 16:, :D]) + (xs_send[1] + da_v[16:32, D:2 * D]), BLK - 16)
     stores += started([local(n_v, o_input, load_sem.at[6])])
@@ -713,7 +738,7 @@
             dma((8,)), dma((6,)), dma((3,)), dma((5,)), dma((6,)), dma((6,)),
             dma((2, 3)), dma((2, 3)), dma((3,)), dma((3,)),
             dma((4,)), dma((4,)), dma((2,)), dma((2,)), dma((5,)), dma((5,)),
-            dma((10,)), dma((10,)), dma((5,)), dma((5,)), dma((2,)), dma((2,)),
+            dma((10,)), dma((10,)), dma((8,)), dma((8,)), dma((2,)), dma((2,)),
             dma((2,)), dma((2,)), dma((2,)),
         ],
         compiler_params=pltpu.CompilerParams(collective_id=1, has_side_effects=True, vmem_limit_bytes=LIMIT),

time: 117 us -> 115 us (0.983)
  Pallas kernels: 116 us -> 114 us
    pallas_call x1, Pallas kernels: 114 us -> 111 us  [run_layer(): pl.pallas_call(layer_kernel, out_shape=[shape((BLK, D), BF16), shape((BLK...]
where the time goes in v8:
time: 115 us
  Pallas kernels  114 us (99%)
    pallas_call x1, Pallas kernels, run_layer(): pl.pallas_call(layer_kernel, out_shape=[shape((BLK, D), BF16), shape((BLK...  111 us
    pallas_call x1, Pallas kernels, place_outputs(): pl.pallas_call(place_kernel, out_shape=[shape((BLK, D), BF16), shape((BLK...  2.46 us

profile of v8, /device:TPU:0, one launch (start us, length us, event | category | flops | bytes accessed | tf_op | source)
XLA Modules:
  0.0 114.7 jit_solution(12725516007107564502)
XLA Ops:
  0.6 111.4 %layer.1 = (bf16[128,1536]{1,0:T(8,128)(2,1)}, bf16[128,1536]{1,0:T(8,128)(2,1)}, f32[8,768]{1,0:T(8,128)}, f32[24,3456]{1,0:T(8,128)}, f32[24,3456]{1,0:T(8,128...) custom-call(s32[4]{0:T(128)} %seq_lengths.1, s32[64]{0:T(128)} %block_slots.1, f32[1536]{0:T(1024)} %mixgain_1d.1, ...), custom_call_target="tpu_custom_call" | custom-call | tf_op jit(solution)/shard_map/layer/pallas_call | solution.py:715
  112.0 2.5 %place.1 = (bf16[128,1536]{1,0:T(8,128)(2,1)}, bf16[128,1536]{1,0:T(8,128)(2,1)}, f32[768]{0:T(1024)}, f32[768]{0:T(1024)}, f32[3,768]{1,0:T(4,128)}, /*index=5*...) custom-call(bf16[128,1536]{1,0:T(8,128)(2,1)} %get-tuple-element.28.refs_0, ...), custom_call_target="tpu_custom_call" | custom-call | tf_op jit(solution)/shard_map/place/pallas_call | solution.py:769

commit v9 on v8

--- a/solution.py
+++ b/solution.py
@@ -275,12 +275,12 @@
     u_v[...] = tap0 * v0 + tap1 * v1 + tap2 * v2
     y_v[...] = (c_v[...] * u_v[...]).astype(BF16)
     out_load.wait()
-    dn2_v[...] = dot_nn(y_v[...], out_v[...])
-    swap = cross(dn2_v, h2_v, x_send.at[0], x_recv.at[0])
+    xh_send[0] = dot_nn(y_v[...], out_v[...]).astype(BF16)
+    swap = cross(xh_send.at[0], xh_recv.at[0], x_send.at[0], x_recv.at[0])
     swap.start()
     hidden_grads(4, 6)
     swap.wait()
-    h2_v[...] = tok_v[...].astype(F32) + (dn2_v[...] + h2_v[...])
+    h2_v[...] = tok_v[...].astype(F32) + (xh_send[0].astype(F32) + xh_recv[0].astype(F32))
     h2 = h2_v[...]
     scale_b = lax.rsqrt(jnp.mean(h2 * h2, axis=1, keepdims=True) + EPS)
     n_v[...] = (h2 * scale_b * glugain[...]).astype(BF16)

time: 115 us -> 116 us (level)
  no operation moved by 1% of the time
where the time goes in v9:
time: 116 us; the launch traced here: 115 us
  Pallas kernels  114 us (98%)
    pallas_call x1, Pallas kernels, run_layer(): pl.pallas_call(layer_kernel, out_shape=[shape((BLK, D), BF16), shape((BLK...  112 us
    pallas_call x1, Pallas kernels, place_outputs(): pl.pallas_call(place_kernel, out_shape=[shape((BLK, D), BF16), shape((BLK...  2.46 us

profile of v9, /device:TPU:0, one launch (start us, length us, event | category | flops | bytes accessed | tf_op | source)
XLA Modules:
  0.0 115.3 jit_solution(17658052865392134621)
XLA Ops:
  0.6 112.0 %layer.1 = (bf16[128,1536]{1,0:T(8,128)(2,1)}, bf16[128,1536]{1,0:T(8,128)(2,1)}, f32[8,768]{1,0:T(8,128)}, f32[24,3456]{1,0:T(8,128)}, f32[24,3456]{1,0:T(8,128...) custom-call(s32[4]{0:T(128)} %seq_lengths.1, s32[64]{0:T(128)} %block_slots.1, f32[1536]{0:T(1024)} %mixgain_1d.1, ...), custom_call_target="tpu_custom_call" | custom-call | tf_op jit(solution)/shard_map/layer/pallas_call | solution.py:715
  112.7 2.5 %place.1 = (bf16[128,1536]{1,0:T(8,128)(2,1)}, bf16[128,1536]{1,0:T(8,128)(2,1)}, f32[768]{0:T(1024)}, f32[768]{0:T(1024)}, f32[3,768]{1,0:T(4,128)}, /*index=5*...) custom-call(bf16[128,1536]{1,0:T(8,128)(2,1)} %get-tuple-element.28.refs_0, ...), custom_call_target="tpu_custom_call" | custom-call | tf_op jit(solution)/shard_map/place/pallas_call | solution.py:769
